TPU v7x, 256 devices: a whole 4x4x8 slice. The times are simulated.
256 devices in a mesh: dp: 2 (over y_lo), chan: 16 (over z, core), tm: 8 (over y_hi, x).
Axes of the slice: x: 4, y: 4 (y_hi: 2, y_lo: 2; y = y_hi * 2 + y_lo), z: 8, core: 2. Of those that a mesh axis runs over, the one named last changes fastest.
Arguments:
- features: bfloat16 [4, 16, 1024, 768], P('dp', 'chan', 'tm'), may hold values from -6 to 6
- lengths: int32 [4], P('dp'), may hold values from 256 to 1024, as said below
- chan_valid: int32 [4, 16], P('dp'), may hold values from 0 to 1, as said below
- norm_gains: float32 [3, 768], replicated, may hold values from 0.1 to 1.9
- branch_qkv: bfloat16 [768, 2304], replicated, may hold values from -32 to 32, as said below
- branch_out: bfloat16 [768, 768], replicated, may hold values from -0.6484375 to 0.6484375
- depth_taps: bfloat16 [31, 768], replicated, may hold values from -1 to 1
- point_in: bfloat16 [768, 1536], P(('dp', 'chan')), may hold values from -0.21875 to 0.21875
- point_out: bfloat16 [768, 768], P(('dp', 'chan')), may hold values from -0.21875 to 0.21875
- merge_qkv: bfloat16 [768, 2304], P(('dp', 'chan')), may hold values from -32 to 32, as said below
- merge_out: bfloat16 [768, 768], P(('dp', 'chan')), may hold values from -0.21875 to 0.21875
Outputs:
- merged: bfloat16 [4, 16, 1024, 768], P('dp', 'chan', 'tm')
Inputs may be any that keep to these rules, and one draw needn't show every extreme that they name: `lengths`: one utterance has all 1024 frames valid and one has at most 512. `chan_valid`: every utterance has one or more working channels. `branch_qkv`: entries of order 768^-0.5. `merge_qkv`: entries of order 768^-0.5.
All inputs are finite; a program needn't handle non-finite values.
Results may differ from a plain program's by a relative error of at most 0.018.
Values may be sent and summed in bfloat16 or wider, within the bound.
No kernel may reach another device: no remote copies, remote signals or barrier semaphores. Data moves between devices by JAX's collectives and lax.ppermute only.
A program may use at most 128 MiB of HBM per device.

v0:
```python
import jax
import jax.numpy as jnp
from jax import lax
from jax.sharding import PartitionSpec as P

HEADS = 12


def with_halo(cells, sides, width):
    for axis, dim in sides:
        count = lax.axis_size(axis)
        ends = count - 1
        head = lax.slice_in_dim(cells, 0, width, axis=dim)
        tail = lax.slice_in_dim(cells, cells.shape[dim] - width, cells.shape[dim], axis=dim)
        cells = jnp.concatenate(
            [
                lax.ppermute(tail, axis, [(i, (i + 1) % count) for i in range(ends)]),
                cells,
                lax.ppermute(head, axis, [((i + 1) % count, i) for i in range(ends)]),
            ],
            axis=dim,
        )
    return cells


def layer_norm(values, gain):
    data = values.astype(jnp.float32)
    center = data - jnp.mean(data, axis=-1, keepdims=True)
    spread = jnp.mean(center * center, axis=-1, keepdims=True)
    return center * lax.rsqrt(spread + 1e-05) * gain


def shards(
    features,
    lengths,
    chan_valid,
    norm_gains,
    branch_qkv,
    branch_out,
    depth_taps,
    point_in,
    point_out,
    merge_qkv,
    merge_out,
):
    count_b = features.shape[0]
    span = features.shape[2]
    model = features.shape[3]
    head_size = model // HEADS
    inputs = features[:, 0]
    offset_t = lax.axis_index("tm") * span
    local_pos = offset_t + jnp.arange(span, dtype=jnp.int32)
    frame_live = local_pos[None, :] < lengths[:, None]
    normed = layer_norm(inputs, norm_gains[0]).astype(jnp.bfloat16)
    project = jnp.dot(
        normed.reshape(count_b * span, model), branch_qkv, preferred_element_type=jnp.float32
    )
    project = project.astype(jnp.bfloat16).reshape(count_b, span, 3 * model)
    query = project[..., :model].reshape(count_b, span, HEADS, head_size)
    gathered = lax.all_gather(project[..., model:], "tm", axis=1, tiled=True)
    total_rows = gathered.shape[1]
    keyed = gathered[..., :model].reshape(count_b, total_rows, HEADS, head_size)
    valued = gathered[..., model:].reshape(count_b, total_rows, HEADS, head_size)
    key_live = jnp.arange(total_rows, dtype=jnp.int32)[None, :] < lengths[:, None]
    scores = jnp.einsum(
        "bqhd,bkhd->bhqk", query, keyed, preferred_element_type=jnp.float32
    ) * head_size ** (-0.5)
    scores = jnp.where(key_live[:, None, None, :], scores, -1e30)
    attend = jax.nn.softmax(scores, axis=-1).astype(jnp.bfloat16)
    context = jnp.einsum("bhqk,bkhd->bqhd", attend, valued, preferred_element_type=jnp.float32)
    context = context.astype(jnp.bfloat16).reshape(count_b * span, model)
    first = inputs.reshape(count_b * span, model).astype(jnp.float32) + jnp.dot(
        context, branch_out, preferred_element_type=jnp.float32
    )
    first = first.astype(jnp.bfloat16)
    conv_in, conv_out = (
        lax.all_gather(point_in, ("dp", "chan"), axis=0, tiled=True),
        lax.all_gather(point_out, ("dp", "chan"), axis=0, tiled=True),
    )
    normed_two = layer_norm(first, norm_gains[1]).astype(jnp.bfloat16)
    widened = jnp.dot(normed_two, conv_in, preferred_element_type=jnp.float32)
    gated = widened[:, :model] * jax.nn.sigmoid(widened[:, model:])
    gated = jnp.where(frame_live.reshape(count_b * span)[:, None], gated, 0.0).astype(jnp.bfloat16)
    gated = gated.reshape(count_b, span, model)
    reach = depth_taps.shape[0] // 2
    padded = with_halo(gated, (("tm", 1),), reach).astype(jnp.float32)
    taps = depth_taps.astype(jnp.float32)
    mixed = jnp.zeros((count_b, span, model), jnp.float32)
    for offset in range(depth_taps.shape[0]):
        mixed = mixed + taps[offset] * padded[:, offset : offset + span]
    swished = jax.nn.silu(mixed).astype(jnp.bfloat16).reshape(count_b * span, model)
    second = first.astype(jnp.float32) + jnp.dot(
        swished, conv_out, preferred_element_type=jnp.float32
    )
    second = second.astype(jnp.bfloat16)
    merge_in, merge_back = (
        lax.all_gather(merge_qkv, ("dp", "chan"), axis=0, tiled=True),
        lax.all_gather(merge_out, ("dp", "chan"), axis=0, tiled=True),
    )
    normed_three = layer_norm(second, norm_gains[2]).astype(jnp.bfloat16)
    channels = lax.axis_size("chan")
    local_qkv = jnp.dot(normed_three, merge_in, preferred_element_type=jnp.float32).astype(
        jnp.bfloat16
    )
    grouped = lax.all_to_all(
        local_qkv.reshape(count_b, 1, span, 3 * model),
        "chan",
        split_axis=2,
        concat_axis=1,
        tiled=True,
    )
    part_rows = grouped.shape[2]
    merge_query = grouped[..., :model].reshape(count_b, channels, part_rows, HEADS, head_size)
    merge_key = grouped[..., model : 2 * model].reshape(
        count_b, channels, part_rows, HEADS, head_size
    )
    merge_value = grouped[..., 2 * model :].reshape(count_b, channels, part_rows, HEADS, head_size)
    cross = jnp.einsum(
        "bcfhd,befhd->bfhce", merge_query, merge_key, preferred_element_type=jnp.float32
    ) * head_size ** (-0.5)
    cross = jnp.where(chan_valid[:, None, None, None, :] > 0, cross, -1e30)
    cross_attend = jax.nn.softmax(cross, axis=-1).astype(jnp.bfloat16)
    joined = jnp.einsum(
        "bfhce,befhd->bcfhd", cross_attend, merge_value, preferred_element_type=jnp.float32
    )
    joined = joined.astype(jnp.bfloat16).reshape(count_b, channels, part_rows, model)
    returned = lax.all_to_all(joined, "chan", split_axis=1, concat_axis=2, tiled=True)
    result = second.astype(jnp.float32) + jnp.dot(
        returned.reshape(count_b * span, model), merge_back, preferred_element_type=jnp.float32
    )
    return result.astype(jnp.bfloat16).reshape(count_b, 1, span, model)


def solution(mesh):
    placed = (
        P("dp", "chan", "tm", None),
        P("dp"),
        P("dp", None),
        P(),
        P(),
        P(),
        P(),
        P(("dp", "chan"), None),
        P(("dp", "chan"), None),
        P(("dp", "chan"), None),
        P(("dp", "chan"), None),
    )
    return jax.shard_map(
        shards, mesh=mesh, in_specs=placed, out_specs=P("dp", "chan", "tm", None), check_vma=False
    )
```

profile of v0, /device:TPU:1, one launch (start us, length us, event | category | flops | bytes accessed | tf_op | source)
XLA Modules:
  0.0 408.3 jit_solution(8000729961926941780)
XLA Ops:
  20.2 92.8 %all-gather.6.cloned.1.call-done = bf16[2,1024,1536]{2,1,0:T(8,128)(2,1)} async-done(((bf16[2,128,1536]{2,1,0:T(8,128)(2,1)}), bf16[2,1024,1536]{2,1,0:T(8,128)(2,1)}) %all-gather.6.cloned.1.call-update) | async-done | bytes 6291472 | tf_op jit(solution)/shard_map/all_gather | solution.py:60
  113.0 4.9 %fusion.80 = (bf16[2,1024,768]{2,1,0:T(8,128)(2,1)S(1)}, bf16[2,1024,768]{2,1,0:T(8,128)(2,1)}) fusion(bf16[2,1024,1536]{2,1,0:T(8,128)(2,1)} %all-gather.6.cloned.1.call-done), kind=kLoop, calls=%fused_computation.171 | loop fusion | bytes 12582912 | tf_op jit(solution)/shard_map/slice | solution.py:62
  118.0 4.6 %copy.42 = bf16[2,1024,768]{1,2,0:T(8,128)(2,1)} copy(bf16[2,1024,768]{2,1,0:T(8,128)(2,1)} %get-tuple-element.40) | data formatting | bytes 6291456 | tf_op jit(solution)/shard_map/slice | solution.py:63
  122.6 2.9 copy.44
  125.5 10.7 %fusion.83 = (f32[2,12,128]{2,1,0:T(8,128)S(1)}, f32[2,12,128,1024]{3,2,1,0:T(8,128)}) fusion(pred[2,1024]{1,0:T(4,128)(4,1)} %iota_compare_fusion, bf16[2,128,12,64]{1,3,2,0:T(8,128)(2,1)S(1)} %bitcast.80, bf16[2,1024,12,64]{1,3,2,0:T(8,128)(2,1)} %bitcast.71), kind=kOutput, calls=%fused_computation.174 | convolution fusion | flops 415237120 | bytes 16136192 | tf_op jit(solution)/shard_map/sub | solution.py:69
  136.2 8.1 %fusion.16 = bf16[2,128,12,64]{1,3,2,0:T(8,128)(2,1)S(1)} fusion(bf16[2,1024,12,64]{1,3,2,0:T(8,128)(2,1)} %bitcast.70, f32[2,12,128,1024]{3,2,1,0:T(8,128)} %get-tuple-element.49, f32[2,12,128]{2,1,0:T(8,128)S(1)} %get-tuple-element.48), kind=kOutput, calls=%fused_computation.27 | convolution fusion | flops 409141248 | bytes 16134144 | tf_op jit(solution)/shard_map/bhqk,bkhd->bqhd/dot_general | solution.py:70
  145.6 33.3 %all-gather.8.cloned.1.call-done = bf16[768,1536]{1,0:T(8,128)(2,1)} async-done(((bf16[24,1536]{1,0:T(8,128)(2,1)}), bf16[768,1536]{1,0:T(8,128)(2,1)}) %all-gather.8.cloned.1.call-update) | async-done | bytes 2359312 | tf_op jit(solution)/shard_map/all_gather | solution.py:77
  178.9 2.5 fusion.64
  183.1 4.2 %collective-permute-start = (bf16[2,15,768]{2,1,0:T(8,128)(2,1)S(1)}, bf16[2,15,768]{2,1,0:T(8,128)(2,1)S(1)}, u32[]{:S(2)}, u32[]{:S(2)}) collective-permute-start(bf16[2,15,768]{2,1,0:T(8,128)(2,1)S(1)} %get-tuple-element.44), channel_id=1, source_target_pairs={{0,1},{1,2},{2,3},{3,4},{4,5},{5,6},{6,7},{8,9},{9,10},{10,11},{11... | collective-permute-start | bytes 138248 | tf_op jit(solution)/shard_map/ppermute | solution.py:17
  188.8 3.2 multiply_convert_fusion.1
  192.0 52.5 %all-gather.10.cloned.1.call-done = bf16[768,768]{1,0:T(8,128)(2,1)} async-done(((bf16[24,768]{1,0:T(8,128)(2,1)}), bf16[768,768]{1,0:T(8,128)(2,1)}) %all-gather.10.cloned.1.call-update) | async-done | bytes 1179664 | tf_op jit(solution)/shard_map/all_gather | solution.py:78
  244.6 1.8 fusion.85
  246.7 65.3 %all-gather.12.cloned.1.call-done = bf16[768,2304]{1,0:T(8,128)(2,1)} async-done(((bf16[24,2304]{1,0:T(8,128)(2,1)}), bf16[768,2304]{1,0:T(8,128)(2,1)}) %all-gather.12.cloned.1.call-update) | async-done | bytes 3538960 | tf_op jit(solution)/shard_map/all_gather | solution.py:97
  312.0 3.1 convolution_convert_fusion
  315.1 2.2 copy.46
  317.4 5.9 %all-to-all-start = ((bf16[2,1,128,2304]{3,0,1,2:T(2,128)(2,1)}), bf16[2,1,128,2304]{3,0,1,2:T(2,128)(2,1)S(1)}, u32[]{:S(2)}, u32[]{:S(2)}) async-start(bf16[2,1,128,2304]{3,0,1,2:T(2,128)(2,1)} %copy.46), calls=%async_computation | async-start | bytes 2359296 | tf_op jit(solution)/shard_map/all_to_all | solution.py:105
  323.9 30.6 %all-to-all-done = bf16[2,1,128,2304]{3,0,1,2:T(2,128)(2,1)S(1)} async-done(((bf16[2,1,128,2304]{3,0,1,2:T(2,128)(2,1)}), bf16[2,1,128,2304]{3,0,1,2:T(2,128)(2,1)S(1)}, u32[]{:S(2)}, u32[]{:S(2)}) %all-to-all-start) | async-done | bytes 1179680 | tf_op jit(solution)/shard_map/all_to_all | solution.py:105
  356.5 1.5 reshape.226
  358.0 2.6 fusion.86
  360.7 2.4 fusion.9
  364.4 2.7 reshape.191
  367.1 19.6 %all_to_all.21 = bf16[2,16,8,768]{3,2,0,1:T(8,128)(2,1)S(1)} all-to-all(bf16[2,16,8,768]{3,2,0,1:T(8,128)(2,1)} %reshape.191), channel_id=1, replica_groups=mesh['dp'=2,'chan'=16,'tm'=8] {'chan'}, dimensions={1} | all-to-all | bytes 786432 | tf_op jit(solution)/shard_map/all_to_all | solution.py:127
  387.5 11.5 %all-gather.14.cloned.1.call-done = bf16[768,768]{1,0:T(8,128)(2,1)} async-done(((bf16[24,768]{1,0:T(8,128)(2,1)}), bf16[768,768]{1,0:T(8,128)(2,1)}) %all-gather.14.cloned.1.call-update) | async-done | bytes 1179664 | tf_op jit(solution)/shard_map/all_gather | solution.py:98
  398.9 2.8 fusion.14
  (102 shorter events, 22.5 us)
Async XLA Ops:
  6.5 106.5 %all-gather.6.cloned.1.call-start = ((), (), s32[]{:S(2)}) async-start(), calls=%async_computation.2 | async-start | bytes 7077888 | tf_op jit(solution)/shard_map/all_gather | solution.py:60
  14.8 164.1 %all-gather.8.cloned.1.call-start = ((), (), s32[]{:S(2)}) async-start(), calls=%async_computation.3 | async-start | bytes 2433024 | tf_op jit(solution)/shard_map/all_gather | solution.py:77
  15.5 229.1 %all-gather.10.cloned.1.call-start = ((), (), s32[]{:S(2)}) async-start(), calls=%async_computation.4 | async-start | bytes 1216512 | tf_op jit(solution)/shard_map/all_gather | solution.py:78
  16.3 295.7 %all-gather.12.cloned.1.call-start = ((), (), s32[]{:S(2)}) async-start(), calls=%async_computation.5 | async-start | bytes 3649536 | tf_op jit(solution)/shard_map/all_gather | solution.py:97
  136.2 8.5 %copy-start.3 = (bf16[2,1,128,768]{3,2,1,0:T(8,128)(2,1)S(1)}, bf16[2,1,128,768]{3,2,1,0:T(8,128)(2,1)}, u32[]{:S(2)}) copy-start(bf16[2,1,128,768]{3,2,1,0:T(8,128)(2,1)} %param.11) | copy-start | bytes 1179652
  136.2 8.6 %copy-start.4 = (bf16[768,768]{1,0:T(8,128)(2,1)S(1)}, bf16[768,768]{1,0:T(8,128)(2,1)}, u32[]{:S(2)}) copy-start(bf16[768,768]{1,0:T(8,128)(2,1)} %param.16) | copy-start | bytes 3538948
  181.4 7.2 %copy-start.8 = (f32[768]{0:T(1024)S(1)}, f32[768]{0:T(1024)}, u32[]{:S(2)}) copy-start(f32[768]{0:T(1024)} %get-tuple-element.8) | copy-start | bytes 9220
  181.4 7.2 %copy-start.9 = (f32[768]{0:T(1024)S(1)}, f32[768]{0:T(1024)}, u32[]{:S(2)}) copy-start(f32[768]{0:T(1024)} %get-tuple-element.9) | copy-start | bytes 9220
  181.4 7.2 %copy-start.10 = (f32[768]{0:T(1024)S(1)}, f32[768]{0:T(1024)}, u32[]{:S(2)}) copy-start(f32[768]{0:T(1024)} %get-tuple-element.10) | copy-start | bytes 9220
  181.4 7.2 %copy-start.11 = (f32[768]{0:T(1024)S(1)}, f32[768]{0:T(1024)}, u32[]{:S(2)}) copy-start(f32[768]{0:T(1024)} %get-tuple-element.11) | copy-start | bytes 9220
  181.5 7.2 %copy-start.12 = (f32[768]{0:T(1024)S(1)}, f32[768]{0:T(1024)}, u32[]{:S(2)}) copy-start(f32[768]{0:T(1024)} %get-tuple-element.12) | copy-start | bytes 9220
  181.5 7.2 %copy-start.13 = (f32[768]{0:T(1024)S(1)}, f32[768]{0:T(1024)}, u32[]{:S(2)}) copy-start(f32[768]{0:T(1024)} %get-tuple-element.13) | copy-start | bytes 9220
  181.5 7.2 %copy-start.14 = (f32[768]{0:T(1024)S(1)}, f32[768]{0:T(1024)}, u32[]{:S(2)}) copy-start(f32[768]{0:T(1024)} %get-tuple-element.14) | copy-start | bytes 9220
  181.5 7.2 %copy-start.15 = (f32[768]{0:T(1024)S(1)}, f32[768]{0:T(1024)}, u32[]{:S(2)}) copy-start(f32[768]{0:T(1024)} %get-tuple-element.15) | copy-start | bytes 9220
  181.5 7.2 %copy-start.16 = (f32[768]{0:T(1024)S(1)}, f32[768]{0:T(1024)}, u32[]{:S(2)}) copy-start(f32[768]{0:T(1024)} %get-tuple-element.16) | copy-start | bytes 9220
  181.5 7.2 %copy-start.17 = (f32[768]{0:T(1024)S(1)}, f32[768]{0:T(1024)}, u32[]{:S(2)}) copy-start(f32[768]{0:T(1024)} %get-tuple-element.17) | copy-start | bytes 9220
  181.8 6.7 %collective-permute-start.1 = (bf16[2,15,768]{2,1,0:T(8,128)(2,1)S(1)}, bf16[2,15,768]{2,1,0:T(8,128)(2,1)S(1)}, u32[]{:S(2)}, u32[]{:S(2)}) collective-permute-start(bf16[2,15,768]{2,1,0:T(8,128)(2,1)S(1)} %get-tuple-element.45), channel_id=1, source_target_pairs={{1,0},{2,1},{3,2},{4,3},{5,4},{6,5},{7,6},{9,8},{10,9},{11,10},{12... | collective-permute-start | bytes 138248 | tf_op jit(solution)/shard_map/ppermute | solution.py:19
  183.1 5.4 %collective-permute-start = (bf16[2,15,768]{2,1,0:T(8,128)(2,1)S(1)}, bf16[2,15,768]{2,1,0:T(8,128)(2,1)S(1)}, u32[]{:S(2)}, u32[]{:S(2)}) collective-permute-start(bf16[2,15,768]{2,1,0:T(8,128)(2,1)S(1)} %get-tuple-element.44), channel_id=1, source_target_pairs={{0,1},{1,2},{2,3},{3,4},{4,5},{5,6},{6,7},{8,9},{9,10},{10,11},{11... | collective-permute-start | bytes 138248 | tf_op jit(solution)/shard_map/ppermute | solution.py:17
  192.0 119.9 %copy-start.24 = (f32[768]{0:T(1024)S(1)}, f32[768]{0:T(1024)}, u32[]{:S(2)}) copy-start(f32[768]{0:T(1024)} %get-tuple-element.36) | copy-start | bytes 9220
  246.4 68.7 %copy-start.2 = (f32[256,768]{1,0:T(8,128)}, f32[256,768]{1,0:T(8,128)S(1)}, u32[]{:S(2)}) copy-start(f32[256,768]{1,0:T(8,128)S(1)} %get-tuple-element.53) | copy-start | bytes 2359300
  315.1 8.8 %copy-start.27 = (s32[2,16]{1,0:T(2,128)S(1)}, s32[2,16]{1,0:T(2,128)}, u32[]{:S(2)}) copy-start(s32[2,16]{1,0:T(2,128)} %param.13) | copy-start | bytes 388
  317.4 37.2 %all-to-all-start = ((bf16[2,1,128,2304]{3,0,1,2:T(2,128)(2,1)}), bf16[2,1,128,2304]{3,0,1,2:T(2,128)(2,1)S(1)}, u32[]{:S(2)}, u32[]{:S(2)}) async-start(bf16[2,1,128,2304]{3,0,1,2:T(2,128)(2,1)} %copy.46), calls=%async_computation | async-start | bytes 2359296 | tf_op jit(solution)/shard_map/all_to_all | solution.py:105
  323.3 75.7 %all-gather.14.cloned.1.call-start = ((), (), s32[]{:S(2)}) async-start(), calls=%async_computation.6 | async-start | bytes 1216512 | tf_op jit(solution)/shard_map/all_gather | solution.py:98
  364.4 37.4 %copy-start.1 = (bf16[768,2304]{1,0:T(8,128)(2,1)S(1)}, bf16[768,2304]{1,0:T(8,128)(2,1)}, u32[]{:S(2)}) copy-start(bf16[768,2304]{1,0:T(8,128)(2,1)} %param.15) | copy-start | bytes 10616836
  (12 other events, 64.6 us)
Sparse Core Ops, SparseCore 0:
  14.9 98.0 all-gather.5
  114.9 63.9 all-gather.7
  180.8 63.7 all-gather.9
  246.3 65.6 all-gather.11
  325.7 73.2 all-gather.13
where the time goes:
time: 409 us; the launch traced here: 408 us
  waiting for transfers between devices  288 us (70%)
  matrix products  35.9 us (9%)
  local copies, waits for them, and re-layouts  30 us (7%)
  blocking collectives  19.6 us (5%)
  between operations  13.7 us (3%)
  starting transfers between devices  11.6 us (3%)
  other arithmetic  8.98 us (2%)
    all_gather x1, waiting for transfers between devices, shards(): gathered = lax.all_gather(project[..., model:], 'tm', axis=1, tiled=True)  92.8 us
    all_gather x1, waiting for transfers between devices, shards(): lax.all_gather(merge_qkv, ('dp', 'chan'), axis=0, tiled=True)  65.3 us
    all_gather x1, waiting for transfers between devices, shards(): lax.all_gather(point_out, ('dp', 'chan'), axis=0, tiled=True)  52.5 us
    all_gather x1, waiting for transfers between devices, shards(): lax.all_gather(point_in, ('dp', 'chan'), axis=0, tiled=True)  33.3 us
    all_to_all x1, waiting for transfers between devices, shards(): lax.all_to_all(local_qkv.reshape(count_b, 1, span, 3 * model), 'chan', sp...  30.6 us
    all_to_all x1, blocking collectives, shards(): lax.all_to_all(joined, 'chan', split_axis=1, concat_axis=2, tiled=True)  19.6 us
    all_gather x1, waiting for transfers between devices, shards(): lax.all_gather(merge_out, ('dp', 'chan'), axis=0, tiled=True)  11.5 us
    sub x1, matrix products, shards(): attend = jax.nn.softmax(scores, axis=-1).astype(jnp.bfloat16)  10.7 us
  transfers between devices with their start and end apart: 8, of which 6 were waited for; matrix products, arithmetic and copies ran while one was open for 14% of the time, Pallas kernels for 0%

commit v1 on v0

v1 whole, which is shorter than its diff:
```python
import functools

import jax
import jax.numpy as jnp
from jax import lax
from jax.experimental import pallas as pl
from jax.experimental.pallas import tpu as pltpu
from jax.sharding import PartitionSpec as P

D = 768
PAIRS = 6
SPAN = 128
PAD = 16
SEG = SPAN + 2 * PAD
FRAMES = 1024
ROWS = 4
TAPS = 31
MIB = 1024 * 1024
LOG2E = 1.4426950408889634


def normalize(values, gain):
    data = values.astype(jnp.float32)
    center = data - jnp.mean(data, axis=-1, keepdims=True)
    spread = jnp.mean(center * center, axis=-1, keepdims=True)
    return (center * lax.rsqrt(spread + 1e-05) * gain).astype(jnp.bfloat16)


def mm(left, right):
    return jnp.dot(left, right, preferred_element_type=jnp.float32)


def mm_t(left, right):
    return lax.dot_general(left, right, (((1,), (1,)), ((), ())), preferred_element_type=jnp.float32)


def pair_attention(query, key, value_ones, allowed):
    low = lax.broadcasted_iota(jnp.int32, query.shape, 1) < 64
    zero = jnp.zeros_like(query)
    outs = []
    for one in (jnp.where(low, query, zero), jnp.where(low, zero, query)):
        scores = jnp.where(allowed, mm_t(one, key), -1e30)
        top = jnp.max(scores, axis=1, keepdims=True)
        weights = jnp.exp2((scores - top) * LOG2E).astype(jnp.bfloat16)
        out = mm(weights, value_ones)
        outs.append(out[:, :128] / out[:, 128:])
    return jnp.where(low, outs[0], outs[1]).astype(jnp.bfloat16)


def branch_kernel(
    where_ref, h0, h1, h3, h2, g0, g1, g3, g2, gains, wq, wk, wv, wout,
    first_ref, normed_ref, norm_s, raw_s, query_s, context_s,
):
    step = pl.program_id(0)
    col, row, length = where_ref[0], where_ref[1], where_ref[2]
    blocks = (h0, h1, h3, h2, g0, g1, g3, g2)

    @pl.when(step == 0)
    def _():
        for j, block in enumerate(blocks):
            norm_s[j * SPAN : (j + 1) * SPAN] = normalize(block[...], gains[0:1])
        inner_right, inner_left = col < ROWS - 1, col > 0

        def lay(dst, read):
            dst[PAD : PAD + SPAN] = read(0, 0, SPAN)
            dst[SEG + PAD : SEG + PAD + SPAN] = read(4, 0, SPAN)
            last, lo = SPAN - PAD, SPAN
            prev_h, prev_g = read(1, last, SPAN), read(5, last, SPAN)
            next_h, next_g = read(2, 0, PAD), read(6, 0, PAD)
            dst[0:PAD] = jnp.where(inner_left, prev_h, prev_g)
            dst[SEG : SEG + PAD] = jnp.where(inner_left, prev_g, prev_h)
            dst[PAD + SPAN : SEG] = jnp.where(inner_right, next_h, next_g)
            dst[SEG + PAD + SPAN :] = jnp.where(inner_right, next_g, next_h)

        lay(raw_s, lambda j, a, b: blocks[j][a:b])
        lay(query_s, lambda j, a, b: norm_s[j * SPAN + a : j * SPAN + b])

    both = mm(norm_s[...], jnp.concatenate([wk[...], wv[...]], axis=1)).astype(jnp.bfloat16)
    key, value = both[:, :128], both[:, 128:]
    value_ones = jnp.concatenate([value, jnp.ones_like(value)], axis=1)
    query = mm(query_s[...], wq[...]).astype(jnp.bfloat16) * jnp.bfloat16(0.125)
    lane = lax.broadcasted_iota(jnp.int32, (1, SPAN), 1)
    starts = []
    for r in (row, 1 - row):
        for k in (0, 1, 3, 2):
            starts.append((r * ROWS + lax.rem(col + ROWS - k, ROWS)) * SPAN)
    allowed = jnp.concatenate([lane + s for s in starts], axis=1) < length
    columns = pl.ds(pl.multiple_of(step * 128, 128), 128)
    for seg in range(2):
        at = slice(seg * SEG, (seg + 1) * SEG)
        context_s[at, columns] = pair_attention(query[at], key, value_ones, allowed)

    @pl.when(step == PAIRS - 1)
    def _():
        first = (raw_s[...].astype(jnp.float32) + mm(context_s[...], wout[...])).astype(jnp.bfloat16)
        first_ref[...] = first
        normed_ref[...] = normalize(first, gains[1:2])


def run_branch(where, blocks, gains, qkv, wout):
    whole = lambda shape: pl.BlockSpec(shape, lambda p: (0,) * len(shape))
    return pl.pallas_call(
        branch_kernel,
        grid=(PAIRS,),
        in_specs=[pl.BlockSpec(memory_space=pltpu.SMEM)]
        + [whole((SPAN, D))] * 8
        + [
            whole((3, D)),
            pl.BlockSpec((D, 128), lambda p: (0, p)),
            pl.BlockSpec((D, 128), lambda p: (0, PAIRS + p)),
            pl.BlockSpec((D, 128), lambda p: (0, 2 * PAIRS + p)),
            whole((D, D)),
        ],
        out_specs=[whole((2 * SEG, D))] * 2,
        out_shape=[jax.ShapeDtypeStruct((2 * SEG, D), jnp.bfloat16)] * 2,
        scratch_shapes=[
            pltpu.VMEM((FRAMES, D), jnp.bfloat16),
            pltpu.VMEM((2 * SEG, D), jnp.bfloat16),
            pltpu.VMEM((2 * SEG, D), jnp.bfloat16),
            pltpu.VMEM((2 * SEG, D), jnp.bfloat16),
        ],
        compiler_params=pltpu.CompilerParams(vmem_limit_bytes=48 * MIB),
        cost_estimate=pl.CostEstimate(
            flops=6 * 10**9, bytes_accessed=8 * 10**6, transcendentals=4 * 10**6
        ),
        name="branch",
    )(where, *blocks, gains, qkv, qkv, qkv, wout)


def conv_kernel(where_ref, normed, first, wide, back, taps, out_ref, gated_s, swish_s):
    col, row, length = where_ref[0], where_ref[1], where_ref[2]
    for seg in range(2):
        at = slice(seg * SEG, (seg + 1) * SEG)
        begin = ((row if seg == 0 else 1 - row) * ROWS + col) * SPAN - PAD
        frame = begin + lax.broadcasted_iota(jnp.int32, (SEG, 1), 0)
        live = (frame >= 0) & (frame < length)
        rows = normed[at]
        for chunk in range(PAIRS):
            lo = chunk * 128
            value = mm(rows, wide[:, lo : lo + 128])
            gate = mm(rows, wide[:, D + lo : D + lo + 128])
            gated = jnp.where(live, value * jax.nn.sigmoid(gate), 0.0)
            gated_s[chunk, at] = gated.astype(jnp.bfloat16).astype(jnp.float32)
    for seg in range(2):
        for chunk in range(PAIRS):
            lo = chunk * 128
            mixed = jnp.zeros((SPAN, 128), jnp.float32)
            for o in range(TAPS):
                begin = seg * SEG + PAD - TAPS // 2 + o
                tap = taps[o : o + 1, lo : lo + 128]
                mixed = mixed + tap * gated_s[chunk, begin : begin + SPAN]
            swish = mixed * jax.nn.sigmoid(mixed)
            swish_s[seg * SPAN : (seg + 1) * SPAN, lo : lo + 128] = swish.astype(jnp.bfloat16)
    out = mm(swish_s[...], back[...])
    for seg in range(2):
        kept = first[seg * SEG + PAD : seg * SEG + PAD + SPAN].astype(jnp.float32)
        out_ref[seg * SPAN : (seg + 1) * SPAN] = (
            kept + out[seg * SPAN : (seg + 1) * SPAN]
        ).astype(jnp.bfloat16)


def run_conv(where, normed, first, weights, taps):
    return pl.pallas_call(
        conv_kernel,
        grid=(1,),
        in_specs=[
            pl.BlockSpec(memory_space=pltpu.SMEM),
            pl.BlockSpec((2 * SEG, D), lambda i: (0, 0)),
            pl.BlockSpec((2 * SEG, D), lambda i: (0, 0)),
            pl.BlockSpec((D, 2 * D), lambda i: (0, 0)),
            pl.BlockSpec((D, D), lambda i: (0, 2)),
            pl.BlockSpec((TAPS, D), lambda i: (0, 0)),
        ],
        out_specs=pl.BlockSpec((2 * SPAN, D), lambda i: (0, 0)),
        out_shape=jax.ShapeDtypeStruct((2 * SPAN, D), jnp.bfloat16),
        scratch_shapes=[
            pltpu.VMEM((PAIRS, 2 * SEG, 128), jnp.float32),
            pltpu.VMEM((2 * SPAN, D), jnp.bfloat16),
        ],
        compiler_params=pltpu.CompilerParams(vmem_limit_bytes=48 * MIB),
        cost_estimate=pl.CostEstimate(
            flops=2 * 10**9, bytes_accessed=8 * 10**6, transcendentals=10**6
        ),
        name="conv",
    )(where, normed, first, weights, weights, taps)


def merge_kernel(live, block, gains, wq, wk, wv, wout, out_ref, norm_s, context_s):
    step = pl.program_id(0)

    @pl.when(step == 0)
    def _():
        norm_s[...] = normalize(block[...], gains[2:3])

    projected = mm(norm_s[...], jnp.concatenate([wk[...], wv[...]], axis=1)).astype(jnp.bfloat16)
    key, value = projected[:, :128], projected[:, 128:]
    value_ones = jnp.concatenate([value, jnp.ones_like(value)], axis=1)
    query = mm(norm_s[...], wq[...]).astype(jnp.bfloat16) * jnp.bfloat16(0.125)
    count = block.shape[0]
    mine = lax.broadcasted_iota(jnp.int32, (count, count), 0) & 15
    theirs = lax.broadcasted_iota(jnp.int32, (count, count), 1) & 15
    allowed = (mine == theirs) & (live[...] > 0)
    columns = pl.ds(pl.multiple_of(step * 128, 128), 128)
    context_s[:, columns] = pair_attention(query, key, value_ones, allowed)

    @pl.when(step == PAIRS - 1)
    def _():
        out = block[...].astype(jnp.float32) + mm(context_s[...], wout[...])
        out_ref[...] = out.astype(jnp.bfloat16)


def run_merge(live, block, gains, weights, first_column):
    whole = lambda shape: pl.BlockSpec(shape, lambda p: (0,) * len(shape))
    count = block.shape[0]
    base = first_column // 128
    return pl.pallas_call(
        merge_kernel,
        grid=(PAIRS,),
        in_specs=[
            whole((1, count)),
            whole((count, D)),
            whole((3, D)),
            pl.BlockSpec((D, 128), lambda p: (0, base + p)),
            pl.BlockSpec((D, 128), lambda p: (0, base + PAIRS + p)),
            pl.BlockSpec((D, 128), lambda p: (0, base + 2 * PAIRS + p)),
            pl.BlockSpec((D, D), lambda p: (0, base // PAIRS + 3)),
        ],
        out_specs=whole((count, D)),
        out_shape=jax.ShapeDtypeStruct((count, D), jnp.bfloat16),
        scratch_shapes=[
            pltpu.VMEM((count, D), jnp.bfloat16),
            pltpu.VMEM((count, D), jnp.bfloat16),
        ],
        compiler_params=pltpu.CompilerParams(vmem_limit_bytes=48 * MIB),
        cost_estimate=pl.CostEstimate(
            flops=2 * 10**9, bytes_accessed=8 * 10**6, transcendentals=10**6
        ),
        name="merge",
    )(live, block, gains, weights, weights, weights, weights)


def shards(
    features, lengths, chan_valid, norm_gains, branch_qkv, branch_out, depth_taps,
    point_in, point_out, merge_qkv, merge_out,
):
    place = lax.axis_index("tm")
    row, col = place // ROWS, place % ROWS
    count = 2 * ROWS
    packed = jnp.concatenate([point_in, point_out, merge_qkv, merge_out], axis=1)
    weights = lax.all_gather(packed, ("dp", "chan"), axis=0, tiled=True)

    other_row = [(i, (i + ROWS) % count) for i in range(count)]

    def along(values, k):
        return lax.ppermute(
            values, "tm", [(i, i // ROWS * ROWS + (i + k) % ROWS) for i in range(count)]
        )

    home = lax.dynamic_index_in_dim(features[:, 0], row, 0, keepdims=False)
    away = lax.dynamic_index_in_dim(features[:, 0], 1 - row, 0, keepdims=False)
    swapped = lax.ppermute(away, "tm", other_row)
    blocks = [home] + [along(home, k) for k in (1, 3, 2)]
    blocks += [swapped] + [along(swapped, k) for k in (1, 3, 2)]
    where = jnp.stack([col, row, lengths[row]]).astype(jnp.int32)
    first, normed = run_branch(where, blocks, norm_gains, branch_qkv, branch_out)
    second = run_conv(where, normed, first, weights, depth_taps.astype(jnp.float32))
    back = lax.ppermute(second[SPAN:], "tm", other_row)
    second = jnp.concatenate([second[:SPAN], back], axis=0)
    channels = lax.axis_size("chan")
    part = 2 * SPAN // channels
    joined = lax.all_to_all(
        second.reshape(channels, part, D), "chan", split_axis=0, concat_axis=0, tiled=True
    )
    mine = jnp.where(lax.axis_index("chan") < channels // 2, row, 1 - row)
    live = jnp.repeat(chan_valid[mine], part)[None]
    merged = run_merge(live, joined.reshape(channels * part, D), norm_gains, weights, 3 * D)
    returned = lax.all_to_all(
        merged.reshape(channels, part, D), "chan", split_axis=0, concat_axis=0, tiled=True
    ).reshape(2, SPAN, D)
    return jnp.where(row == 0, returned, returned[::-1])[:, None]


def solution(mesh):
    placed = (
        P("dp", "chan", "tm", None),
        P("dp"),
        P("dp", None),
        P(),
        P(),
        P(),
        P(),
        P(("dp", "chan"), None),
        P(("dp", "chan"), None),
        P(("dp", "chan"), None),
        P(("dp", "chan"), None),
    )
    return jax.shard_map(
        shards, mesh=mesh, in_specs=placed, out_specs=P("dp", "chan", "tm", None), check_vma=False
    )
```

time: 409 us -> 156 us (0.38)
  waiting for transfers between devices: 288 us -> 74.3 us
  matrix products: 35.9 us -> 0 us
  Pallas kernels: 0 us -> 33.4 us
  local copies, waits for them, and re-layouts: 30 us -> 4.5 us
  blocking collectives: 19.6 us -> 0 us
  starting transfers between devices: 11.6 us -> 25.3 us
  other arithmetic: 8.98 us -> 4.73 us
    all_gather x5 -> x1, waiting for transfers between devices: 255 us -> 31.8 us  [shards(): weights = lax.all_gather(packed, ('dp', 'chan'), axis=0, tiled=True)]
    pallas_call x0 -> x3, Pallas kernels: none -> 33.4 us  [the longest x1 18.4 us: run_branch(): pl.pallas_call(branch_kernel, grid=(PAIRS,), in_specs=[pl.BlockSpec(memor...]
    dot_general x8 -> x0, matrix products: 22.5 us -> none  [the longest x1 8.11 us: shards(): jnp.einsum('bhqk,bkhd->bqhd', attend, valued, preferred_element_type=jnp....]
    all_to_all x1 -> x0, blocking collectives: 19.6 us -> none  [shards(): lax.all_to_all(joined, 'chan', split_axis=1, concat_axis=2, tiled=True)]
    slice x11 -> x1, local copies, waits for them, and re-layouts: 18.9 us -> 0.03 us  [shards(): second = jnp.concatenate([second[:SPAN], back], axis=0)]
    ppermute x2 -> x8, waiting for transfers between devices: 0.01 us -> 14.2 us  [the longest x6 9.09 us: along(): lax.ppermute(values, 'tm', [(i, i // ROWS * ROWS + (i + k) % ROWS) for i...]
    sub x2 -> x0, matrix products: 13.4 us -> none  [the longest x1 10.7 us: shards(): attend = jax.nn.softmax(scores, axis=-1).astype(jnp.bfloat16)]
    ppermute x2 -> x8, starting transfers between devices: 5.46 us -> 15.2 us  [the longest x6 8.57 us: along(): lax.ppermute(values, 'tm', [(i, i // ROWS * ROWS + (i + k) % ROWS) for i...]
  transfers between devices with their start and end apart: 8 -> 11, of which waited for: 6 -> 7; matrix products, arithmetic and copies ran while one was open for 14% -> 2% of each run, Pallas kernels for 0% -> 12%
where the time goes in v1:
time: 156 us
  waiting for transfers between devices  74.3 us (48%)
  Pallas kernels  33.4 us (21%)
  starting transfers between devices  25.3 us (16%)
  between operations  13.5 us (9%)
  other arithmetic  4.73 us (3%)
  local copies, waits for them, and re-layouts  4.5 us (3%)
    all_gather x1, waiting for transfers between devices, shards(): weights = lax.all_gather(packed, ('dp', 'chan'), axis=0, tiled=True)  31.8 us
    pallas_call x1, Pallas kernels, run_branch(): pl.pallas_call(branch_kernel, grid=(PAIRS,), in_specs=[pl.BlockSpec(memor...  18.4 us
    all_to_all x1, waiting for transfers between devices, shards(): lax.all_to_all(second.reshape(channels, part, D), 'chan', split_axis=0, c...  14.4 us
    all_to_all x1, waiting for transfers between devices, shards(): lax.all_to_all(merged.reshape(channels, part, D), 'chan', split_axis=0, c...  14 us
    ppermute x6, waiting for transfers between devices, along(): lax.ppermute(values, 'tm', [(i, i // ROWS * ROWS + (i + k) % ROWS) for i...  9.09 us
    pallas_call x1, Pallas kernels, run_merge(): pl.pallas_call(merge_kernel, grid=(PAIRS,), in_specs=[whole((1, count)),...  8.86 us
    ppermute x6, starting transfers between devices, along(): lax.ppermute(values, 'tm', [(i, i // ROWS * ROWS + (i + k) % ROWS) for i...  8.57 us
    all_to_all x1, starting transfers between devices, shards(): lax.all_to_all(second.reshape(channels, part, D), 'chan', split_axis=0, c...  6.69 us
  transfers between devices with their start and end apart: 11, of which 7 were waited for; matrix products, arithmetic and copies ran while one was open for 2% of the time, Pallas kernels for 12%

profile of v1, /device:TPU:1, one launch (start us, length us, event | category | flops | bytes accessed | tf_op | source)
XLA Modules:
  0.0 155.7 jit_solution(7706567708059950228)
XLA Ops:
  6.5 1.7 %pad_maximum_fusion.1 = bf16[24,5376]{1,0:T(8,128)(2,1)} fusion(bf16[24,768]{1,0:T(8,128)(2,1)} %param.21, bf16[24,2304]{1,0:T(8,128)(2,1)} %param.20, bf16[24,768]{1,0:T(8,128)(2,1)} %param.19, bf16[24,1536]{1,0:T(8,128)(2,1)} %param.18), kind=kLoop, calls=%fused_computation.3 | loop fusion | flops 1032192 | bytes 516096 | tf_op jit(solution)/shard_map/concatenate | solution.py:249
  8.3 1.1 dynamic-slice_bitcast_fusion
  9.4 3.8 %collective-permute-start.3 = (bf16[128,768]{1,0:T(8,128)(2,1)S(1)}, bf16[128,768]{1,0:T(8,128)(2,1)S(1)}, u32[]{:S(2)}, u32[]{:S(2)}) collective-permute-start(bf16[128,768]{1,0:T(8,128)(2,1)S(1)} %get-tuple-element.11), channel_id=1, source_target_pairs={{0,4},{1,5},{2,6},{3,7},{4,0},{5,1},{6,2},{7,3},{8,12},{9,13},{10,... | collective-permute-start | bytes 589832 | tf_op jit(solution)/shard_map/ppermute | solution.py:261
  13.2 1.2 collective-permute-start
  14.4 1.5 collective-permute-start.1
  15.9 1.5 collective-permute-start.2
  17.4 1.4 collective-permute-start.4
  18.8 1.3 collective-permute-start.5
  20.1 1.7 %collective-permute-start.6 = (bf16[128,768]{1,0:T(8,128)(2,1)S(1)}, bf16[128,768]{1,0:T(8,128)(2,1)S(1)}, u32[]{:S(2)}, u32[]{:S(2)}) collective-permute-start(bf16[128,768]{1,0:T(8,128)(2,1)S(1)} %collective-permute-done.3.g0), channel_id=1, source_target_pairs={{0,2},{1,3},{2,0},{3,1},{4,6},{5,7},{6,4},{7,5},{8,10},{9,11},{10,... | collective-permute-start | bytes 589832 | tf_op jit(solution)/shard_map/ppermute | solution.py:255
  21.8 1.2 dynamic_slice.14
  25.1 3.5 %collective-permute-done.4.g1 = bf16[128,768]{1,0:T(8,128)(2,1)S(1)} collective-permute-done((bf16[128,768]{1,0:T(8,128)(2,1)S(1)}, bf16[128,768]{1,0:T(8,128)(2,1)S(1)}, u32[]{:S(2)}, u32[]{:S(2)}) %collective-permute-start.4) | collective-permute-done | bytes 196640 | tf_op jit(solution)/shard_map/ppermute | solution.py:255
  28.6 4.9 %collective-permute-done.6.g2 = bf16[128,768]{1,0:T(8,128)(2,1)S(1)} collective-permute-done((bf16[128,768]{1,0:T(8,128)(2,1)S(1)}, bf16[128,768]{1,0:T(8,128)(2,1)S(1)}, u32[]{:S(2)}, u32[]{:S(2)}) %collective-permute-start.6) | collective-permute-done | bytes 196640 | tf_op jit(solution)/shard_map/ppermute | solution.py:255
  34.2 1.3 copy-done.3
  35.5 18.4 %branch.1 = (bf16[320,768]{1,0:T(8,128)(2,1)S(1)}, bf16[320,768]{1,0:T(8,128)(2,1)S(1)}) custom-call(s32[3]{0:T(128)S(1)} %pad_add_fusion.where_ref, bf16[128,768]{1,0:T(8,128)(2,1)S(1)} %get-tuple-element.12.h0, bf16[128,768]{1,0:T(8,128)(2,1)S(1)} %collective-permute-done.h1, bf16[128,768]{1,0:T(8,128)(2,1)S(1)} %collective-permute-done.1.h3, ...), custom_call_target="tpu_custom_call" | custom-call | flops 6000000000 | bytes 8000000 | tf_op jit(solution)/shard_map/branch/pallas_call | solution.py:102
  53.9 31.8 %all-gather.2.cloned.1.call-done.wide.back.wq.wk.wv.wout = bf16[768,5376]{1,0:T(8,128)(2,1)} async-done(((bf16[24,5376]{1,0:T(8,128)(2,1)}), bf16[768,5376]{1,0:T(8,128)(2,1)}) %all-gather.2.cloned.1.call-update) | async-done | bytes 8257552 | tf_op jit(solution)/shard_map/all_gather | solution.py:250
  85.7 6.2 %conv.1 = bf16[256,768]{1,0:T(8,128)(2,1)S(1)} custom-call(s32[3]{0:T(128)S(1)} %pad_add_fusion.where_ref, bf16[320,768]{1,0:T(8,128)(2,1)S(1)} %get-tuple-element.7.normed, bf16[320,768]{1,0:T(8,128)(2,1)S(1)} %get-tuple-element.8.first, bf16[768,5376]{1,0:T(8,128)(2,1)} %all-gather.2.cloned.1.call-done.wide.back.wq.wk.wv.wout, ...), custom_call_target="tpu_custom_call" | custom-call | flops 2000000000 | bytes 8000000 | tf_op jit(solution)/shard_map/conv/pallas_call | solution.py:163
  91.9 2.8 %collective-permute-start.7 = (bf16[128,768]{1,0:T(8,128)(2,1)S(1)}, bf16[128,768]{1,0:T(8,128)(2,1)S(1)}, u32[]{:S(2)}, u32[]{:S(2)}) collective-permute-start(bf16[128,768]{1,0:T(8,128)(2,1)S(1)} %get-tuple-element.10), channel_id=1, source_target_pairs={{0,4},{1,5},{2,6},{3,7},{4,0},{5,1},{6,2},{7,3},{8,12},{9,13},{10,... | collective-permute-start | bytes 589832 | tf_op jit(solution)/shard_map/ppermute | solution.py:267
  94.7 5.1 %collective-permute-done.7 = bf16[128,768]{1,0:T(8,128)(2,1)S(1)} collective-permute-done((bf16[128,768]{1,0:T(8,128)(2,1)S(1)}, bf16[128,768]{1,0:T(8,128)(2,1)S(1)}, u32[]{:S(2)}, u32[]{:S(2)}) %collective-permute-start.7) | collective-permute-done | bytes 196640 | tf_op jit(solution)/shard_map/ppermute | solution.py:267
  100.5 6.7 %all-to-all-start = ((bf16[16,16,768]{2,1,0:T(8,128)(2,1)}), bf16[16,16,768]{2,1,0:T(8,128)(2,1)S(1)}, u32[]{:S(2)}, u32[]{:S(2)}) async-start(bf16[16,16,768]{2,1,0:T(8,128)(2,1)} %bitcast.5), calls=%async_computation | async-start | bytes 786432 | tf_op jit(solution)/shard_map/all_to_all | solution.py:271
  107.4 14.4 %all-to-all-done = bf16[16,16,768]{2,1,0:T(8,128)(2,1)S(1)} async-done(((bf16[16,16,768]{2,1,0:T(8,128)(2,1)}), bf16[16,16,768]{2,1,0:T(8,128)(2,1)S(1)}, u32[]{:S(2)}, u32[]{:S(2)}) %all-to-all-start) | async-done | bytes 393248 | tf_op jit(solution)/shard_map/all_to_all | solution.py:271
  121.8 8.9 %merge.1 = bf16[256,768]{1,0:T(8,128)(2,1)} custom-call(s32[1,256]{1,0:T(1,128)S(1)} %broadcast_in_dim_reshape.3.live, bf16[256,768]{1,0:T(8,128)(2,1)S(1)} %bitcast.14, f32[3,768]{1,0:T(4,128)S(1)} %copy-done.2, bf16[768,5376]{1,0:T(8,128)(2,1)} %all-gather.2.cloned.1.call-done.wide.back.wq.wk.wv.wout, ...), custom_call_target="tpu_custom_call" | custom-call | flops 2000000000 | bytes 8000000 | tf_op jit(solution)/shard_map/merge/pallas_call | solution.py:216
  130.6 3.5 %all-to-all-start.1 = ((bf16[16,16,768]{2,1,0:T(8,128)(2,1)}), bf16[16,16,768]{2,1,0:T(8,128)(2,1)S(1)}, u32[]{:S(2)}, u32[]{:S(2)}) async-start(bf16[16,16,768]{2,1,0:T(8,128)(2,1)} %bitcast.7), calls=%async_computation.1 | async-start | bytes 786432 | tf_op jit(solution)/shard_map/all_to_all | solution.py:277
  134.1 14.0 %all-to-all-done.1 = bf16[16,16,768]{2,1,0:T(8,128)(2,1)S(1)} async-done(((bf16[16,16,768]{2,1,0:T(8,128)(2,1)}), bf16[16,16,768]{2,1,0:T(8,128)(2,1)S(1)}, u32[]{:S(2)}, u32[]{:S(2)}) %all-to-all-start.1) | async-done | bytes 393248 | tf_op jit(solution)/shard_map/all_to_all | solution.py:277
  148.1 0.8 fusion
  (21 shorter events, 3.8 us)
Async XLA Ops:
  6.5 100.7 %copy-start = (s32[2,16]{1,0:T(2,128)S(1)}, s32[2,16]{1,0:T(2,128)}, u32[]{:S(2)}) copy-start(s32[2,16]{1,0:T(2,128)} %param.13) | copy-start | bytes 388
  6.5 79.2 %all-gather.2.cloned.1.call-start = ((), (), s32[]{:S(2)}) async-start(), calls=%async_computation.2 | async-start | bytes 8515584 | tf_op jit(solution)/shard_map/all_gather | solution.py:250
  9.4 8.0 %collective-permute-start.3 = (bf16[128,768]{1,0:T(8,128)(2,1)S(1)}, bf16[128,768]{1,0:T(8,128)(2,1)S(1)}, u32[]{:S(2)}, u32[]{:S(2)}) collective-permute-start(bf16[128,768]{1,0:T(8,128)(2,1)S(1)} %get-tuple-element.11), channel_id=1, source_target_pairs={{0,4},{1,5},{2,6},{3,7},{4,0},{5,1},{6,2},{7,3},{8,12},{9,13},{10,... | collective-permute-start | bytes 589832 | tf_op jit(solution)/shard_map/ppermute | solution.py:261
  13.2 6.9 %collective-permute-start = (bf16[128,768]{1,0:T(8,128)(2,1)S(1)}, bf16[128,768]{1,0:T(8,128)(2,1)S(1)}, u32[]{:S(2)}, u32[]{:S(2)}) collective-permute-start(bf16[128,768]{1,0:T(8,128)(2,1)S(1)} %get-tuple-element.12.h0), channel_id=1, source_target_pairs={{0,1},{1,2},{2,3},{3,0},{4,5},{5,6},{6,7},{7,4},{8,9},{9,10},{10,1... | collective-permute-start | bytes 589832 | tf_op jit(solution)/shard_map/ppermute | solution.py:255
  14.4 10.0 %collective-permute-start.1 = (bf16[128,768]{1,0:T(8,128)(2,1)S(1)}, bf16[128,768]{1,0:T(8,128)(2,1)S(1)}, u32[]{:S(2)}, u32[]{:S(2)}) collective-permute-start(bf16[128,768]{1,0:T(8,128)(2,1)S(1)} %get-tuple-element.12.h0), channel_id=1, source_target_pairs={{0,3},{1,0},{2,1},{3,2},{4,7},{5,4},{6,5},{7,6},{8,11},{9,8},{10,9... | collective-permute-start | bytes 589832 | tf_op jit(solution)/shard_map/ppermute | solution.py:255
  15.9 9.2 %collective-permute-start.2 = (bf16[128,768]{1,0:T(8,128)(2,1)S(1)}, bf16[128,768]{1,0:T(8,128)(2,1)S(1)}, u32[]{:S(2)}, u32[]{:S(2)}) collective-permute-start(bf16[128,768]{1,0:T(8,128)(2,1)S(1)} %get-tuple-element.12.h0), channel_id=1, source_target_pairs={{0,2},{1,3},{2,0},{3,1},{4,6},{5,7},{6,4},{7,5},{8,10},{9,11},{10,... | collective-permute-start | bytes 589832 | tf_op jit(solution)/shard_map/ppermute | solution.py:255
  17.4 11.2 %collective-permute-start.4 = (bf16[128,768]{1,0:T(8,128)(2,1)S(1)}, bf16[128,768]{1,0:T(8,128)(2,1)S(1)}, u32[]{:S(2)}, u32[]{:S(2)}) collective-permute-start(bf16[128,768]{1,0:T(8,128)(2,1)S(1)} %collective-permute-done.3.g0), channel_id=1, source_target_pairs={{0,1},{1,2},{2,3},{3,0},{4,5},{5,6},{6,7},{7,4},{8,9},{9,10},{10,1... | collective-permute-start | bytes 589832 | tf_op jit(solution)/shard_map/ppermute | solution.py:255
  18.8 9.9 %collective-permute-start.5 = (bf16[128,768]{1,0:T(8,128)(2,1)S(1)}, bf16[128,768]{1,0:T(8,128)(2,1)S(1)}, u32[]{:S(2)}, u32[]{:S(2)}) collective-permute-start(bf16[128,768]{1,0:T(8,128)(2,1)S(1)} %collective-permute-done.3.g0), channel_id=1, source_target_pairs={{0,3},{1,0},{2,1},{3,2},{4,7},{5,4},{6,5},{7,6},{8,11},{9,8},{10,9... | collective-permute-start | bytes 589832 | tf_op jit(solution)/shard_map/ppermute | solution.py:255
  20.1 13.4 %collective-permute-start.6 = (bf16[128,768]{1,0:T(8,128)(2,1)S(1)}, bf16[128,768]{1,0:T(8,128)(2,1)S(1)}, u32[]{:S(2)}, u32[]{:S(2)}) collective-permute-start(bf16[128,768]{1,0:T(8,128)(2,1)S(1)} %collective-permute-done.3.g0), channel_id=1, source_target_pairs={{0,2},{1,3},{2,0},{3,1},{4,6},{5,7},{6,4},{7,5},{8,10},{9,11},{10,... | collective-permute-start | bytes 589832 | tf_op jit(solution)/shard_map/ppermute | solution.py:255
  33.5 0.7 copy-start.1
  34.2 1.3 copy-start.3
  85.7 36.1 %copy-start.2 = (f32[3,768]{1,0:T(4,128)S(1)}, f32[3,768]{1,0:T(4,128)}, u32[]{:S(2)}) copy-start(f32[3,768]{1,0:T(4,128)} %gains.3) | copy-start | bytes 27652
  91.9 7.8 %collective-permute-start.7 = (bf16[128,768]{1,0:T(8,128)(2,1)S(1)}, bf16[128,768]{1,0:T(8,128)(2,1)S(1)}, u32[]{:S(2)}, u32[]{:S(2)}) collective-permute-start(bf16[128,768]{1,0:T(8,128)(2,1)S(1)} %get-tuple-element.10), channel_id=1, source_target_pairs={{0,4},{1,5},{2,6},{3,7},{4,0},{5,1},{6,2},{7,3},{8,12},{9,13},{10,... | collective-permute-start | bytes 589832 | tf_op jit(solution)/shard_map/ppermute | solution.py:267
  100.5 21.2 %all-to-all-start = ((bf16[16,16,768]{2,1,0:T(8,128)(2,1)}), bf16[16,16,768]{2,1,0:T(8,128)(2,1)S(1)}, u32[]{:S(2)}, u32[]{:S(2)}) async-start(bf16[16,16,768]{2,1,0:T(8,128)(2,1)} %bitcast.5), calls=%async_computation | async-start | bytes 786432 | tf_op jit(solution)/shard_map/all_to_all | solution.py:271
  130.6 17.4 %all-to-all-start.1 = ((bf16[16,16,768]{2,1,0:T(8,128)(2,1)}), bf16[16,16,768]{2,1,0:T(8,128)(2,1)S(1)}, u32[]{:S(2)}, u32[]{:S(2)}) async-start(bf16[16,16,768]{2,1,0:T(8,128)(2,1)} %bitcast.7), calls=%async_computation.1 | async-start | bytes 786432 | tf_op jit(solution)/shard_map/all_to_all | solution.py:277
Sparse Core Ops, SparseCore 0:
  9.2 76.4 all-gather.1

commit v2 on v0

v2 whole, which is shorter than its diff:
```python
import jax
import jax.numpy as jnp
from jax import lax
from jax.experimental import pallas as pl
from jax.experimental.pallas import tpu as pltpu
from jax.sharding import PartitionSpec as P

D = 768
PAIRS = 6
SPAN = 128
PAD = 16
SEG = SPAN + 2 * PAD
FRAMES = 1024
ROWS = 4
TAPS = 31
MIB = 1024 * 1024
LOG2E = 1.4426950408889634


def normalize(values, gain):
    data = values.astype(jnp.float32)
    center = data - jnp.mean(data, axis=-1, keepdims=True)
    spread = jnp.mean(center * center, axis=-1, keepdims=True)
    return (center * lax.rsqrt(spread + 1e-05) * gain).astype(jnp.bfloat16)


def mm(left, right):
    return jnp.dot(left, right, preferred_element_type=jnp.float32)


def mm_t(left, right):
    return lax.dot_general(left, right, (((1,), (1,)), ((), ())), preferred_element_type=jnp.float32)


def pair_attention(query, key, value_ones, allowed):
    low = lax.broadcasted_iota(jnp.int32, query.shape, 1) < 64
    zero = jnp.zeros_like(query)
    outs = []
    for one in (jnp.where(low, query, zero), jnp.where(low, zero, query)):
        scores = jnp.where(allowed, mm_t(one, key), -1e30)
        top = jnp.max(scores, axis=1, keepdims=True)
        weights = jnp.exp2((scores - top) * LOG2E).astype(jnp.bfloat16)
        out = mm(weights, value_ones)
        outs.append(out[:, :128] / out[:, 128:])
    return jnp.where(low, outs[0], outs[1]).astype(jnp.bfloat16)


def with_ones(both):
    value = both[:, 128:]
    return both[:, :128], jnp.concatenate([value, jnp.ones_like(value)], axis=1)


def bf16(*shape):
    return jax.ShapeDtypeStruct(shape, jnp.bfloat16)


def call(kernel, outs, scratch, cost, name, operands, where=None, limit=24):
    vmem = pl.BlockSpec(memory_space=pltpu.VMEM)
    flops, moved, exps = cost
    lead = [] if where is None else [where]
    return pl.pallas_call(
        kernel,
        in_specs=[pl.BlockSpec(memory_space=pltpu.SMEM)] * len(lead)
        + [pl.BlockSpec(memory_space=pltpu.HBM) if isinstance(x, Far) else vmem for x in operands],
        out_specs=[vmem] * len(outs),
        out_shape=outs,
        scratch_shapes=scratch,
        compiler_params=pltpu.CompilerParams(vmem_limit_bytes=limit * MIB),
        cost_estimate=pl.CostEstimate(flops=flops, bytes_accessed=moved, transcendentals=exps),
        name=name,
    )(*lead, *[x.array if isinstance(x, Far) else x for x in operands])


class Far:
    def __init__(self, array):
        self.array = array


def prepare_kernel(
    pin, pout, mqkv, mout, features, out_ref, spread_ref, pin_s, pout_s, mqkv_s, mout_s, sems
):
    shards_in = ((pin, pin_s), (pout, pout_s), (mqkv, mqkv_s), (mout, mout_s))
    blocks = [(features.at[t // ROWS, 0], spread_ref.at[t]) for t in range(2 * ROWS)]
    copies = [
        pltpu.make_async_copy(a, b, sems.at[n]) for n, (a, b) in enumerate((*shards_in, *blocks))
    ]
    for copy in copies:
        copy.start()
    for copy in copies[:4]:
        copy.wait()
    half = D // 2
    col = lax.rem(lax.axis_index("tm"), ROWS)
    for h in range(2):
        lo, base = h * half, h * 2 * D
        out_ref[:, base : base + half] = pin_s[:, lo : lo + half]
        out_ref[:, base + half : base + 2 * half] = pin_s[:, D + lo : D + lo + half]
        out_ref[:, base + 2 * half : base + 3 * half] = pout_s[:, lo : lo + half]

        @pl.when(col < ROWS - 1)
        def _():
            for n in range(3):
                lanes = pl.ds(pl.multiple_of(n * D + (2 * col + h) * 128, 128), 128)
                at = base + 3 * half + n * 128
                out_ref[:, at : at + 128] = mqkv_s[:, lanes]

        @pl.when(col == ROWS - 1)
        def _():
            out_ref[:, base + 3 * half : base + 4 * half] = mout_s[:, lo : lo + half]

    for copy in copies[4:]:
        copy.wait()


def run_prepare(features, *shards_in):
    height, count = shards_in[0].shape[0], 2 * ROWS
    scratch = [pltpu.VMEM(w.shape, w.dtype) for w in shards_in]
    return call(
        prepare_kernel, [bf16(height, 4 * D), bf16(count, SPAN, D)],
        scratch + [pltpu.SemaphoreType.DMA((4 + count,))],
        (0, 3 * 10**6, 0), "prepare", [Far(w) for w in (*shards_in, features)], limit=56,
    )


def my_core():
    return lax.rem(lax.axis_index("chan"), 2)


def my_length(lengths):
    return lengths[lax.axis_index("tm") // ROWS]


def attend_pairs(length, norm_s, query_s, weights, context_ref):
    allowed = lax.broadcasted_iota(jnp.int32, (1, FRAMES), 1) < length
    query_two = mm(query_s[...], weights[:, :256]).astype(jnp.bfloat16) * jnp.bfloat16(0.125)
    for n in range(2):
        lanes = slice(n * 128, (n + 1) * 128)
        both = jnp.concatenate([weights[:, 256:512][:, lanes], weights[:, 512:][:, lanes]], axis=1)
        key, value_ones = with_ones(mm(norm_s[...], both).astype(jnp.bfloat16))
        context_ref[:, lanes] = pair_attention(query_two[:, lanes], key, value_ones, allowed)


def attend_a_kernel(
    lengths, blocks, gains, qkv, wout,
    context_ref, norm_s, query_s, raw_s, group_b, group_c, wout_ref, group_a, sems,
):
    copies = []
    for n, group in enumerate((group_a, group_b, group_c)):
        for m in range(3):
            columns = pl.ds(m * D + n * 256, 256)
            copies.append((qkv.at[:, columns], group.at[:, pl.ds(m * 256, 256)]))
    copies.append((wout, wout_ref))
    copies = [pltpu.make_async_copy(a, b, sems.at[n]) for n, (a, b) in enumerate(copies)]
    for copy in copies:
        copy.start()
    for b in range(2 * ROWS):
        norm_s[b * SPAN : (b + 1) * SPAN] = normalize(blocks[b], gains[0:1])
    count = 2 * ROWS
    place = lax.axis_index("tm")
    for seg, b in enumerate((place, lax.rem(place + ROWS, count))):
        at, start = seg * SEG, b * SPAN
        before, following = jnp.maximum(b - 1, 0), jnp.minimum(b + 1, count - 1)
        raw_s[at : at + PAD] = blocks[before, SPAN - PAD :]
        raw_s[at + PAD : at + PAD + SPAN] = blocks[b]
        raw_s[at + PAD + SPAN : at + SEG] = blocks[following, :PAD]
        rows = lambda begin, size: norm_s[pl.ds(pl.multiple_of(begin, PAD), size)]
        query_s[at : at + PAD] = rows(before * SPAN + SPAN - PAD, PAD)
        query_s[at + PAD : at + PAD + SPAN] = rows(start, SPAN)
        query_s[at + PAD + SPAN : at + SEG] = rows(following * SPAN, PAD)
    for copy in copies[:3]:
        copy.wait()
    attend_pairs(my_length(lengths), norm_s, query_s, group_a, context_ref)
    for copy in copies[3:]:
        copy.wait()


def attend_b_kernel(lengths, norm_s, query_s, weights, context_ref):
    attend_pairs(my_length(lengths), norm_s, query_s, weights, context_ref)


def attend_c_kernel(
    lengths, norm_s, query_s, raw_s, context_a, context_b, gains, weights, wout,
    first_ref, normed_ref, context_c,
):
    attend_pairs(my_length(lengths), norm_s, query_s, weights, context_c)
    third = D // 3
    out = sum(
        mm(c[...], wout[n * third : (n + 1) * third])
        for n, c in enumerate((context_a, context_b, context_c))
    )
    first = (raw_s[...].astype(jnp.float32) + out).astype(jnp.bfloat16)
    first_ref[...] = first
    normed_ref[...] = normalize(first, gains[1:2])


WIDE = 2 * SEG
ATTEND_COST = (3 * 10**9, 5 * 10**6, 10**6)


def run_attend_a(lengths, blocks, gains, qkv, wout):
    group = bf16(D, D)
    return call(
        attend_a_kernel,
        [bf16(WIDE, D // 3), bf16(FRAMES, D), bf16(WIDE, D), bf16(WIDE, D), group, group, group],
        [pltpu.VMEM((D, D), jnp.bfloat16), pltpu.SemaphoreType.DMA((10,))],
        ATTEND_COST, "attend_a", [blocks, gains, Far(qkv), Far(wout)], lengths, limit=48,
    )


def run_attend_b(lengths, norm, query, weights):
    (context,) = call(
        attend_b_kernel, [bf16(WIDE, D // 3)], [], ATTEND_COST, "attend_b", [norm, query, weights], lengths,
    )
    return context


def run_attend_c(lengths, *operands):
    return call(
        attend_c_kernel, [bf16(WIDE, D)] * 2, [pltpu.VMEM((WIDE, D // 3), jnp.bfloat16)],
        ATTEND_COST, "attend_c", list(operands), lengths,
    )


def depthwise(gated, base, taps, swish_s):
    for chunk in range(PAIRS):
        lo = chunk * 128
        mixed = jnp.zeros((SPAN, 128), jnp.float32)
        for o in range(TAPS):
            begin = base + PAD - TAPS // 2 + o
            tap = taps[o : o + 1, lo : lo + 128]
            mixed = mixed + tap * gated[chunk, begin : begin + SPAN]
        swish = mixed * jax.nn.sigmoid(mixed)
        swish_s[:, lo : lo + 128] = swish.astype(jnp.bfloat16)


def project_out(swish_s, kept, core, halves, out_ref):
    for h, half in zip((core, 1 - core), halves):
        lanes = pl.ds(pl.multiple_of(h * (D // 2), 128), D // 2)
        out = kept[:, lanes].astype(jnp.float32) + mm(swish_s[...], half[:, D:])
        out_ref[:, lanes] = out.astype(jnp.bfloat16)


def conv_a_kernel(
    lengths, normed, first, mine, other, taps, out_ref, home_ref, gated_s, swish_s, kept_s
):
    place, length, core = lax.axis_index("tm"), my_length(lengths), my_core()
    lives = []
    for b in (place, lax.rem(place + ROWS, 2 * ROWS)):
        frame = b * SPAN - PAD + lax.broadcasted_iota(jnp.int32, (SEG, 1), 0)
        lives.append((frame >= 0) & (frame < length))
    live = jnp.concatenate(lives, axis=0)
    for h, half in zip((core, 1 - core), (mine, other)):
        for n in range(PAIRS // 2):
            lo = n * 128
            both = jnp.concatenate(
                [half[:, lo : lo + 128], half[:, D // 2 + lo : D // 2 + lo + 128]], axis=1
            )
            wide = mm(normed[...], both)
            gated = jnp.where(live, wide[:, :128] * jax.nn.sigmoid(wide[:, 128:]), 0.0)
            gated = gated.astype(jnp.bfloat16).astype(jnp.float32)
            chunk = h * (PAIRS // 2) + n
            home_ref[chunk] = gated[:SEG]
            gated_s[chunk] = gated[SEG:]
    depthwise(gated_s, 0, taps, swish_s)
    kept_s[...] = first[SEG + PAD : SEG + PAD + SPAN]
    project_out(swish_s, kept_s, core, (mine, other), out_ref)


def conv_b_kernel(home, first, mine, other, taps, out_ref, swish_s, kept_s):
    depthwise(home, 0, taps, swish_s)
    kept_s[...] = first[PAD : PAD + SPAN]
    project_out(swish_s, kept_s, my_core(), (mine, other), out_ref)


def run_conv(lengths, normed, first, mine, other, taps):
    gated = jax.ShapeDtypeStruct((PAIRS, SEG, 128), jnp.float32)
    block = pltpu.VMEM((SPAN, D), jnp.bfloat16)
    away, home = call(
        conv_a_kernel, [bf16(SPAN, D), gated], [pltpu.VMEM(gated.shape, jnp.float32), block, block],
        (2 * 10**9, 6 * 10**6, 10**6), "conv_a", [normed, first, mine, other, taps], lengths,
    )
    (kept,) = call(
        conv_b_kernel, [bf16(SPAN, D)], [block, block],
        (10**9, 4 * 10**6, 10**6), "conv_b", [home, first, mine, other, taps],
    )
    return kept, away


def merge_kernel(live, block, gains, *refs):
    eighths, (out_ref, norm_s, context_s, weights_s) = refs[:8], refs[8:]
    col, core = lax.rem(lax.axis_index("tm"), ROWS), my_core()
    for n, eighth in enumerate(eighths):
        k = (0, 1, 3, 2)[n % 4]
        e = 2 * lax.rem(col + ROWS - k, ROWS) + (core if n < 4 else 1 - core)
        weights_s[e] = eighth[...]
    norm_s[...] = normalize(block[...], gains[2:3])
    count = block.shape[0]
    mine = lax.broadcasted_iota(jnp.int32, (count, count), 0) & 15
    theirs = lax.broadcasted_iota(jnp.int32, (count, count), 1) & 15
    allowed = (mine == theirs) & (live[...] > 0)
    for p in range(PAIRS):
        key, value_ones = with_ones(mm(norm_s[...], weights_s[p, :, 128:]).astype(jnp.bfloat16))
        query = mm(norm_s[...], weights_s[p, :, :128]).astype(jnp.bfloat16) * jnp.bfloat16(0.125)
        context_s[:, p * 128 : (p + 1) * 128] = pair_attention(query, key, value_ones, allowed)
    for n in range(2):
        lanes = slice(n * (D // 2), (n + 1) * (D // 2))
        out = block[:, lanes].astype(jnp.float32) + mm(context_s[...], weights_s[PAIRS + n])
        out_ref[:, lanes] = out.astype(jnp.bfloat16)


def run_merge(live, block, gains, eighths):
    count = block.shape[0]
    rows = pltpu.VMEM((count, D), jnp.bfloat16)
    (merged,) = call(
        merge_kernel, [bf16(count, D)], [rows, rows, pltpu.VMEM((8, D, D // 2), jnp.bfloat16)],
        (2 * 10**9, 8 * 10**6, 10**6), "merge", [live, block, gains, *eighths],
    )
    return merged


def after(value, *others):
    return lax.optimization_barrier((value,) + others)[0]


def assemble_kernel(*refs):
    pieces, outs = refs[:-2], refs[-2:]
    z = lax.axis_index("chan") // 2
    part = pieces[0].shape[0] // 2
    count = outs[0].shape[0] // (2 * part)

    def put(rows, d, at):
        at = lax.rem(at + 2 * count, count)
        lo = 0
        for out_ref in outs:
            width = out_ref.shape[1]
            begin = pl.multiple_of((d * count + at) * part, part)
            out_ref[pl.ds(begin, part)] = rows[:, lo : lo + width]
            lo += width

    for n, piece in enumerate(pieces[:-2]):
        step = (n + 1) // 2
        at = z - step if n % 2 else z + step
        for d in range(2):
            put(piece[d * part : (d + 1) * part], d, at)
    for d in range(2):
        put(pieces[d - 2][...], d, z + count // 2)


class WeightRing:
    def __init__(self, shard):
        dp, chan = lax.axis_index("dp"), lax.axis_index("chan")
        core, channels = chan % 2, lax.axis_size("chan")
        height, cols = shard.shape
        half = cols // 2
        mate = lax.ppermute(shard, "dp", [(0, 1), (1, 0)])
        pair = jnp.where(dp == 0, jnp.stack([shard, mate]), jnp.stack([mate, shard]))
        mine = jnp.where(core == 0, pair[..., :half], pair[..., half:])
        give = jnp.where(core == 0, pair[..., half:], pair[..., :half])
        self.swap = [(i, i ^ 1) for i in range(channels)]
        beside = lax.ppermute(give, "chan", self.swap)
        chip = jnp.where(core == 0, jnp.stack([mine, beside], 1), jnp.stack([beside, mine], 1))
        block = chip.reshape(4 * height, half)
        self.up = [(i, (i + 2) % channels) for i in range(channels)]
        self.down = [(i, (i - 2) % channels) for i in range(channels)]
        self.ends, self.pieces, self.left = (block, block), [block], channels // 4
        self.shape = (2 * channels * height, half)

    def step(self, *others):
        high, low = self.ends
        self.left -= 1
        if not self.left:
            part = high.shape[0] // 2
            high, low = high[:part], low[part:]
        high = lax.ppermute(after(high, *others) if others else high, "chan", self.up)
        low = lax.ppermute(after(low, *others) if others else low, "chan", self.down)
        self.ends = (high, low)
        self.pieces += [high, low]

    def assemble(self, split, *others):
        self.pieces[0] = after(self.pieces[0], *others)
        rows, cols = self.shape
        return call(
            assemble_kernel, [bf16(rows, split), bf16(rows, cols - split)], [],
            (0, 4 * 10**6, 0), "assemble", self.pieces,
        )


def shards(
    features, lengths, chan_valid, norm_gains, branch_qkv, branch_out, depth_taps,
    point_in, point_out, merge_qkv, merge_out,
):
    place, chan = lax.axis_index("tm"), lax.axis_index("chan")
    count = 2 * ROWS
    row = place // ROWS
    packed, spread = run_prepare(features, point_in, point_out, merge_qkv, merge_out)
    point = WeightRing(packed)
    other_row = [(i, (i + ROWS) % count) for i in range(count)]
    blocks = lax.all_to_all(spread, "tm", split_axis=0, concat_axis=0, tiled=True)
    point.step()
    point.step()
    point.step(blocks)
    context_a, norm, query, raw, group_b, group_c, wout = run_attend_a(
        lengths, blocks, norm_gains, branch_qkv, branch_out
    )
    point.step(context_a)
    context_b = run_attend_b(lengths, norm, query, group_b)
    mine, eighth = point.assemble(3 * D // 2, context_b)
    other = lax.ppermute(mine, "chan", point.swap)
    first, normed = run_attend_c(
        lengths, norm, query, raw, context_a, context_b, norm_gains, after(group_c, mine), wout
    )
    held = [eighth]
    for k in (1, 3, 2):
        pairs = [(i, i // ROWS * ROWS + (i + k) % ROWS) for i in range(count)]
        held.append(lax.ppermute(after(eighth, first), "tm", pairs))
    eighths = held + [lax.ppermute(one, "chan", point.swap) for one in held]
    kept, away = run_conv(lengths, normed, first, mine, other, depth_taps.astype(jnp.float32))
    back = lax.ppermute(away, "tm", other_row)
    second = jnp.concatenate([kept, back], axis=0)
    channels = lax.axis_size("chan")
    part = 2 * SPAN // channels
    joined = lax.all_to_all(
        second.reshape(channels, part, D), "chan", split_axis=0, concat_axis=0, tiled=True
    )
    owner = jnp.where(chan < channels // 2, row, 1 - row)
    live = jnp.repeat(chan_valid[owner], part)[None]
    merged = run_merge(live, joined.reshape(channels * part, D), norm_gains, eighths)
    returned = lax.all_to_all(
        merged.reshape(channels, part, D), "chan", split_axis=0, concat_axis=0, tiled=True
    ).reshape(2, SPAN, D)
    return jnp.where(row == 0, returned, returned[::-1])[:, None]


def solution(mesh):
    placed = (
        P("dp", "chan", "tm", None),
        P("dp"),
        P("dp", None),
        P(),
        P(),
        P(),
        P(),
        P(("dp", "chan"), None),
        P(("dp", "chan"), None),
        P(("dp", "chan"), None),
        P(("dp", "chan"), None),
    )
    return jax.shard_map(
        shards, mesh=mesh, in_specs=placed, out_specs=P("dp", "chan", "tm", None), check_vma=False
    )
```

time: 409 us -> 125 us (0.31)
  waiting for transfers between devices: 288 us -> 33.8 us
  starting transfers between devices: 11.6 us -> 56.1 us
  matrix products: 35.9 us -> 0 us
  Pallas kernels: 0 us -> 31.2 us
  local copies, waits for them, and re-layouts: 30 us -> 1.64 us
  blocking collectives: 19.6 us -> 0 us
  between operations: 13.7 us -> 0.27 us
  other arithmetic: 8.98 us -> 1.68 us
    all_gather x5 -> x0, waiting for transfers between devices: 255 us -> none  [the longest x1 92.8 us: shards(): gathered = lax.all_gather(project[..., model:], 'tm', axis=1, tiled=True)]
    ppermute x2 -> x19, starting transfers between devices: 5.46 us -> 39.6 us  [the longest x4 17.5 us: step(): lax.ppermute(after(low, *others) if others else low, 'chan', self.down)]
    pallas_call x0 -> x8, Pallas kernels: none -> 31.2 us  [call(): pl.pallas_call(kernel, in_specs=[pl.BlockSpec(memory_space=pltpu.SMEM)] *...]
    dot_general x8 -> x0, matrix products: 22.5 us -> none  [the longest x1 8.11 us: shards(): jnp.einsum('bhqk,bkhd->bqhd', attend, valued, preferred_element_type=jnp....]
    all_to_all x1 -> x0, blocking collectives: 19.6 us -> none  [shards(): lax.all_to_all(joined, 'chan', split_axis=1, concat_axis=2, tiled=True)]
    slice x11 -> x2, local copies, waits for them, and re-layouts: 18.9 us -> 0.02 us  [step(): high, low = (high[:part], low[part:])]
    ppermute x2 -> x19, waiting for transfers between devices: 0.01 us -> 16.5 us  [the longest x4 11.2 us: step(): lax.ppermute(after(low, *others) if others else low, 'chan', self.down)]
    all_to_all x1 -> x3, waiting for transfers between devices: 30.6 us -> 17.3 us  [the longest x1 14 us: shards(): lax.all_to_all(merged.reshape(channels, part, D), 'chan', split_axis=0, c...]
  transfers between devices with their start and end apart: 8 -> 22, of which waited for: 6 -> 9; matrix products, arithmetic and copies ran while one was open for 14% -> 1% of each run, Pallas kernels for 0% -> 17%
where the time goes in v2:
time: 125 us
  starting transfers between devices  56.1 us (45%)
  waiting for transfers between devices  33.8 us (27%)
  Pallas kernels  31.2 us (25%)
  other arithmetic  1.68 us (1%)
  local copies, waits for them, and re-layouts  1.64 us (1%)
    pallas_call x8, Pallas kernels, call(): pl.pallas_call(kernel, in_specs=[pl.BlockSpec(memory_space=pltpu.SMEM)] *...  31.2 us
    ppermute x4, starting transfers between devices, step(): lax.ppermute(after(low, *others) if others else low, 'chan', self.down)  17.5 us
    all_to_all x1, waiting for transfers between devices, shards(): lax.all_to_all(merged.reshape(channels, part, D), 'chan', split_axis=0, c...  14 us
    ppermute x4, waiting for transfers between devices, step(): lax.ppermute(after(low, *others) if others else low, 'chan', self.down)  11.2 us
    ppermute x4, starting transfers between devices, shards(): eighths = held + [lax.ppermute(one, 'chan', point.swap) for one in held]  9.59 us
    all_to_all x1, starting transfers between devices, shards(): lax.all_to_all(second.reshape(channels, part, D), 'chan', split_axis=0, c...  6.5 us
    all_to_all x1, starting transfers between devices, shards(): lax.all_to_all(spread, 'tm', split_axis=0, concat_axis=0, tiled=True)  6.49 us
    ppermute x3, starting transfers between devices, shards(): held.append(lax.ppermute(after(eighth, first), 'tm', pairs))  3.68 us
  transfers between devices with their start and end apart: 22, of which 9 were waited for; matrix products, arithmetic and copies ran while one was open for 1% of the time, Pallas kernels for 17%

profile of v2, /device:TPU:1, one launch (start us, length us, event | category | flops | bytes accessed | tf_op | source)
XLA Modules:
  0.0 124.6 jit_solution(17097615594563079613)
XLA Ops:
  0.0 3.0 %prepare.1 = (bf16[24,3072]{1,0:T(8,128)(2,1)}, bf16[8,128,768]{2,1,0:T(8,128)(2,1)}) custom-call(bf16[24,1536]{1,0:T(8,128)(2,1)} %pin.1, bf16[24,768]{1,0:T(8,128)(2,1)} %pout.1, bf16[24,2304]{1,0:T(8,128)(2,1)} %mqkv.1, bf16[24,768]{1,0:T(8,128)(2,1)} %mout.1, bf16[2,1,128,768]{3,2,1,0:T(8,128)(2,1)} %features.1), custom_call_target="tpu_custom_call" | custom-call | bytes 3000000 | tf_op jit(solution)/shard_map/prepare/pallas_call | solution.py:61
  3.0 2.2 %collective-permute-start = (bf16[24,3072]{1,0:T(8,128)(2,1)}, bf16[24,3072]{1,0:T(8,128)(2,1)S(1)}, u32[]{:S(2)}, u32[]{:S(2)}) collective-permute-start(bf16[24,3072]{1,0:T(8,128)(2,1)} %get-tuple-element.34), channel_id=1, source_target_pairs={{0,128},{128,0},{1,129},{129,1},{2,130},{130,2},{3,131},{131,3},{4... | collective-permute-start | bytes 442376 | tf_op jit(solution)/shard_map/ppermute | solution.py:354
  5.2 6.5 %all-to-all-start = ((bf16[8,128,768]{2,1,0:T(8,128)(2,1)}), bf16[8,128,768]{2,1,0:T(8,128)(2,1)}, u32[]{:S(2)}, u32[]{:S(2)}) async-start(bf16[8,128,768]{2,1,0:T(8,128)(2,1)} %get-tuple-element.27), calls=%async_computation | async-start | bytes 3145728 | tf_op jit(solution)/shard_map/all_to_all | solution.py:397
  14.2 5.7 %collective-permute-start.3 = (bf16[96,1536]{1,0:T(8,128)(2,1)S(1)}, bf16[96,1536]{1,0:T(8,128)(2,1)S(1)}, u32[]{:S(2)}, u32[]{:S(2)}) collective-permute-start(bf16[96,1536]{1,0:T(8,128)(2,1)S(1)} %bitcast.14), channel_id=1, source_target_pairs={{0,112},{8,120},{16,0},{24,8},{32,16},{40,24},{48,32},{56,40},{64,... | collective-permute-start | bytes 884744 | tf_op jit(solution)/shard_map/ppermute | solution.py:374
  19.9 6.0 %collective-permute-done.3.refs_2_ = bf16[96,1536]{1,0:T(8,128)(2,1)S(1)} collective-permute-done((bf16[96,1536]{1,0:T(8,128)(2,1)S(1)}, bf16[96,1536]{1,0:T(8,128)(2,1)S(1)}, u32[]{:S(2)}, u32[]{:S(2)}) %collective-permute-start.3) | collective-permute-done | bytes 294944 | tf_op jit(solution)/shard_map/ppermute | solution.py:374
  25.9 3.5 %collective-permute-start.5 = (bf16[96,1536]{1,0:T(8,128)(2,1)S(1)}, bf16[96,1536]{1,0:T(8,128)(2,1)S(1)}, u32[]{:S(2)}, u32[]{:S(2)}) collective-permute-start(bf16[96,1536]{1,0:T(8,128)(2,1)S(1)} %collective-permute-done.3.refs_2_), channel_id=1, source_target_pairs={{0,112},{8,120},{16,0},{24,8},{32,16},{40,24},{48,32},{56,40},{64,... | collective-permute-start | bytes 884744 | tf_op jit(solution)/shard_map/ppermute | solution.py:374
  29.4 5.2 %collective-permute-done.5.refs_4_ = bf16[96,1536]{1,0:T(8,128)(2,1)S(1)} collective-permute-done((bf16[96,1536]{1,0:T(8,128)(2,1)S(1)}, bf16[96,1536]{1,0:T(8,128)(2,1)S(1)}, u32[]{:S(2)}, u32[]{:S(2)}) %collective-permute-start.5) | collective-permute-done | bytes 294944 | tf_op jit(solution)/shard_map/ppermute | solution.py:374
  34.7 5.6 %collective-permute-start.7 = (bf16[96,1536]{1,0:T(8,128)(2,1)S(1)}, bf16[96,1536]{1,0:T(8,128)(2,1)S(1)}, u32[]{:S(2)}, u32[]{:S(2)}) collective-permute-start(bf16[96,1536]{1,0:T(8,128)(2,1)S(1)} %collective-permute-done.5.refs_4_), channel_id=1, source_target_pairs={{0,112},{8,120},{16,0},{24,8},{32,16},{40,24},{48,32},{56,40},{64,... | collective-permute-start | bytes 884744 | tf_op jit(solution)/shard_map/ppermute | solution.py:374
  40.3 7.8 %attend_a.1 = (bf16[320,256]{1,0:T(8,128)(2,1)S(1)}, bf16[1024,768]{1,0:T(8,128)(2,1)}, bf16[320,768]{1,0:T(8,128)(2,1)S(1)}, bf16[320,768]{1,0:T(8,128)(2,1)S(1...) custom-call(s32[2]{0:T(128)S(1)} %copy-done.3, ...), custom_call_target="tpu_custom_call" | custom-call | flops 3000000000 | bytes 5000000 | tf_op jit(solution)/shard_map/attend_a/pallas_call | solution.py:61
  48.2 2.7 %collective-permute-start.9 = (bf16[48,1536]{1,0:T(8,128)(2,1)S(1)}, bf16[48,1536]{1,0:T(8,128)(2,1)S(1)}, u32[]{:S(2)}, u32[]{:S(2)}) collective-permute-start(bf16[48,1536]{1,0:T(8,128)(2,1)S(1)} %slice.21), channel_id=1, source_target_pairs={{0,112},{8,120},{16,0},{24,8},{32,16},{40,24},{48,32},{56,40},{64,... | collective-permute-start | bytes 442376 | tf_op jit(solution)/shard_map/ppermute | solution.py:374
  51.2 1.4 %copy-done.4 = bf16[1024,768]{1,0:T(8,128)(2,1)S(1)} copy-done((bf16[1024,768]{1,0:T(8,128)(2,1)S(1)}, bf16[1024,768]{1,0:T(8,128)(2,1)}, u32[]{:S(2)}) %copy-start.4) | copy-done | bytes 1572888
  52.6 4.3 %attend_b.1.context_b = bf16[320,256]{1,0:T(8,128)(2,1)S(1)} custom-call(s32[2]{0:T(128)S(1)} %copy-done.3, bf16[1024,768]{1,0:T(8,128)(2,1)S(1)} %copy-done.4, bf16[320,768]{1,0:T(8,128)(2,1)S(1)} %get-tuple-element.29.query_s, bf16[768,768]{1,0:T(8,128)(2,1)S(1)} %get-tuple-element.32.weights), custom_call_target="tpu_custom_call" | custom-call | flops 3000000000 | bytes 5000000 | tf_op jit(solution)/shard_map/attend_b/pallas_call | solution.py:61
  57.2 2.3 %collective-permute-start.10 = (bf16[768,1152]{1,0:T(8,128)(2,1)S(1)}, bf16[768,1152]{1,0:T(8,128)(2,1)S(1)}, u32[]{:S(2)}, u32[]{:S(2)}) collective-permute-start(bf16[768,1152]{1,0:T(8,128)(2,1)S(1)} %get-tuple-element.40.mine), channel_id=1, source_target_pairs={{0,8},{8,0},{16,24},{24,16},{32,40},{40,32},{48,56},{56,48},{64,72... | collective-permute-start | bytes 5308424 | tf_op jit(solution)/shard_map/ppermute | solution.py:407
  59.5 4.7 %attend_c.1 = (bf16[320,768]{1,0:T(8,128)(2,1)S(1)}, bf16[320,768]{1,0:T(8,128)(2,1)S(1)}) custom-call(s32[2]{0:T(128)S(1)} %copy-done.3, bf16[1024,768]{1,0:T(8,128)(2,1)S(1)} %copy-done.5, bf16[320,768]{1,0:T(8,128)(2,1)S(1)} %get-tuple-element.29.query_s, bf16[320,768]{1,0:T(8,128)(2,1)S(1)} %get-tuple-element.30.raw_s, ...), custom_call_target="tpu_custom_call" | custom-call | flops 3000000000 | bytes 5000000 | tf_op jit(solution)/shard_map/attend_c/pallas_call | solution.py:61
  65.0 2.0 %collective-permute-start.13 = (bf16[768,384]{1,0:T(8,128)(2,1)S(1)}, bf16[768,384]{1,0:T(8,128)(2,1)S(1)}, u32[]{:S(2)}, u32[]{:S(2)}) collective-permute-start(bf16[768,384]{1,0:T(8,128)(2,1)S(1)} %get-tuple-element.48.refs_0_), channel_id=1, source_target_pairs={{0,3},{1,0},{2,1},{3,2},{4,7},{5,4},{6,5},{7,6},{8,11},{9,8},{10,9... | collective-permute-start | bytes 1769480 | tf_op jit(solution)/shard_map/ppermute | solution.py:414
  67.9 2.8 %conv_a.1 = (bf16[128,768]{1,0:T(8,128)(2,1)S(1)}, f32[6,160,128]{2,1,0:T(8,128)S(1)}) custom-call(s32[2]{0:T(128)S(1)} %copy-done.3, bf16[320,768]{1,0:T(8,128)(2,1)S(1)} %get-tuple-element.43.normed, bf16[320,768]{1,0:T(8,128)(2,1)S(1)} %get-tuple-element.44.first, bf16[768,1152]{1,0:T(8,128)(2,1)S(1)} %get-tuple-element.40.mine, ...), custom_call_target="tpu_custom_call" | custom-call | flops 2000000000 | bytes 6000000 | tf_op jit(solution)/shard_map/conv_a/pallas_call | solution.py:61
  70.8 2.8 %collective-permute-start.11 = (bf16[128,768]{1,0:T(8,128)(2,1)S(1)}, bf16[128,768]{1,0:T(8,128)(2,1)S(1)}, u32[]{:S(2)}, u32[]{:S(2)}) collective-permute-start(bf16[128,768]{1,0:T(8,128)(2,1)S(1)} %get-tuple-element.46), channel_id=1, source_target_pairs={{0,4},{1,5},{2,6},{3,7},{4,0},{5,1},{6,2},{7,3},{8,12},{9,13},{10,... | collective-permute-start | bytes 589832 | tf_op jit(solution)/shard_map/ppermute | solution.py:417
  74.7 2.7 %collective-permute-done.11 = bf16[128,768]{1,0:T(8,128)(2,1)S(1)} collective-permute-done((bf16[128,768]{1,0:T(8,128)(2,1)S(1)}, bf16[128,768]{1,0:T(8,128)(2,1)S(1)}, u32[]{:S(2)}, u32[]{:S(2)}) %collective-permute-start.11) | collective-permute-done | bytes 196640 | tf_op jit(solution)/shard_map/ppermute | solution.py:417
  78.2 6.5 %all-to-all-start.1 = ((bf16[16,16,768]{2,1,0:T(8,128)(2,1)}), bf16[16,16,768]{2,1,0:T(8,128)(2,1)S(1)}, u32[]{:S(2)}, u32[]{:S(2)}) async-start(bf16[16,16,768]{2,1,0:T(8,128)(2,1)} %bitcast.6), calls=%async_computation.1 | async-start | bytes 786432 | tf_op jit(solution)/shard_map/all_to_all | solution.py:421
  85.2 8.0 %collective-permute-start.17 = (bf16[768,384]{1,0:T(8,128)(2,1)S(1)}, bf16[768,384]{1,0:T(8,128)(2,1)}, u32[]{:S(2)}, u32[]{:S(2)}) collective-permute-start(bf16[768,384]{1,0:T(8,128)(2,1)S(1)} %collective-permute-done.13.refs_2_), channel_id=1, source_target_pairs={{0,8},{8,0},{16,24},{24,16},{32,40},{40,32},{48,56},{56,48},{64,72... | collective-permute-start | bytes 1769480 | tf_op jit(solution)/shard_map/ppermute | solution.py:415
  96.0 3.2 %all-to-all-done.1 = bf16[16,16,768]{2,1,0:T(8,128)(2,1)S(1)} async-done(((bf16[16,16,768]{2,1,0:T(8,128)(2,1)}), bf16[16,16,768]{2,1,0:T(8,128)(2,1)S(1)}, u32[]{:S(2)}, u32[]{:S(2)}) %all-to-all-start.1) | async-done | bytes 393248 | tf_op jit(solution)/shard_map/all_to_all | solution.py:421
  99.2 7.2 %merge.1 = bf16[256,768]{1,0:T(8,128)(2,1)} custom-call(s32[1,256]{1,0:T(1,128)S(1)} %broadcast_in_dim_reshape.3.live, bf16[256,768]{1,0:T(8,128)(2,1)S(1)} %bitcast.17, f32[3,768]{1,0:T(4,128)S(1)} %copy-done.2, bf16[768,384]{1,0:T(8,128)(2,1)S(1)} %get-tuple-element.48.refs_0_, bf16[768,384]{1,0:T(8,128)(2,1)S(1)} %collective-permute-done.12.refs_1_, ...), custom_call_target="tpu_custom_call" | custom-call | flops 2000000000 | bytes 8000000 | tf_op jit(solution)/shard_map/merge/pallas_call | solution.py:61
  106.4 3.5 %all-to-all-start.2 = ((bf16[16,16,768]{2,1,0:T(8,128)(2,1)}), bf16[16,16,768]{2,1,0:T(8,128)(2,1)S(1)}, u32[]{:S(2)}, u32[]{:S(2)}) async-start(bf16[16,16,768]{2,1,0:T(8,128)(2,1)} %bitcast.8), calls=%async_computation.2 | async-start | bytes 786432 | tf_op jit(solution)/shard_map/all_to_all | solution.py:427
  109.8 14.0 %all-to-all-done.2 = bf16[16,16,768]{2,1,0:T(8,128)(2,1)S(1)} async-done(((bf16[16,16,768]{2,1,0:T(8,128)(2,1)}), bf16[16,16,768]{2,1,0:T(8,128)(2,1)S(1)}, u32[]{:S(2)}, u32[]{:S(2)}) %all-to-all-start.2) | async-done | bytes 393248 | tf_op jit(solution)/shard_map/all_to_all | solution.py:427
  (56 shorter events, 10.8 us)
Async XLA Ops:
  0.0 94.3 %copy-start = (s32[2,16]{1,0:T(2,128)S(1)}, s32[2,16]{1,0:T(2,128)}, u32[]{:S(2)}) copy-start(s32[2,16]{1,0:T(2,128)} %param.13) | copy-start | bytes 388
  3.0 8.8 %collective-permute-start = (bf16[24,3072]{1,0:T(8,128)(2,1)}, bf16[24,3072]{1,0:T(8,128)(2,1)S(1)}, u32[]{:S(2)}, u32[]{:S(2)}) collective-permute-start(bf16[24,3072]{1,0:T(8,128)(2,1)} %get-tuple-element.34), channel_id=1, source_target_pairs={{0,128},{128,0},{1,129},{129,1},{2,130},{130,2},{3,131},{131,3},{4... | collective-permute-start | bytes 442376 | tf_op jit(solution)/shard_map/ppermute | solution.py:354
  5.2 29.5 %all-to-all-start = ((bf16[8,128,768]{2,1,0:T(8,128)(2,1)}), bf16[8,128,768]{2,1,0:T(8,128)(2,1)}, u32[]{:S(2)}, u32[]{:S(2)}) async-start(bf16[8,128,768]{2,1,0:T(8,128)(2,1)} %get-tuple-element.27), calls=%async_computation | async-start | bytes 3145728 | tf_op jit(solution)/shard_map/all_to_all | solution.py:397
  11.7 28.6 %copy-start.2 = (f32[3,768]{1,0:T(4,128)S(1)}, f32[3,768]{1,0:T(4,128)}, u32[]{:S(2)}) copy-start(f32[3,768]{1,0:T(4,128)} %gains.5) | copy-start | bytes 27652
  11.8 2.3 %collective-permute-start.1 = (bf16[2,24,1536]{2,1,0:T(8,128)(2,1)S(1)}, bf16[2,24,1536]{2,1,0:T(8,128)(2,1)S(1)}, u32[]{:S(2)}, u32[]{:S(2)}) collective-permute-start(bf16[2,24,1536]{2,1,0:T(8,128)(2,1)S(1)} %get-tuple-element.50), channel_id=1, source_target_pairs={{0,8},{8,0},{16,24},{24,16},{32,40},{40,32},{48,56},{56,48},{64,72... | collective-permute-start | bytes 442376 | tf_op jit(solution)/shard_map/ppermute | solution.py:359
  14.2 11.7 %collective-permute-start.3 = (bf16[96,1536]{1,0:T(8,128)(2,1)S(1)}, bf16[96,1536]{1,0:T(8,128)(2,1)S(1)}, u32[]{:S(2)}, u32[]{:S(2)}) collective-permute-start(bf16[96,1536]{1,0:T(8,128)(2,1)S(1)} %bitcast.14), channel_id=1, source_target_pairs={{0,112},{8,120},{16,0},{24,8},{32,16},{40,24},{48,32},{56,40},{64,... | collective-permute-start | bytes 884744 | tf_op jit(solution)/shard_map/ppermute | solution.py:374
  19.9 9.5 %collective-permute-start.2 = (bf16[96,1536]{1,0:T(8,128)(2,1)S(1)}, bf16[96,1536]{1,0:T(8,128)(2,1)S(1)}, u32[]{:S(2)}, u32[]{:S(2)}) collective-permute-start(bf16[96,1536]{1,0:T(8,128)(2,1)S(1)} %bitcast.15), channel_id=1, source_target_pairs={{0,16},{8,24},{16,32},{24,40},{32,48},{40,56},{48,64},{56,72},{64,... | collective-permute-start | bytes 884744 | tf_op jit(solution)/shard_map/ppermute | solution.py:373
  25.9 8.7 %collective-permute-start.5 = (bf16[96,1536]{1,0:T(8,128)(2,1)S(1)}, bf16[96,1536]{1,0:T(8,128)(2,1)S(1)}, u32[]{:S(2)}, u32[]{:S(2)}) collective-permute-start(bf16[96,1536]{1,0:T(8,128)(2,1)S(1)} %collective-permute-done.3.refs_2_), channel_id=1, source_target_pairs={{0,112},{8,120},{16,0},{24,8},{32,16},{40,24},{48,32},{56,40},{64,... | collective-permute-start | bytes 884744 | tf_op jit(solution)/shard_map/ppermute | solution.py:374
  29.4 10.9 %collective-permute-start.4 = (bf16[96,1536]{1,0:T(8,128)(2,1)S(1)}, bf16[96,1536]{1,0:T(8,128)(2,1)S(1)}, u32[]{:S(2)}, u32[]{:S(2)}) collective-permute-start(bf16[96,1536]{1,0:T(8,128)(2,1)S(1)} %collective-permute-done.2.refs_1_), channel_id=1, source_target_pairs={{0,16},{8,24},{16,32},{24,40},{32,48},{40,56},{48,64},{56,72},{64,... | collective-permute-start | bytes 884744 | tf_op jit(solution)/shard_map/ppermute | solution.py:373
  34.7 13.4 %collective-permute-start.7 = (bf16[96,1536]{1,0:T(8,128)(2,1)S(1)}, bf16[96,1536]{1,0:T(8,128)(2,1)S(1)}, u32[]{:S(2)}, u32[]{:S(2)}) collective-permute-start(bf16[96,1536]{1,0:T(8,128)(2,1)S(1)} %collective-permute-done.5.refs_4_), channel_id=1, source_target_pairs={{0,112},{8,120},{16,0},{24,8},{32,16},{40,24},{48,32},{56,40},{64,... | collective-permute-start | bytes 884744 | tf_op jit(solution)/shard_map/ppermute | solution.py:374
  40.3 10.6 %collective-permute-start.6 = (bf16[96,1536]{1,0:T(8,128)(2,1)S(1)}, bf16[96,1536]{1,0:T(8,128)(2,1)S(1)}, u32[]{:S(2)}, u32[]{:S(2)}) collective-permute-start(bf16[96,1536]{1,0:T(8,128)(2,1)S(1)} %collective-permute-done.4.refs_3_), channel_id=1, source_target_pairs={{0,16},{8,24},{16,32},{24,40},{32,48},{40,56},{48,64},{56,72},{64,... | collective-permute-start | bytes 884744 | tf_op jit(solution)/shard_map/ppermute | solution.py:373
  48.2 8.8 %collective-permute-start.9 = (bf16[48,1536]{1,0:T(8,128)(2,1)S(1)}, bf16[48,1536]{1,0:T(8,128)(2,1)S(1)}, u32[]{:S(2)}, u32[]{:S(2)}) collective-permute-start(bf16[48,1536]{1,0:T(8,128)(2,1)S(1)} %slice.21), channel_id=1, source_target_pairs={{0,112},{8,120},{16,0},{24,8},{32,16},{40,24},{48,32},{56,40},{64,... | collective-permute-start | bytes 442376 | tf_op jit(solution)/shard_map/ppermute | solution.py:374
  50.9 6.1 %collective-permute-start.8 = (bf16[48,1536]{1,0:T(8,128)(2,1)S(1)}, bf16[48,1536]{1,0:T(8,128)(2,1)S(1)}, u32[]{:S(2)}, u32[]{:S(2)}) collective-permute-start(bf16[48,1536]{1,0:T(8,128)(2,1)S(1)} %slice.20), channel_id=1, source_target_pairs={{0,16},{8,24},{16,32},{24,40},{32,48},{40,56},{48,64},{56,72},{64,... | collective-permute-start | bytes 442376 | tf_op jit(solution)/shard_map/ppermute | solution.py:373
  57.2 10.7 %collective-permute-start.10 = (bf16[768,1152]{1,0:T(8,128)(2,1)S(1)}, bf16[768,1152]{1,0:T(8,128)(2,1)S(1)}, u32[]{:S(2)}, u32[]{:S(2)}) collective-permute-start(bf16[768,1152]{1,0:T(8,128)(2,1)S(1)} %get-tuple-element.40.mine), channel_id=1, source_target_pairs={{0,8},{8,0},{16,24},{24,16},{32,40},{40,32},{48,56},{56,48},{64,72... | collective-permute-start | bytes 5308424 | tf_op jit(solution)/shard_map/ppermute | solution.py:407
  64.2 20.6 %collective-permute-start.12 = (bf16[768,384]{1,0:T(8,128)(2,1)S(1)}, bf16[768,384]{1,0:T(8,128)(2,1)S(1)}, u32[]{:S(2)}, u32[]{:S(2)}) collective-permute-start(bf16[768,384]{1,0:T(8,128)(2,1)S(1)} %get-tuple-element.48.refs_0_), channel_id=1, source_target_pairs={{0,1},{1,2},{2,3},{3,0},{4,5},{5,6},{6,7},{7,4},{8,9},{9,10},{10,1... | collective-permute-start | bytes 1769480 | tf_op jit(solution)/shard_map/ppermute | solution.py:414
  65.0 20.2 %collective-permute-start.13 = (bf16[768,384]{1,0:T(8,128)(2,1)S(1)}, bf16[768,384]{1,0:T(8,128)(2,1)S(1)}, u32[]{:S(2)}, u32[]{:S(2)}) collective-permute-start(bf16[768,384]{1,0:T(8,128)(2,1)S(1)} %get-tuple-element.48.refs_0_), channel_id=1, source_target_pairs={{0,3},{1,0},{2,1},{3,2},{4,7},{5,4},{6,5},{7,6},{8,11},{9,8},{10,9... | collective-permute-start | bytes 1769480 | tf_op jit(solution)/shard_map/ppermute | solution.py:414
  67.0 26.2 %collective-permute-start.14 = (bf16[768,384]{1,0:T(8,128)(2,1)S(1)}, bf16[768,384]{1,0:T(8,128)(2,1)S(1)}, u32[]{:S(2)}, u32[]{:S(2)}) collective-permute-start(bf16[768,384]{1,0:T(8,128)(2,1)S(1)} %get-tuple-element.48.refs_0_), channel_id=1, source_target_pairs={{0,2},{1,3},{2,0},{3,1},{4,6},{5,7},{6,4},{7,5},{8,10},{9,11},{10,... | collective-permute-start | bytes 1769480 | tf_op jit(solution)/shard_map/ppermute | solution.py:414
  70.8 6.6 %collective-permute-start.11 = (bf16[128,768]{1,0:T(8,128)(2,1)S(1)}, bf16[128,768]{1,0:T(8,128)(2,1)S(1)}, u32[]{:S(2)}, u32[]{:S(2)}) collective-permute-start(bf16[128,768]{1,0:T(8,128)(2,1)S(1)} %get-tuple-element.46), channel_id=1, source_target_pairs={{0,4},{1,5},{2,6},{3,7},{4,0},{5,1},{6,2},{7,3},{8,12},{9,13},{10,... | collective-permute-start | bytes 589832 | tf_op jit(solution)/shard_map/ppermute | solution.py:417
  78.2 21.1 %all-to-all-start.1 = ((bf16[16,16,768]{2,1,0:T(8,128)(2,1)}), bf16[16,16,768]{2,1,0:T(8,128)(2,1)S(1)}, u32[]{:S(2)}, u32[]{:S(2)}) async-start(bf16[16,16,768]{2,1,0:T(8,128)(2,1)} %bitcast.6), calls=%async_computation.1 | async-start | bytes 786432 | tf_op jit(solution)/shard_map/all_to_all | solution.py:421
  84.7 9.8 %collective-permute-start.15 = (bf16[768,384]{1,0:T(8,128)(2,1)S(1)}, bf16[768,384]{1,0:T(8,128)(2,1)}, u32[]{:S(2)}, u32[]{:S(2)}) collective-permute-start(bf16[768,384]{1,0:T(8,128)(2,1)S(1)} %get-tuple-element.48.refs_0_), channel_id=1, source_target_pairs={{0,8},{8,0},{16,24},{24,16},{32,40},{40,32},{48,56},{56,48},{64,72... | collective-permute-start | bytes 1769480 | tf_op jit(solution)/shard_map/ppermute | solution.py:415
  84.9 9.6 %collective-permute-start.16 = (bf16[768,384]{1,0:T(8,128)(2,1)S(1)}, bf16[768,384]{1,0:T(8,128)(2,1)}, u32[]{:S(2)}, u32[]{:S(2)}) collective-permute-start(bf16[768,384]{1,0:T(8,128)(2,1)S(1)} %collective-permute-done.12.refs_1_), channel_id=1, source_target_pairs={{0,8},{8,0},{16,24},{24,16},{32,40},{40,32},{48,56},{56,48},{64,72... | collective-permute-start | bytes 1769480 | tf_op jit(solution)/shard_map/ppermute | solution.py:415
  85.2 9.8 %collective-permute-start.17 = (bf16[768,384]{1,0:T(8,128)(2,1)S(1)}, bf16[768,384]{1,0:T(8,128)(2,1)}, u32[]{:S(2)}, u32[]{:S(2)}) collective-permute-start(bf16[768,384]{1,0:T(8,128)(2,1)S(1)} %collective-permute-done.13.refs_2_), channel_id=1, source_target_pairs={{0,8},{8,0},{16,24},{24,16},{32,40},{40,32},{48,56},{56,48},{64,72... | collective-permute-start | bytes 1769480 | tf_op jit(solution)/shard_map/ppermute | solution.py:415
  93.2 2.8 %collective-permute-start.18 = (bf16[768,384]{1,0:T(8,128)(2,1)S(1)}, bf16[768,384]{1,0:T(8,128)(2,1)}, u32[]{:S(2)}, u32[]{:S(2)}) collective-permute-start(bf16[768,384]{1,0:T(8,128)(2,1)S(1)} %collective-permute-done.14.refs_3_), channel_id=1, source_target_pairs={{0,8},{8,0},{16,24},{24,16},{32,40},{40,32},{48,56},{56,48},{64,72... | collective-permute-start | bytes 1769480 | tf_op jit(solution)/shard_map/ppermute | solution.py:415
  106.4 17.4 %all-to-all-start.2 = ((bf16[16,16,768]{2,1,0:T(8,128)(2,1)}), bf16[16,16,768]{2,1,0:T(8,128)(2,1)S(1)}, u32[]{:S(2)}, u32[]{:S(2)}) async-start(bf16[16,16,768]{2,1,0:T(8,128)(2,1)} %bitcast.8), calls=%async_computation.2 | async-start | bytes 786432 | tf_op jit(solution)/shard_map/all_to_all | solution.py:427
  (6 other events, 70.4 us)

commit v3 on v2

--- a/solution.py
+++ b/solution.py
@@ -43,11 +43,6 @@
         out = mm(weights, value_ones)
         outs.append(out[:, :128] / out[:, 128:])
     return jnp.where(low, outs[0], outs[1]).astype(jnp.bfloat16)
-
-
-def with_ones(both):
-    value = both[:, 128:]
-    return both[:, :128], jnp.concatenate([value, jnp.ones_like(value)], axis=1)
 
 
 def bf16(*shape):
@@ -132,10 +127,11 @@
 def attend_pairs(length, norm_s, query_s, weights, context_ref):
     allowed = lax.broadcasted_iota(jnp.int32, (1, FRAMES), 1) < length
     query_two = mm(query_s[...], weights[:, :256]).astype(jnp.bfloat16) * jnp.bfloat16(0.125)
+    both = mm(norm_s[...], weights[:, 256:]).astype(jnp.bfloat16)
     for n in range(2):
         lanes = slice(n * 128, (n + 1) * 128)
-        both = jnp.concatenate([weights[:, 256:512][:, lanes], weights[:, 512:][:, lanes]], axis=1)
-        key, value_ones = with_ones(mm(norm_s[...], both).astype(jnp.bfloat16))
+        key, value = both[:, :256][:, lanes], both[:, 256:][:, lanes]
+        value_ones = jnp.concatenate([value, jnp.ones_like(value)], axis=1)
         context_ref[:, lanes] = pair_attention(query_two[:, lanes], key, value_ones, allowed)
 
 
@@ -202,7 +198,7 @@
         attend_a_kernel,
         [bf16(WIDE, D // 3), bf16(FRAMES, D), bf16(WIDE, D), bf16(WIDE, D), group, group, group],
         [pltpu.VMEM((D, D), jnp.bfloat16), pltpu.SemaphoreType.DMA((10,))],
-        ATTEND_COST, "attend_a", [blocks, gains, Far(qkv), Far(wout)], lengths, limit=48,
+        ATTEND_COST, "attend_a", [blocks, gains, Far(qkv), Far(wout)], lengths, limit=44,
     )
 
 
@@ -297,9 +293,10 @@
     mine = lax.broadcasted_iota(jnp.int32, (count, count), 0) & 15
     theirs = lax.broadcasted_iota(jnp.int32, (count, count), 1) & 15
     allowed = (mine == theirs) & (live[...] > 0)
-    for p in range(PAIRS):
-        key, value_ones = with_ones(mm(norm_s[...], weights_s[p, :, 128:]).astype(jnp.bfloat16))
-        query = mm(norm_s[...], weights_s[p, :, :128]).astype(jnp.bfloat16) * jnp.bfloat16(0.125)
+    projected = [mm(norm_s[...], weights_s[p]).astype(jnp.bfloat16) for p in range(PAIRS)]
+    for p, both in enumerate(projected):
+        query, key, value = both[:, :128] * jnp.bfloat16(0.125), both[:, 128:256], both[:, 256:]
+        value_ones = jnp.concatenate([value, jnp.ones_like(value)], axis=1)
         context_s[:, p * 128 : (p + 1) * 128] = pair_attention(query, key, value_ones, allowed)
     for n in range(2):
         lanes = slice(n * (D // 2), (n + 1) * (D // 2))
@@ -408,13 +405,16 @@
     first, normed = run_attend_c(
         lengths, norm, query, raw, context_a, context_b, norm_gains, after(group_c, mine), wout
     )
-    held = [eighth]
-    for k in (1, 3, 2):
+    def beside(values, k):
         pairs = [(i, i // ROWS * ROWS + (i + k) % ROWS) for i in range(count)]
-        held.append(lax.ppermute(after(eighth, first), "tm", pairs))
-    eighths = held + [lax.ppermute(one, "chan", point.swap) for one in held]
+        return lax.ppermute(values, "tm", pairs)
+
+    far = beside(eighth, 2)
     kept, away = run_conv(lengths, normed, first, mine, other, depth_taps.astype(jnp.float32))
     back = lax.ppermute(away, "tm", other_row)
+    late = after(eighth, away)
+    held = [eighth, beside(late, 1), beside(late, 3), far]
+    eighths = held + [lax.ppermute(one, "chan", point.swap) for one in held]
     second = jnp.concatenate([kept, back], axis=0)
     channels = lax.axis_size("chan")
     part = 2 * SPAN // channels

time: 125 us -> 122 us (0.976)
  waiting for transfers between devices: 33.8 us -> 44.4 us
  starting transfers between devices: 56.1 us -> 47.7 us
  Pallas kernels: 31.2 us -> 26.1 us
    ppermute x4, waiting for transfers between devices: 0.01 us -> 13.3 us  [step(): lax.ppermute(after(high, *others) if others else high, 'chan', self.up)]
    ppermute x4, waiting for transfers between devices: 11.2 us -> 0.01 us  [step(): lax.ppermute(after(low, *others) if others else low, 'chan', self.down)]
    ppermute x4, starting transfers between devices: 9.59 us -> 1.02 us  [shards(): eighths = held + [lax.ppermute(one, 'chan', point.swap) for one in held]]
    all_to_all x1, waiting for transfers between devices: 3.18 us -> 11.6 us  [shards(): lax.all_to_all(second.reshape(channels, part, D), 'chan', split_axis=0, c...]
    pallas_call x8, Pallas kernels: 31.2 us -> 26.1 us  [call(): pl.pallas_call(kernel, in_specs=[pl.BlockSpec(memory_space=pltpu.SMEM)] *...]
    ppermute x4, starting transfers between devices: 17.5 us -> 13.6 us  [step(): lax.ppermute(after(low, *others) if others else low, 'chan', self.down)]
    ppermute x4, starting transfers between devices: 0.27 us -> 2.24 us  [step(): lax.ppermute(after(high, *others) if others else high, 'chan', self.up)]
    ppermute x3, waiting for transfers between devices: 0.01 us -> 1.67 us  [beside(): return lax.ppermute(values, 'tm', pairs)]
  transfers between devices with their start and end apart: 22 -> 22, of which waited for: 9 -> 9; matrix products, arithmetic and copies ran while one was open for 1% -> 1% of each run, Pallas kernels for 17% -> 14%
where the time goes in v3:
time: 122 us
  starting transfers between devices  47.7 us (39%)
  waiting for transfers between devices  44.4 us (36%)
  Pallas kernels  26.1 us (21%)
  other arithmetic  1.68 us (1%)
  local copies, waits for them, and re-layouts  1.5 us (1%)
    pallas_call x8, Pallas kernels, call(): pl.pallas_call(kernel, in_specs=[pl.BlockSpec(memory_space=pltpu.SMEM)] *...  26.1 us
    all_to_all x1, waiting for transfers between devices, shards(): lax.all_to_all(merged.reshape(channels, part, D), 'chan', split_axis=0, c...  14 us
    ppermute x4, starting transfers between devices, step(): lax.ppermute(after(low, *others) if others else low, 'chan', self.down)  13.6 us
    ppermute x4, waiting for transfers between devices, step(): lax.ppermute(after(high, *others) if others else high, 'chan', self.up)  13.3 us
    all_to_all x1, waiting for transfers between devices, shards(): lax.all_to_all(second.reshape(channels, part, D), 'chan', split_axis=0, c...  11.6 us
    all_to_all x1, starting transfers between devices, shards(): lax.all_to_all(second.reshape(channels, part, D), 'chan', split_axis=0, c...  7.47 us
    all_to_all x1, starting transfers between devices, shards(): lax.all_to_all(spread, 'tm', split_axis=0, concat_axis=0, tiled=True)  6.49 us
    ppermute x3, starting transfers between devices, beside(): return lax.ppermute(values, 'tm', pairs)  5.18 us
  transfers between devices with their start and end apart: 22, of which 9 were waited for; matrix products, arithmetic and copies ran while one was open for 1% of the time, Pallas kernels for 14%

profile of v3, /device:TPU:1, one launch (start us, length us, event | category | flops | bytes accessed | tf_op | source)
XLA Modules:
  0.0 121.5 jit_solution(8766593838413041009)
XLA Ops:
  0.0 3.0 %prepare.1 = (bf16[24,3072]{1,0:T(8,128)(2,1)}, bf16[8,128,768]{2,1,0:T(8,128)(2,1)}) custom-call(bf16[24,1536]{1,0:T(8,128)(2,1)} %pin.1, bf16[24,768]{1,0:T(8,128)(2,1)} %pout.1, bf16[24,2304]{1,0:T(8,128)(2,1)} %mqkv.1, bf16[24,768]{1,0:T(8,128)(2,1)} %mout.1, bf16[2,1,128,768]{3,2,1,0:T(8,128)(2,1)} %features.1), custom_call_target="tpu_custom_call" | custom-call | bytes 3000000 | tf_op jit(solution)/shard_map/prepare/pallas_call | solution.py:56
  3.0 2.2 %collective-permute-start = (bf16[24,3072]{1,0:T(8,128)(2,1)}, bf16[24,3072]{1,0:T(8,128)(2,1)S(1)}, u32[]{:S(2)}, u32[]{:S(2)}) collective-permute-start(bf16[24,3072]{1,0:T(8,128)(2,1)} %get-tuple-element.34), channel_id=1, source_target_pairs={{0,128},{128,0},{1,129},{129,1},{2,130},{130,2},{3,131},{131,3},{4... | collective-permute-start | bytes 442376 | tf_op jit(solution)/shard_map/ppermute | solution.py:351
  5.2 6.5 %all-to-all-start = ((bf16[8,128,768]{2,1,0:T(8,128)(2,1)}), bf16[8,128,768]{2,1,0:T(8,128)(2,1)S(1)}, u32[]{:S(2)}, u32[]{:S(2)}) async-start(bf16[8,128,768]{2,1,0:T(8,128)(2,1)} %get-tuple-element.27), calls=%async_computation | async-start | bytes 3145728 | tf_op jit(solution)/shard_map/all_to_all | solution.py:394
  14.2 1.7 %collective-permute-start.2 = (bf16[96,1536]{1,0:T(8,128)(2,1)S(1)}, bf16[96,1536]{1,0:T(8,128)(2,1)S(1)}, u32[]{:S(2)}, u32[]{:S(2)}) collective-permute-start(bf16[96,1536]{1,0:T(8,128)(2,1)S(1)} %bitcast.14), channel_id=1, source_target_pairs={{0,16},{8,24},{16,32},{24,40},{32,48},{40,56},{48,64},{56,72},{64,... | collective-permute-start | bytes 884744 | tf_op jit(solution)/shard_map/ppermute | solution.py:370
  15.9 4.0 %collective-permute-start.3 = (bf16[96,1536]{1,0:T(8,128)(2,1)S(1)}, bf16[96,1536]{1,0:T(8,128)(2,1)S(1)}, u32[]{:S(2)}, u32[]{:S(2)}) collective-permute-start(bf16[96,1536]{1,0:T(8,128)(2,1)S(1)} %bitcast.15), channel_id=1, source_target_pairs={{0,112},{8,120},{16,0},{24,8},{32,16},{40,24},{48,32},{56,40},{64,... | collective-permute-start | bytes 884744 | tf_op jit(solution)/shard_map/ppermute | solution.py:371
  20.0 7.0 %collective-permute-done.2.refs_1_ = bf16[96,1536]{1,0:T(8,128)(2,1)S(1)} collective-permute-done((bf16[96,1536]{1,0:T(8,128)(2,1)S(1)}, bf16[96,1536]{1,0:T(8,128)(2,1)S(1)}, u32[]{:S(2)}, u32[]{:S(2)}) %collective-permute-start.2) | collective-permute-done | bytes 294944 | tf_op jit(solution)/shard_map/ppermute | solution.py:370
  27.0 2.7 %collective-permute-start.5 = (bf16[96,1536]{1,0:T(8,128)(2,1)S(1)}, bf16[96,1536]{1,0:T(8,128)(2,1)S(1)}, u32[]{:S(2)}, u32[]{:S(2)}) collective-permute-start(bf16[96,1536]{1,0:T(8,128)(2,1)S(1)} %collective-permute-done.3.refs_2_), channel_id=1, source_target_pairs={{0,112},{8,120},{16,0},{24,8},{32,16},{40,24},{48,32},{56,40},{64,... | collective-permute-start | bytes 884744 | tf_op jit(solution)/shard_map/ppermute | solution.py:371
  29.6 6.2 %collective-permute-done.4.refs_3_ = bf16[96,1536]{1,0:T(8,128)(2,1)S(1)} collective-permute-done((bf16[96,1536]{1,0:T(8,128)(2,1)S(1)}, bf16[96,1536]{1,0:T(8,128)(2,1)S(1)}, u32[]{:S(2)}, u32[]{:S(2)}) %collective-permute-start.4) | collective-permute-done | bytes 294944 | tf_op jit(solution)/shard_map/ppermute | solution.py:370
  36.3 3.9 %collective-permute-start.7 = (bf16[96,1536]{1,0:T(8,128)(2,1)S(1)}, bf16[96,1536]{1,0:T(8,128)(2,1)S(1)}, u32[]{:S(2)}, u32[]{:S(2)}) collective-permute-start(bf16[96,1536]{1,0:T(8,128)(2,1)S(1)} %collective-permute-done.5.refs_4_), channel_id=1, source_target_pairs={{0,112},{8,120},{16,0},{24,8},{32,16},{40,24},{48,32},{56,40},{64,... | collective-permute-start | bytes 884744 | tf_op jit(solution)/shard_map/ppermute | solution.py:371
  41.5 5.2 %attend_a.1 = (bf16[320,256]{1,0:T(8,128)(2,1)S(1)}, bf16[1024,768]{1,0:T(8,128)(2,1)S(1)}, bf16[320,768]{1,0:T(8,128)(2,1)S(1)}, bf16[320,768]{1,0:T(8,128)(2,1...) custom-call(s32[2]{0:T(128)S(1)} %copy-done.3, ...), custom_call_target="tpu_custom_call" | custom-call | flops 3000000000 | bytes 5000000 | tf_op jit(solution)/shard_map/attend_a/pallas_call | solution.py:56
  46.9 2.9 %collective-permute-start.9 = (bf16[48,1536]{1,0:T(8,128)(2,1)S(1)}, bf16[48,1536]{1,0:T(8,128)(2,1)S(1)}, u32[]{:S(2)}, u32[]{:S(2)}) collective-permute-start(bf16[48,1536]{1,0:T(8,128)(2,1)S(1)} %slice.21), channel_id=1, source_target_pairs={{0,112},{8,120},{16,0},{24,8},{32,16},{40,24},{48,32},{56,40},{64,... | collective-permute-start | bytes 442376 | tf_op jit(solution)/shard_map/ppermute | solution.py:371
  49.8 3.7 %attend_b.1.context_b = bf16[320,256]{1,0:T(8,128)(2,1)S(1)} custom-call(s32[2]{0:T(128)S(1)} %copy-done.3, bf16[1024,768]{1,0:T(8,128)(2,1)S(1)} %get-tuple-element.28.norm_s, bf16[320,768]{1,0:T(8,128)(2,1)S(1)} %get-tuple-element.29.query_s, bf16[768,768]{1,0:T(8,128)(2,1)S(1)} %get-tuple-element.32.weights), custom_call_target="tpu_custom_call" | custom-call | flops 3000000000 | bytes 5000000 | tf_op jit(solution)/shard_map/attend_b/pallas_call | solution.py:56
  53.7 2.1 %collective-permute-start.10 = (bf16[768,1152]{1,0:T(8,128)(2,1)S(1)}, bf16[768,1152]{1,0:T(8,128)(2,1)S(1)}, u32[]{:S(2)}, u32[]{:S(2)}) collective-permute-start(bf16[768,1152]{1,0:T(8,128)(2,1)S(1)} %get-tuple-element.40.mine), channel_id=1, source_target_pairs={{0,8},{8,0},{16,24},{24,16},{32,40},{40,32},{48,56},{56,48},{64,72... | collective-permute-start | bytes 5308424 | tf_op jit(solution)/shard_map/ppermute | solution.py:404
  55.8 2.4 %collective-permute-start.14 = (bf16[768,384]{1,0:T(8,128)(2,1)S(1)}, bf16[768,384]{1,0:T(8,128)(2,1)S(1)}, u32[]{:S(2)}, u32[]{:S(2)}) collective-permute-start(bf16[768,384]{1,0:T(8,128)(2,1)S(1)} %get-tuple-element.48.refs_0_), channel_id=1, source_target_pairs={{0,2},{1,3},{2,0},{3,1},{4,6},{5,7},{6,4},{7,5},{8,10},{9,11},{10,... | collective-permute-start | bytes 1769480 | tf_op jit(solution)/shard_map/ppermute | solution.py:410
  58.2 4.4 %attend_c.1 = (bf16[320,768]{1,0:T(8,128)(2,1)S(1)}, bf16[320,768]{1,0:T(8,128)(2,1)S(1)}) custom-call(s32[2]{0:T(128)S(1)} %copy-done.3, bf16[1024,768]{1,0:T(8,128)(2,1)S(1)} %get-tuple-element.28.norm_s, bf16[320,768]{1,0:T(8,128)(2,1)S(1)} %get-tuple-element.29.query_s, bf16[320,768]{1,0:T(8,128)(2,1)S(1)} %get-tuple-element.30.raw_s, ...), custom_call_target="tpu_custom_call" | custom-call | flops 3000000000 | bytes 5000000 | tf_op jit(solution)/shard_map/attend_c/pallas_call | solution.py:56
  62.7 2.8 %conv_a.1 = (bf16[128,768]{1,0:T(8,128)(2,1)S(1)}, f32[6,160,128]{2,1,0:T(8,128)S(1)}) custom-call(s32[2]{0:T(128)S(1)} %copy-done.3, bf16[320,768]{1,0:T(8,128)(2,1)S(1)} %get-tuple-element.43.normed, bf16[320,768]{1,0:T(8,128)(2,1)S(1)} %get-tuple-element.44.first, bf16[768,1152]{1,0:T(8,128)(2,1)S(1)} %get-tuple-element.40.mine, ...), custom_call_target="tpu_custom_call" | custom-call | flops 2000000000 | bytes 6000000 | tf_op jit(solution)/shard_map/conv_a/pallas_call | solution.py:56
  65.9 2.4 %collective-permute-start.13 = (bf16[768,384]{1,0:T(8,128)(2,1)S(1)}, bf16[768,384]{1,0:T(8,128)(2,1)S(1)}, u32[]{:S(2)}, u32[]{:S(2)}) collective-permute-start(bf16[768,384]{1,0:T(8,128)(2,1)S(1)} %get-tuple-element.48.refs_0_), channel_id=1, source_target_pairs={{0,3},{1,0},{2,1},{3,2},{4,7},{5,4},{6,5},{7,6},{8,11},{9,8},{10,9... | collective-permute-start | bytes 1769480 | tf_op jit(solution)/shard_map/ppermute | solution.py:410
  68.3 2.7 %collective-permute-start.11 = (bf16[128,768]{1,0:T(8,128)(2,1)S(1)}, bf16[128,768]{1,0:T(8,128)(2,1)S(1)}, u32[]{:S(2)}, u32[]{:S(2)}) collective-permute-start(bf16[128,768]{1,0:T(8,128)(2,1)S(1)} %get-tuple-element.46), channel_id=1, source_target_pairs={{0,4},{1,5},{2,6},{3,7},{4,0},{5,1},{6,2},{7,3},{8,12},{9,13},{10,... | collective-permute-start | bytes 589832 | tf_op jit(solution)/shard_map/ppermute | solution.py:414
  72.1 2.7 %collective-permute-done.11 = bf16[128,768]{1,0:T(8,128)(2,1)S(1)} collective-permute-done((bf16[128,768]{1,0:T(8,128)(2,1)S(1)}, bf16[128,768]{1,0:T(8,128)(2,1)S(1)}, u32[]{:S(2)}, u32[]{:S(2)}) %collective-permute-start.11) | collective-permute-done | bytes 196640 | tf_op jit(solution)/shard_map/ppermute | solution.py:414
  75.6 7.5 %all-to-all-start.1 = ((bf16[16,16,768]{2,1,0:T(8,128)(2,1)}), bf16[16,16,768]{2,1,0:T(8,128)(2,1)S(1)}, u32[]{:S(2)}, u32[]{:S(2)}) async-start(bf16[16,16,768]{2,1,0:T(8,128)(2,1)} %bitcast.6), calls=%async_computation.1 | async-start | bytes 786432 | tf_op jit(solution)/shard_map/all_to_all | solution.py:421
  86.1 11.6 %all-to-all-done.1 = bf16[16,16,768]{2,1,0:T(8,128)(2,1)S(1)} async-done(((bf16[16,16,768]{2,1,0:T(8,128)(2,1)}), bf16[16,16,768]{2,1,0:T(8,128)(2,1)S(1)}, u32[]{:S(2)}, u32[]{:S(2)}) %all-to-all-start.1) | async-done | bytes 393248 | tf_op jit(solution)/shard_map/all_to_all | solution.py:421
  97.7 5.6 %merge.1 = bf16[256,768]{1,0:T(8,128)(2,1)} custom-call(s32[1,256]{1,0:T(1,128)S(1)} %broadcast_in_dim_reshape.3.live, bf16[256,768]{1,0:T(8,128)(2,1)S(1)} %bitcast.17, f32[3,768]{1,0:T(4,128)S(1)} %copy-done.2, bf16[768,384]{1,0:T(8,128)(2,1)S(1)} %get-tuple-element.48.refs_0_, bf16[768,384]{1,0:T(8,128)(2,1)S(1)} %collective-permute-done.12.refs_1_, ...), custom_call_target="tpu_custom_call" | custom-call | flops 2000000000 | bytes 8000000 | tf_op jit(solution)/shard_map/merge/pallas_call | solution.py:56
  103.3 3.5 %all-to-all-start.2 = ((bf16[16,16,768]{2,1,0:T(8,128)(2,1)}), bf16[16,16,768]{2,1,0:T(8,128)(2,1)S(1)}, u32[]{:S(2)}, u32[]{:S(2)}) async-start(bf16[16,16,768]{2,1,0:T(8,128)(2,1)} %bitcast.8), calls=%async_computation.2 | async-start | bytes 786432 | tf_op jit(solution)/shard_map/all_to_all | solution.py:427
  106.7 14.0 %all-to-all-done.2 = bf16[16,16,768]{2,1,0:T(8,128)(2,1)S(1)} async-done(((bf16[16,16,768]{2,1,0:T(8,128)(2,1)}), bf16[16,16,768]{2,1,0:T(8,128)(2,1)S(1)}, u32[]{:S(2)}, u32[]{:S(2)}) %all-to-all-start.2) | async-done | bytes 393248 | tf_op jit(solution)/shard_map/all_to_all | solution.py:427
  (52 shorter events, 10.7 us)
Async XLA Ops:
  0.0 85.8 %copy-start = (s32[2,16]{1,0:T(2,128)S(1)}, s32[2,16]{1,0:T(2,128)}, u32[]{:S(2)}) copy-start(s32[2,16]{1,0:T(2,128)} %param.13) | copy-start | bytes 388
  3.0 8.7 %collective-permute-start = (bf16[24,3072]{1,0:T(8,128)(2,1)}, bf16[24,3072]{1,0:T(8,128)(2,1)S(1)}, u32[]{:S(2)}, u32[]{:S(2)}) collective-permute-start(bf16[24,3072]{1,0:T(8,128)(2,1)} %get-tuple-element.34), channel_id=1, source_target_pairs={{0,128},{128,0},{1,129},{129,1},{2,130},{130,2},{3,131},{131,3},{4... | collective-permute-start | bytes 442376 | tf_op jit(solution)/shard_map/ppermute | solution.py:351
  5.2 30.6 %all-to-all-start = ((bf16[8,128,768]{2,1,0:T(8,128)(2,1)}), bf16[8,128,768]{2,1,0:T(8,128)(2,1)S(1)}, u32[]{:S(2)}, u32[]{:S(2)}) async-start(bf16[8,128,768]{2,1,0:T(8,128)(2,1)} %get-tuple-element.27), calls=%async_computation | async-start | bytes 3145728 | tf_op jit(solution)/shard_map/all_to_all | solution.py:394
  11.7 28.5 %copy-start.2 = (f32[3,768]{1,0:T(4,128)S(1)}, f32[3,768]{1,0:T(4,128)}, u32[]{:S(2)}) copy-start(f32[3,768]{1,0:T(4,128)} %gains.5) | copy-start | bytes 27652
  11.8 2.3 %collective-permute-start.1 = (bf16[2,24,1536]{2,1,0:T(8,128)(2,1)S(1)}, bf16[2,24,1536]{2,1,0:T(8,128)(2,1)S(1)}, u32[]{:S(2)}, u32[]{:S(2)}) collective-permute-start(bf16[2,24,1536]{2,1,0:T(8,128)(2,1)S(1)} %get-tuple-element.50), channel_id=1, source_target_pairs={{0,8},{8,0},{16,24},{24,16},{32,40},{40,32},{48,56},{56,48},{64,72... | collective-permute-start | bytes 442376 | tf_op jit(solution)/shard_map/ppermute | solution.py:356
  14.2 12.7 %collective-permute-start.2 = (bf16[96,1536]{1,0:T(8,128)(2,1)S(1)}, bf16[96,1536]{1,0:T(8,128)(2,1)S(1)}, u32[]{:S(2)}, u32[]{:S(2)}) collective-permute-start(bf16[96,1536]{1,0:T(8,128)(2,1)S(1)} %bitcast.14), channel_id=1, source_target_pairs={{0,16},{8,24},{16,32},{24,40},{32,48},{40,56},{48,64},{56,72},{64,... | collective-permute-start | bytes 884744 | tf_op jit(solution)/shard_map/ppermute | solution.py:370
  15.9 11.0 %collective-permute-start.3 = (bf16[96,1536]{1,0:T(8,128)(2,1)S(1)}, bf16[96,1536]{1,0:T(8,128)(2,1)S(1)}, u32[]{:S(2)}, u32[]{:S(2)}) collective-permute-start(bf16[96,1536]{1,0:T(8,128)(2,1)S(1)} %bitcast.15), channel_id=1, source_target_pairs={{0,112},{8,120},{16,0},{24,8},{32,16},{40,24},{48,32},{56,40},{64,... | collective-permute-start | bytes 884744 | tf_op jit(solution)/shard_map/ppermute | solution.py:371
  26.9 8.9 %collective-permute-start.4 = (bf16[96,1536]{1,0:T(8,128)(2,1)S(1)}, bf16[96,1536]{1,0:T(8,128)(2,1)S(1)}, u32[]{:S(2)}, u32[]{:S(2)}) collective-permute-start(bf16[96,1536]{1,0:T(8,128)(2,1)S(1)} %collective-permute-done.2.refs_1_), channel_id=1, source_target_pairs={{0,16},{8,24},{16,32},{24,40},{32,48},{40,56},{48,64},{56,72},{64,... | collective-permute-start | bytes 884744 | tf_op jit(solution)/shard_map/ppermute | solution.py:370
  27.0 9.3 %collective-permute-start.5 = (bf16[96,1536]{1,0:T(8,128)(2,1)S(1)}, bf16[96,1536]{1,0:T(8,128)(2,1)S(1)}, u32[]{:S(2)}, u32[]{:S(2)}) collective-permute-start(bf16[96,1536]{1,0:T(8,128)(2,1)S(1)} %collective-permute-done.3.refs_2_), channel_id=1, source_target_pairs={{0,112},{8,120},{16,0},{24,8},{32,16},{40,24},{48,32},{56,40},{64,... | collective-permute-start | bytes 884744 | tf_op jit(solution)/shard_map/ppermute | solution.py:371
  35.8 10.9 %collective-permute-start.6 = (bf16[96,1536]{1,0:T(8,128)(2,1)S(1)}, bf16[96,1536]{1,0:T(8,128)(2,1)S(1)}, u32[]{:S(2)}, u32[]{:S(2)}) collective-permute-start(bf16[96,1536]{1,0:T(8,128)(2,1)S(1)} %collective-permute-done.4.refs_3_), channel_id=1, source_target_pairs={{0,16},{8,24},{16,32},{24,40},{32,48},{40,56},{48,64},{56,72},{64,... | collective-permute-start | bytes 884744 | tf_op jit(solution)/shard_map/ppermute | solution.py:370
  36.3 10.6 %collective-permute-start.7 = (bf16[96,1536]{1,0:T(8,128)(2,1)S(1)}, bf16[96,1536]{1,0:T(8,128)(2,1)S(1)}, u32[]{:S(2)}, u32[]{:S(2)}) collective-permute-start(bf16[96,1536]{1,0:T(8,128)(2,1)S(1)} %collective-permute-done.5.refs_4_), channel_id=1, source_target_pairs={{0,112},{8,120},{16,0},{24,8},{32,16},{40,24},{48,32},{56,40},{64,... | collective-permute-start | bytes 884744 | tf_op jit(solution)/shard_map/ppermute | solution.py:371
  46.7 6.7 %collective-permute-start.8 = (bf16[48,1536]{1,0:T(8,128)(2,1)S(1)}, bf16[48,1536]{1,0:T(8,128)(2,1)S(1)}, u32[]{:S(2)}, u32[]{:S(2)}) collective-permute-start(bf16[48,1536]{1,0:T(8,128)(2,1)S(1)} %slice.20), channel_id=1, source_target_pairs={{0,16},{8,24},{16,32},{24,40},{32,48},{40,56},{48,64},{56,72},{64,... | collective-permute-start | bytes 442376 | tf_op jit(solution)/shard_map/ppermute | solution.py:370
  46.9 6.6 %collective-permute-start.9 = (bf16[48,1536]{1,0:T(8,128)(2,1)S(1)}, bf16[48,1536]{1,0:T(8,128)(2,1)S(1)}, u32[]{:S(2)}, u32[]{:S(2)}) collective-permute-start(bf16[48,1536]{1,0:T(8,128)(2,1)S(1)} %slice.21), channel_id=1, source_target_pairs={{0,112},{8,120},{16,0},{24,8},{32,16},{40,24},{48,32},{56,40},{64,... | collective-permute-start | bytes 442376 | tf_op jit(solution)/shard_map/ppermute | solution.py:371
  53.7 8.9 %collective-permute-start.10 = (bf16[768,1152]{1,0:T(8,128)(2,1)S(1)}, bf16[768,1152]{1,0:T(8,128)(2,1)S(1)}, u32[]{:S(2)}, u32[]{:S(2)}) collective-permute-start(bf16[768,1152]{1,0:T(8,128)(2,1)S(1)} %get-tuple-element.40.mine), channel_id=1, source_target_pairs={{0,8},{8,0},{16,24},{24,16},{32,40},{40,32},{48,56},{56,48},{64,72... | collective-permute-start | bytes 5308424 | tf_op jit(solution)/shard_map/ppermute | solution.py:404
  55.8 27.5 %collective-permute-start.14 = (bf16[768,384]{1,0:T(8,128)(2,1)S(1)}, bf16[768,384]{1,0:T(8,128)(2,1)S(1)}, u32[]{:S(2)}, u32[]{:S(2)}) collective-permute-start(bf16[768,384]{1,0:T(8,128)(2,1)S(1)} %get-tuple-element.48.refs_0_), channel_id=1, source_target_pairs={{0,2},{1,3},{2,0},{3,1},{4,6},{5,7},{6,4},{7,5},{8,10},{9,11},{10,... | collective-permute-start | bytes 1769480 | tf_op jit(solution)/shard_map/ppermute | solution.py:410
  65.5 19.8 %collective-permute-start.12 = (bf16[768,384]{1,0:T(8,128)(2,1)S(1)}, bf16[768,384]{1,0:T(8,128)(2,1)S(1)}, u32[]{:S(2)}, u32[]{:S(2)}) collective-permute-start(bf16[768,384]{1,0:T(8,128)(2,1)S(1)} %get-tuple-element.48.refs_0_), channel_id=1, source_target_pairs={{0,1},{1,2},{2,3},{3,0},{4,5},{5,6},{6,7},{7,4},{8,9},{9,10},{10,1... | collective-permute-start | bytes 1769480 | tf_op jit(solution)/shard_map/ppermute | solution.py:410
  65.9 19.9 %collective-permute-start.13 = (bf16[768,384]{1,0:T(8,128)(2,1)S(1)}, bf16[768,384]{1,0:T(8,128)(2,1)S(1)}, u32[]{:S(2)}, u32[]{:S(2)}) collective-permute-start(bf16[768,384]{1,0:T(8,128)(2,1)S(1)} %get-tuple-element.48.refs_0_), channel_id=1, source_target_pairs={{0,3},{1,0},{2,1},{3,2},{4,7},{5,4},{6,5},{7,6},{8,11},{9,8},{10,9... | collective-permute-start | bytes 1769480 | tf_op jit(solution)/shard_map/ppermute | solution.py:410
  68.3 6.6 %collective-permute-start.11 = (bf16[128,768]{1,0:T(8,128)(2,1)S(1)}, bf16[128,768]{1,0:T(8,128)(2,1)S(1)}, u32[]{:S(2)}, u32[]{:S(2)}) collective-permute-start(bf16[128,768]{1,0:T(8,128)(2,1)S(1)} %get-tuple-element.46), channel_id=1, source_target_pairs={{0,4},{1,5},{2,6},{3,7},{4,0},{5,1},{6,2},{7,3},{8,12},{9,13},{10,... | collective-permute-start | bytes 589832 | tf_op jit(solution)/shard_map/ppermute | solution.py:414
  75.6 22.0 %all-to-all-start.1 = ((bf16[16,16,768]{2,1,0:T(8,128)(2,1)}), bf16[16,16,768]{2,1,0:T(8,128)(2,1)S(1)}, u32[]{:S(2)}, u32[]{:S(2)}) async-start(bf16[16,16,768]{2,1,0:T(8,128)(2,1)} %bitcast.6), calls=%async_computation.1 | async-start | bytes 786432 | tf_op jit(solution)/shard_map/all_to_all | solution.py:421
  83.1 2.9 %collective-permute-start.15 = (bf16[768,384]{1,0:T(8,128)(2,1)S(1)}, bf16[768,384]{1,0:T(8,128)(2,1)S(1)}, u32[]{:S(2)}, u32[]{:S(2)}) collective-permute-start(bf16[768,384]{1,0:T(8,128)(2,1)S(1)} %get-tuple-element.48.refs_0_), channel_id=1, source_target_pairs={{0,8},{8,0},{16,24},{24,16},{32,40},{40,32},{48,56},{56,48},{64,72... | collective-permute-start | bytes 1769480 | tf_op jit(solution)/shard_map/ppermute | solution.py:417
  83.3 2.8 %collective-permute-start.18 = (bf16[768,384]{1,0:T(8,128)(2,1)S(1)}, bf16[768,384]{1,0:T(8,128)(2,1)}, u32[]{:S(2)}, u32[]{:S(2)}) collective-permute-start(bf16[768,384]{1,0:T(8,128)(2,1)S(1)} %collective-permute-done.14.refs_3_), channel_id=1, source_target_pairs={{0,8},{8,0},{16,24},{24,16},{32,40},{40,32},{48,56},{56,48},{64,72... | collective-permute-start | bytes 1769480 | tf_op jit(solution)/shard_map/ppermute | solution.py:417
  85.3 12.4 %collective-permute-start.16 = (bf16[768,384]{1,0:T(8,128)(2,1)S(1)}, bf16[768,384]{1,0:T(8,128)(2,1)}, u32[]{:S(2)}, u32[]{:S(2)}) collective-permute-start(bf16[768,384]{1,0:T(8,128)(2,1)S(1)} %collective-permute-done.12.refs_1_), channel_id=1, source_target_pairs={{0,8},{8,0},{16,24},{24,16},{32,40},{40,32},{48,56},{56,48},{64,72... | collective-permute-start | bytes 1769480 | tf_op jit(solution)/shard_map/ppermute | solution.py:417
  85.8 11.9 %collective-permute-start.17 = (bf16[768,384]{1,0:T(8,128)(2,1)S(1)}, bf16[768,384]{1,0:T(8,128)(2,1)}, u32[]{:S(2)}, u32[]{:S(2)}) collective-permute-start(bf16[768,384]{1,0:T(8,128)(2,1)S(1)} %collective-permute-done.13.refs_2_), channel_id=1, source_target_pairs={{0,8},{8,0},{16,24},{24,16},{32,40},{40,32},{48,56},{56,48},{64,72... | collective-permute-start | bytes 1769480 | tf_op jit(solution)/shard_map/ppermute | solution.py:417
  103.3 17.4 %all-to-all-start.2 = ((bf16[16,16,768]{2,1,0:T(8,128)(2,1)}), bf16[16,16,768]{2,1,0:T(8,128)(2,1)S(1)}, u32[]{:S(2)}, u32[]{:S(2)}) async-start(bf16[16,16,768]{2,1,0:T(8,128)(2,1)} %bitcast.8), calls=%async_computation.2 | async-start | bytes 786432 | tf_op jit(solution)/shard_map/all_to_all | solution.py:427
  (4 other events, 38.7 us)

commit v4 on v3

--- a/solution.py
+++ b/solution.py
@@ -1,3 +1,5 @@
+import functools
+
 import jax
 import jax.numpy as jnp
 from jax import lax
@@ -75,7 +77,7 @@
     pin, pout, mqkv, mout, features, out_ref, spread_ref, pin_s, pout_s, mqkv_s, mout_s, sems
 ):
     shards_in = ((pin, pin_s), (pout, pout_s), (mqkv, mqkv_s), (mout, mout_s))
-    blocks = [(features.at[t // ROWS, 0], spread_ref.at[t]) for t in range(2 * ROWS)]
+    blocks = [(features.at[u, 0], spread_ref.at[u * ROWS]) for u in range(2)]
     copies = [
         pltpu.make_async_copy(a, b, sems.at[n]) for n, (a, b) in enumerate((*shards_in, *blocks))
     ]
@@ -104,6 +106,9 @@
 
     for copy in copies[4:]:
         copy.wait()
+    for t in range(2 * ROWS):
+        if t % ROWS:
+            spread_ref[t] = spread_ref[t // ROWS * ROWS]
 
 
 def run_prepare(features, *shards_in):
@@ -111,7 +116,7 @@
     scratch = [pltpu.VMEM(w.shape, w.dtype) for w in shards_in]
     return call(
         prepare_kernel, [bf16(height, 4 * D), bf16(count, SPAN, D)],
-        scratch + [pltpu.SemaphoreType.DMA((4 + count,))],
+        scratch + [pltpu.SemaphoreType.DMA((6,))],
         (0, 3 * 10**6, 0), "prepare", [Far(w) for w in (*shards_in, features)], limit=56,
     )
 
@@ -235,50 +240,33 @@
         out_ref[:, lanes] = out.astype(jnp.bfloat16)
 
 
-def conv_a_kernel(
-    lengths, normed, first, mine, other, taps, out_ref, home_ref, gated_s, swish_s, kept_s
-):
+def conv_kernel(seg, lengths, normed, first, mine, other, taps, out_ref, gated_s, swish_s, kept_s):
     place, length, core = lax.axis_index("tm"), my_length(lengths), my_core()
-    lives = []
-    for b in (place, lax.rem(place + ROWS, 2 * ROWS)):
-        frame = b * SPAN - PAD + lax.broadcasted_iota(jnp.int32, (SEG, 1), 0)
-        lives.append((frame >= 0) & (frame < length))
-    live = jnp.concatenate(lives, axis=0)
+    at = seg * SEG
+    block = lax.rem(place + seg * ROWS, 2 * ROWS)
+    frame = block * SPAN - PAD + lax.broadcasted_iota(jnp.int32, (SEG, 1), 0)
+    live = (frame >= 0) & (frame < length)
+    rows = normed[at : at + SEG]
     for h, half in zip((core, 1 - core), (mine, other)):
+        wide = mm(rows, half[:, :D])
         for n in range(PAIRS // 2):
             lo = n * 128
-            both = jnp.concatenate(
-                [half[:, lo : lo + 128], half[:, D // 2 + lo : D // 2 + lo + 128]], axis=1
-            )
-            wide = mm(normed[...], both)
-            gated = jnp.where(live, wide[:, :128] * jax.nn.sigmoid(wide[:, 128:]), 0.0)
-            gated = gated.astype(jnp.bfloat16).astype(jnp.float32)
-            chunk = h * (PAIRS // 2) + n
-            home_ref[chunk] = gated[:SEG]
-            gated_s[chunk] = gated[SEG:]
+            gate = wide[:, D // 2 + lo : D // 2 + lo + 128]
+            gated = jnp.where(live, wide[:, lo : lo + 128] * jax.nn.sigmoid(gate), 0.0)
+            gated_s[h * (PAIRS // 2) + n] = gated.astype(jnp.bfloat16).astype(jnp.float32)
     depthwise(gated_s, 0, taps, swish_s)
-    kept_s[...] = first[SEG + PAD : SEG + PAD + SPAN]
+    kept_s[...] = first[at + PAD : at + PAD + SPAN]
     project_out(swish_s, kept_s, core, (mine, other), out_ref)
 
 
-def conv_b_kernel(home, first, mine, other, taps, out_ref, swish_s, kept_s):
-    depthwise(home, 0, taps, swish_s)
-    kept_s[...] = first[PAD : PAD + SPAN]
-    project_out(swish_s, kept_s, my_core(), (mine, other), out_ref)
-
-
-def run_conv(lengths, normed, first, mine, other, taps):
-    gated = jax.ShapeDtypeStruct((PAIRS, SEG, 128), jnp.float32)
+def run_conv(seg, lengths, *operands):
     block = pltpu.VMEM((SPAN, D), jnp.bfloat16)
-    away, home = call(
-        conv_a_kernel, [bf16(SPAN, D), gated], [pltpu.VMEM(gated.shape, jnp.float32), block, block],
-        (2 * 10**9, 6 * 10**6, 10**6), "conv_a", [normed, first, mine, other, taps], lengths,
-    )
-    (kept,) = call(
-        conv_b_kernel, [bf16(SPAN, D)], [block, block],
-        (10**9, 4 * 10**6, 10**6), "conv_b", [home, first, mine, other, taps],
-    )
-    return kept, away
+    (out,) = call(
+        functools.partial(conv_kernel, seg), [bf16(SPAN, D)],
+        [pltpu.VMEM((PAIRS, SEG, 128), jnp.float32), block, block],
+        (10**9, 6 * 10**6, 10**6), "conv", list(operands), lengths,
+    )
+    return out
 
 
 def merge_kernel(live, block, gains, *refs):
@@ -409,11 +397,11 @@
         pairs = [(i, i // ROWS * ROWS + (i + k) % ROWS) for i in range(count)]
         return lax.ppermute(values, "tm", pairs)
 
-    far = beside(eighth, 2)
-    kept, away = run_conv(lengths, normed, first, mine, other, depth_taps.astype(jnp.float32))
+    held = [eighth] + [beside(after(eighth, first), k) for k in (1, 3, 2)]
+    operands = (normed, first, mine, other, depth_taps.astype(jnp.float32))
+    away = run_conv(1, lengths, *operands)
     back = lax.ppermute(away, "tm", other_row)
-    late = after(eighth, away)
-    held = [eighth, beside(late, 1), beside(late, 3), far]
+    kept = run_conv(0, lengths, after(normed, away), *operands[1:])
     eighths = held + [lax.ppermute(one, "chan", point.swap) for one in held]
     second = jnp.concatenate([kept, back], axis=0)
     channels = lax.axis_size("chan")

time: 122 us -> 120 us (0.984)
  waiting for transfers between devices: 44.4 us -> 33.6 us
  starting transfers between devices: 47.7 us -> 56.1 us
    ppermute x4, waiting for transfers between devices: 13.3 us -> 1.5 us  [step(): lax.ppermute(after(high, *others) if others else high, 'chan', self.up)]
    ppermute x4, waiting for transfers between devices: 0.01 us -> 11.1 us  [step(): lax.ppermute(after(low, *others) if others else low, 'chan', self.down)]
    ppermute x4, starting transfers between devices: 1.02 us -> 10.3 us  [shards(): eighths = held + [lax.ppermute(one, 'chan', point.swap) for one in held]]
    all_to_all x1, waiting for transfers between devices: 11.6 us -> 2.34 us  [shards(): lax.all_to_all(second.reshape(channels, part, D), 'chan', split_axis=0, c...]
    ppermute x4, starting transfers between devices: 13.6 us -> 17.4 us  [step(): lax.ppermute(after(low, *others) if others else low, 'chan', self.down)]
    all_to_all x1, starting transfers between devices: 7.47 us -> 5.1 us  [shards(): lax.all_to_all(second.reshape(channels, part, D), 'chan', split_axis=0, c...]
    ppermute x4, starting transfers between devices: 2.24 us -> 0.27 us  [step(): lax.ppermute(after(high, *others) if others else high, 'chan', self.up)]
    ppermute x3, starting transfers between devices: 5.18 us -> 3.56 us  [beside(): return lax.ppermute(values, 'tm', pairs)]
  transfers between devices with their start and end apart: 22 -> 22, of which waited for: 9 -> 11; matrix products, arithmetic and copies ran while one was open for 1% -> 1% of each run, Pallas kernels for 14% -> 15%
where the time goes in v4:
time: 120 us
  starting transfers between devices  56.1 us (47%)
  waiting for transfers between devices  33.6 us (28%)
  Pallas kernels  26.8 us (22%)
  other arithmetic  1.68 us (1%)
  local copies, waits for them, and re-layouts  1.49 us (1%)
    pallas_call x8, Pallas kernels, call(): pl.pallas_call(kernel, in_specs=[pl.BlockSpec(memory_space=pltpu.SMEM)] *...  26.8 us
    ppermute x4, starting transfers between devices, step(): lax.ppermute(after(low, *others) if others else low, 'chan', self.down)  17.4 us
    all_to_all x1, waiting for transfers between devices, shards(): lax.all_to_all(merged.reshape(channels, part, D), 'chan', split_axis=0, c...  14 us
    ppermute x4, waiting for transfers between devices, step(): lax.ppermute(after(low, *others) if others else low, 'chan', self.down)  11.1 us
    ppermute x4, starting transfers between devices, shards(): eighths = held + [lax.ppermute(one, 'chan', point.swap) for one in held]  10.3 us
    all_to_all x1, starting transfers between devices, shards(): lax.all_to_all(spread, 'tm', split_axis=0, concat_axis=0, tiled=True)  6.49 us
    all_to_all x1, starting transfers between devices, shards(): lax.all_to_all(second.reshape(channels, part, D), 'chan', split_axis=0, c...  5.1 us
    ppermute x3, starting transfers between devices, beside(): return lax.ppermute(values, 'tm', pairs)  3.56 us
  transfers between devices with their start and end apart: 22, of which 11 were waited for; matrix products, arithmetic and copies ran while one was open for 1% of the time, Pallas kernels for 15%

profile of v4, /device:TPU:1, one launch (start us, length us, event | category | flops | bytes accessed | tf_op | source)
XLA Modules:
  0.0 119.9 jit_solution(16038660237823438684)
XLA Ops:
  0.0 2.5 %prepare.1 = (bf16[24,3072]{1,0:T(8,128)(2,1)}, bf16[8,128,768]{2,1,0:T(8,128)(2,1)}) custom-call(bf16[24,1536]{1,0:T(8,128)(2,1)} %pin.1, bf16[24,768]{1,0:T(8,128)(2,1)} %pout.1, bf16[24,2304]{1,0:T(8,128)(2,1)} %mqkv.1, bf16[24,768]{1,0:T(8,128)(2,1)} %mout.1, bf16[2,1,128,768]{3,2,1,0:T(8,128)(2,1)} %features.1), custom_call_target="tpu_custom_call" | custom-call | bytes 3000000 | tf_op jit(solution)/shard_map/prepare/pallas_call | solution.py:58
  2.5 2.2 %collective-permute-start = (bf16[24,3072]{1,0:T(8,128)(2,1)}, bf16[24,3072]{1,0:T(8,128)(2,1)S(1)}, u32[]{:S(2)}, u32[]{:S(2)}) collective-permute-start(bf16[24,3072]{1,0:T(8,128)(2,1)} %get-tuple-element.33), channel_id=1, source_target_pairs={{0,128},{128,0},{1,129},{129,1},{2,130},{130,2},{3,131},{131,3},{4... | collective-permute-start | bytes 442376 | tf_op jit(solution)/shard_map/ppermute | solution.py:339
  4.7 6.5 %all-to-all-start = ((bf16[8,128,768]{2,1,0:T(8,128)(2,1)}), bf16[8,128,768]{2,1,0:T(8,128)(2,1)S(1)}, u32[]{:S(2)}, u32[]{:S(2)}) async-start(bf16[8,128,768]{2,1,0:T(8,128)(2,1)} %get-tuple-element.26), calls=%async_computation | async-start | bytes 3145728 | tf_op jit(solution)/shard_map/all_to_all | solution.py:382
  13.7 5.7 %collective-permute-start.3 = (bf16[96,1536]{1,0:T(8,128)(2,1)S(1)}, bf16[96,1536]{1,0:T(8,128)(2,1)S(1)}, u32[]{:S(2)}, u32[]{:S(2)}) collective-permute-start(bf16[96,1536]{1,0:T(8,128)(2,1)S(1)} %bitcast.14), channel_id=1, source_target_pairs={{0,112},{8,120},{16,0},{24,8},{32,16},{40,24},{48,32},{56,40},{64,... | collective-permute-start | bytes 884744 | tf_op jit(solution)/shard_map/ppermute | solution.py:359
  19.4 6.0 %collective-permute-done.3.refs_2_ = bf16[96,1536]{1,0:T(8,128)(2,1)S(1)} collective-permute-done((bf16[96,1536]{1,0:T(8,128)(2,1)S(1)}, bf16[96,1536]{1,0:T(8,128)(2,1)S(1)}, u32[]{:S(2)}, u32[]{:S(2)}) %collective-permute-start.3) | collective-permute-done | bytes 294944 | tf_op jit(solution)/shard_map/ppermute | solution.py:359
  25.4 3.4 %collective-permute-start.5 = (bf16[96,1536]{1,0:T(8,128)(2,1)S(1)}, bf16[96,1536]{1,0:T(8,128)(2,1)S(1)}, u32[]{:S(2)}, u32[]{:S(2)}) collective-permute-start(bf16[96,1536]{1,0:T(8,128)(2,1)S(1)} %collective-permute-done.3.refs_2_), channel_id=1, source_target_pairs={{0,112},{8,120},{16,0},{24,8},{32,16},{40,24},{48,32},{56,40},{64,... | collective-permute-start | bytes 884744 | tf_op jit(solution)/shard_map/ppermute | solution.py:359
  28.8 5.1 %collective-permute-done.5.refs_4_ = bf16[96,1536]{1,0:T(8,128)(2,1)S(1)} collective-permute-done((bf16[96,1536]{1,0:T(8,128)(2,1)S(1)}, bf16[96,1536]{1,0:T(8,128)(2,1)S(1)}, u32[]{:S(2)}, u32[]{:S(2)}) %collective-permute-start.5) | collective-permute-done | bytes 294944 | tf_op jit(solution)/shard_map/ppermute | solution.py:359
  34.1 5.6 %collective-permute-start.7 = (bf16[96,1536]{1,0:T(8,128)(2,1)S(1)}, bf16[96,1536]{1,0:T(8,128)(2,1)S(1)}, u32[]{:S(2)}, u32[]{:S(2)}) collective-permute-start(bf16[96,1536]{1,0:T(8,128)(2,1)S(1)} %collective-permute-done.5.refs_4_), channel_id=1, source_target_pairs={{0,112},{8,120},{16,0},{24,8},{32,16},{40,24},{48,32},{56,40},{64,... | collective-permute-start | bytes 884744 | tf_op jit(solution)/shard_map/ppermute | solution.py:359
  41.0 5.1 %attend_a.1 = (bf16[320,256]{1,0:T(8,128)(2,1)S(1)}, bf16[1024,768]{1,0:T(8,128)(2,1)S(1)}, bf16[320,768]{1,0:T(8,128)(2,1)S(1)}, bf16[320,768]{1,0:T(8,128)(2,1...) custom-call(s32[2]{0:T(128)S(1)} %copy-done.1, ...), custom_call_target="tpu_custom_call" | custom-call | flops 3000000000 | bytes 5000000 | tf_op jit(solution)/shard_map/attend_a/pallas_call | solution.py:58
  46.2 2.7 %collective-permute-start.9 = (bf16[48,1536]{1,0:T(8,128)(2,1)S(1)}, bf16[48,1536]{1,0:T(8,128)(2,1)S(1)}, u32[]{:S(2)}, u32[]{:S(2)}) collective-permute-start(bf16[48,1536]{1,0:T(8,128)(2,1)S(1)} %slice.21), channel_id=1, source_target_pairs={{0,112},{8,120},{16,0},{24,8},{32,16},{40,24},{48,32},{56,40},{64,... | collective-permute-start | bytes 442376 | tf_op jit(solution)/shard_map/ppermute | solution.py:359
  49.2 3.7 %attend_b.1.context_b = bf16[320,256]{1,0:T(8,128)(2,1)S(1)} custom-call(s32[2]{0:T(128)S(1)} %copy-done.1, bf16[1024,768]{1,0:T(8,128)(2,1)S(1)} %get-tuple-element.27.norm_s, bf16[320,768]{1,0:T(8,128)(2,1)S(1)} %get-tuple-element.28.query_s, bf16[768,768]{1,0:T(8,128)(2,1)S(1)} %get-tuple-element.31.weights), custom_call_target="tpu_custom_call" | custom-call | flops 3000000000 | bytes 5000000 | tf_op jit(solution)/shard_map/attend_b/pallas_call | solution.py:58
  54.6 3.0 %collective-permute-start.10 = (bf16[768,1152]{1,0:T(8,128)(2,1)S(1)}, bf16[768,1152]{1,0:T(8,128)(2,1)S(1)}, u32[]{:S(2)}, u32[]{:S(2)}) collective-permute-start(bf16[768,1152]{1,0:T(8,128)(2,1)S(1)} %get-tuple-element.39.mine), channel_id=1, source_target_pairs={{0,8},{8,0},{16,24},{24,16},{32,40},{40,32},{48,56},{56,48},{64,72... | collective-permute-start | bytes 5308424 | tf_op jit(solution)/shard_map/ppermute | solution.py:392
  57.6 4.4 %attend_c.1 = (bf16[320,768]{1,0:T(8,128)(2,1)S(1)}, bf16[320,768]{1,0:T(8,128)(2,1)S(1)}) custom-call(s32[2]{0:T(128)S(1)} %copy-done.1, bf16[1024,768]{1,0:T(8,128)(2,1)S(1)} %get-tuple-element.27.norm_s, bf16[320,768]{1,0:T(8,128)(2,1)S(1)} %get-tuple-element.28.query_s, bf16[320,768]{1,0:T(8,128)(2,1)S(1)} %get-tuple-element.29.raw_s, ...), custom_call_target="tpu_custom_call" | custom-call | flops 3000000000 | bytes 5000000 | tf_op jit(solution)/shard_map/attend_c/pallas_call | solution.py:58
  62.6 2.2 %collective-permute-start.13 = (bf16[768,384]{1,0:T(8,128)(2,1)S(1)}, bf16[768,384]{1,0:T(8,128)(2,1)S(1)}, u32[]{:S(2)}, u32[]{:S(2)}) collective-permute-start(bf16[768,384]{1,0:T(8,128)(2,1)S(1)} %get-tuple-element.46.refs_0_), channel_id=1, source_target_pairs={{0,3},{1,0},{2,1},{3,2},{4,7},{5,4},{6,5},{7,6},{8,11},{9,8},{10,9... | collective-permute-start | bytes 1769480 | tf_op jit(solution)/shard_map/ppermute | solution.py:398
  65.6 2.6 %conv.2 = bf16[128,768]{1,0:T(8,128)(2,1)S(1)} custom-call(s32[2]{0:T(128)S(1)} %copy-done.1, bf16[320,768]{1,0:T(8,128)(2,1)S(1)} %get-tuple-element.44.normed, bf16[320,768]{1,0:T(8,128)(2,1)S(1)} %get-tuple-element.43.first, bf16[768,1152]{1,0:T(8,128)(2,1)S(1)} %get-tuple-element.39.mine, bf16[768,1152]{1,0:T(8,128)(2,1)S(1)} %collective-permute-done.10.other, ...), custom_call_target="tpu_custom_call" | custom-call | flops 1000000000 | bytes 6000000 | tf_op jit(solution)/shard_map/conv/pallas_call | solution.py:58
  68.3 3.0 %collective-permute-start.11 = (bf16[128,768]{1,0:T(8,128)(2,1)S(1)}, bf16[128,768]{1,0:T(8,128)(2,1)S(1)}, u32[]{:S(2)}, u32[]{:S(2)}) collective-permute-start(bf16[128,768]{1,0:T(8,128)(2,1)S(1)} %conv.2), channel_id=1, source_target_pairs={{0,4},{1,5},{2,6},{3,7},{4,0},{5,1},{6,2},{7,3},{8,12},{9,13},{10,... | collective-permute-start | bytes 589832 | tf_op jit(solution)/shard_map/ppermute | solution.py:403
  71.3 2.6 %conv.3 = bf16[128,768]{1,0:T(8,128)(2,1)S(1)} custom-call(s32[2]{0:T(128)S(1)} %copy-done.1, bf16[320,768]{1,0:T(8,128)(2,1)S(1)} %get-tuple-element.44.normed, bf16[320,768]{1,0:T(8,128)(2,1)S(1)} %get-tuple-element.43.first, bf16[768,1152]{1,0:T(8,128)(2,1)S(1)} %get-tuple-element.39.mine, bf16[768,1152]{1,0:T(8,128)(2,1)S(1)} %collective-permute-done.10.other, ...), custom_call_target="tpu_custom_call" | custom-call | flops 1000000000 | bytes 6000000 | tf_op jit(solution)/shard_map/conv/pallas_call | solution.py:58
  73.9 1.7 %collective-permute-done.11 = bf16[128,768]{1,0:T(8,128)(2,1)S(1)} collective-permute-done((bf16[128,768]{1,0:T(8,128)(2,1)S(1)}, bf16[128,768]{1,0:T(8,128)(2,1)S(1)}, u32[]{:S(2)}, u32[]{:S(2)}) %collective-permute-start.11) | collective-permute-done | bytes 196640 | tf_op jit(solution)/shard_map/ppermute | solution.py:403
  76.4 5.1 %all-to-all-start.1 = ((bf16[16,16,768]{2,1,0:T(8,128)(2,1)}), bf16[16,16,768]{2,1,0:T(8,128)(2,1)S(1)}, u32[]{:S(2)}, u32[]{:S(2)}) async-start(bf16[16,16,768]{2,1,0:T(8,128)(2,1)} %bitcast.6), calls=%async_computation.1 | async-start | bytes 786432 | tf_op jit(solution)/shard_map/all_to_all | solution.py:409
  82.0 9.0 %collective-permute-start.17 = (bf16[768,384]{1,0:T(8,128)(2,1)S(1)}, bf16[768,384]{1,0:T(8,128)(2,1)}, u32[]{:S(2)}, u32[]{:S(2)}) collective-permute-start(bf16[768,384]{1,0:T(8,128)(2,1)S(1)} %collective-permute-done.13.refs_2_), channel_id=1, source_target_pairs={{0,8},{8,0},{16,24},{24,16},{32,40},{40,32},{48,56},{56,48},{64,72... | collective-permute-start | bytes 1769480 | tf_op jit(solution)/shard_map/ppermute | solution.py:405
  93.7 2.3 %all-to-all-done.1 = bf16[16,16,768]{2,1,0:T(8,128)(2,1)S(1)} async-done(((bf16[16,16,768]{2,1,0:T(8,128)(2,1)}), bf16[16,16,768]{2,1,0:T(8,128)(2,1)S(1)}, u32[]{:S(2)}, u32[]{:S(2)}) %all-to-all-start.1) | async-done | bytes 393248 | tf_op jit(solution)/shard_map/all_to_all | solution.py:409
  96.1 5.6 %merge.1 = bf16[256,768]{1,0:T(8,128)(2,1)} custom-call(s32[1,256]{1,0:T(1,128)S(1)} %broadcast_in_dim_reshape.3.live, bf16[256,768]{1,0:T(8,128)(2,1)S(1)} %bitcast.17, f32[3,768]{1,0:T(4,128)S(1)} %copy-done.3, bf16[768,384]{1,0:T(8,128)(2,1)S(1)} %get-tuple-element.46.refs_0_, bf16[768,384]{1,0:T(8,128)(2,1)S(1)} %collective-permute-done.12.refs_1_, ...), custom_call_target="tpu_custom_call" | custom-call | flops 2000000000 | bytes 8000000 | tf_op jit(solution)/shard_map/merge/pallas_call | solution.py:58
  101.6 3.5 %all-to-all-start.2 = ((bf16[16,16,768]{2,1,0:T(8,128)(2,1)}), bf16[16,16,768]{2,1,0:T(8,128)(2,1)S(1)}, u32[]{:S(2)}, u32[]{:S(2)}) async-start(bf16[16,16,768]{2,1,0:T(8,128)(2,1)} %bitcast.8), calls=%async_computation.2 | async-start | bytes 786432 | tf_op jit(solution)/shard_map/all_to_all | solution.py:415
  105.1 14.0 %all-to-all-done.2 = bf16[16,16,768]{2,1,0:T(8,128)(2,1)S(1)} async-done(((bf16[16,16,768]{2,1,0:T(8,128)(2,1)}), bf16[16,16,768]{2,1,0:T(8,128)(2,1)S(1)}, u32[]{:S(2)}, u32[]{:S(2)}) %all-to-all-start.2) | async-done | bytes 393248 | tf_op jit(solution)/shard_map/all_to_all | solution.py:415
  (52 shorter events, 12.1 us)
Async XLA Ops:
  0.0 91.9 %copy-start = (s32[2,16]{1,0:T(2,128)S(1)}, s32[2,16]{1,0:T(2,128)}, u32[]{:S(2)}) copy-start(s32[2,16]{1,0:T(2,128)} %param.13) | copy-start | bytes 388
  2.5 8.7 %collective-permute-start = (bf16[24,3072]{1,0:T(8,128)(2,1)}, bf16[24,3072]{1,0:T(8,128)(2,1)S(1)}, u32[]{:S(2)}, u32[]{:S(2)}) collective-permute-start(bf16[24,3072]{1,0:T(8,128)(2,1)} %get-tuple-element.33), channel_id=1, source_target_pairs={{0,128},{128,0},{1,129},{129,1},{2,130},{130,2},{3,131},{131,3},{4... | collective-permute-start | bytes 442376 | tf_op jit(solution)/shard_map/ppermute | solution.py:339
  4.7 29.4 %all-to-all-start = ((bf16[8,128,768]{2,1,0:T(8,128)(2,1)}), bf16[8,128,768]{2,1,0:T(8,128)(2,1)S(1)}, u32[]{:S(2)}, u32[]{:S(2)}) async-start(bf16[8,128,768]{2,1,0:T(8,128)(2,1)} %get-tuple-element.26), calls=%async_computation | async-start | bytes 3145728 | tf_op jit(solution)/shard_map/all_to_all | solution.py:382
  11.2 28.5 %copy-start.3 = (f32[3,768]{1,0:T(4,128)S(1)}, f32[3,768]{1,0:T(4,128)}, u32[]{:S(2)}) copy-start(f32[3,768]{1,0:T(4,128)} %gains.5) | copy-start | bytes 27652
  11.3 2.3 %collective-permute-start.1 = (bf16[2,24,1536]{2,1,0:T(8,128)(2,1)S(1)}, bf16[2,24,1536]{2,1,0:T(8,128)(2,1)S(1)}, u32[]{:S(2)}, u32[]{:S(2)}) collective-permute-start(bf16[2,24,1536]{2,1,0:T(8,128)(2,1)S(1)} %get-tuple-element.48), channel_id=1, source_target_pairs={{0,8},{8,0},{16,24},{24,16},{32,40},{40,32},{48,56},{56,48},{64,72... | collective-permute-start | bytes 442376 | tf_op jit(solution)/shard_map/ppermute | solution.py:344
  13.7 11.7 %collective-permute-start.3 = (bf16[96,1536]{1,0:T(8,128)(2,1)S(1)}, bf16[96,1536]{1,0:T(8,128)(2,1)S(1)}, u32[]{:S(2)}, u32[]{:S(2)}) collective-permute-start(bf16[96,1536]{1,0:T(8,128)(2,1)S(1)} %bitcast.14), channel_id=1, source_target_pairs={{0,112},{8,120},{16,0},{24,8},{32,16},{40,24},{48,32},{56,40},{64,... | collective-permute-start | bytes 884744 | tf_op jit(solution)/shard_map/ppermute | solution.py:359
  19.4 9.4 %collective-permute-start.2 = (bf16[96,1536]{1,0:T(8,128)(2,1)S(1)}, bf16[96,1536]{1,0:T(8,128)(2,1)S(1)}, u32[]{:S(2)}, u32[]{:S(2)}) collective-permute-start(bf16[96,1536]{1,0:T(8,128)(2,1)S(1)} %bitcast.15), channel_id=1, source_target_pairs={{0,16},{8,24},{16,32},{24,40},{32,48},{40,56},{48,64},{56,72},{64,... | collective-permute-start | bytes 884744 | tf_op jit(solution)/shard_map/ppermute | solution.py:358
  25.4 8.5 %collective-permute-start.5 = (bf16[96,1536]{1,0:T(8,128)(2,1)S(1)}, bf16[96,1536]{1,0:T(8,128)(2,1)S(1)}, u32[]{:S(2)}, u32[]{:S(2)}) collective-permute-start(bf16[96,1536]{1,0:T(8,128)(2,1)S(1)} %collective-permute-done.3.refs_2_), channel_id=1, source_target_pairs={{0,112},{8,120},{16,0},{24,8},{32,16},{40,24},{48,32},{56,40},{64,... | collective-permute-start | bytes 884744 | tf_op jit(solution)/shard_map/ppermute | solution.py:359
  28.8 10.9 %collective-permute-start.4 = (bf16[96,1536]{1,0:T(8,128)(2,1)S(1)}, bf16[96,1536]{1,0:T(8,128)(2,1)S(1)}, u32[]{:S(2)}, u32[]{:S(2)}) collective-permute-start(bf16[96,1536]{1,0:T(8,128)(2,1)S(1)} %collective-permute-done.2.refs_1_), channel_id=1, source_target_pairs={{0,16},{8,24},{16,32},{24,40},{32,48},{40,56},{48,64},{56,72},{64,... | collective-permute-start | bytes 884744 | tf_op jit(solution)/shard_map/ppermute | solution.py:358
  34.1 12.0 %collective-permute-start.7 = (bf16[96,1536]{1,0:T(8,128)(2,1)S(1)}, bf16[96,1536]{1,0:T(8,128)(2,1)S(1)}, u32[]{:S(2)}, u32[]{:S(2)}) collective-permute-start(bf16[96,1536]{1,0:T(8,128)(2,1)S(1)} %collective-permute-done.5.refs_4_), channel_id=1, source_target_pairs={{0,112},{8,120},{16,0},{24,8},{32,16},{40,24},{48,32},{56,40},{64,... | collective-permute-start | bytes 884744 | tf_op jit(solution)/shard_map/ppermute | solution.py:359
  39.7 9.2 %collective-permute-start.6 = (bf16[96,1536]{1,0:T(8,128)(2,1)S(1)}, bf16[96,1536]{1,0:T(8,128)(2,1)S(1)}, u32[]{:S(2)}, u32[]{:S(2)}) collective-permute-start(bf16[96,1536]{1,0:T(8,128)(2,1)S(1)} %collective-permute-done.4.refs_3_), channel_id=1, source_target_pairs={{0,16},{8,24},{16,32},{24,40},{32,48},{40,56},{48,64},{56,72},{64,... | collective-permute-start | bytes 884744 | tf_op jit(solution)/shard_map/ppermute | solution.py:358
  46.2 6.7 %collective-permute-start.9 = (bf16[48,1536]{1,0:T(8,128)(2,1)S(1)}, bf16[48,1536]{1,0:T(8,128)(2,1)S(1)}, u32[]{:S(2)}, u32[]{:S(2)}) collective-permute-start(bf16[48,1536]{1,0:T(8,128)(2,1)S(1)} %slice.21), channel_id=1, source_target_pairs={{0,112},{8,120},{16,0},{24,8},{32,16},{40,24},{48,32},{56,40},{64,... | collective-permute-start | bytes 442376 | tf_op jit(solution)/shard_map/ppermute | solution.py:359
  48.9 5.5 %collective-permute-start.8 = (bf16[48,1536]{1,0:T(8,128)(2,1)S(1)}, bf16[48,1536]{1,0:T(8,128)(2,1)S(1)}, u32[]{:S(2)}, u32[]{:S(2)}) collective-permute-start(bf16[48,1536]{1,0:T(8,128)(2,1)S(1)} %slice.20), channel_id=1, source_target_pairs={{0,16},{8,24},{16,32},{24,40},{32,48},{40,56},{48,64},{56,72},{64,... | collective-permute-start | bytes 442376 | tf_op jit(solution)/shard_map/ppermute | solution.py:358
  54.6 11.0 %collective-permute-start.10 = (bf16[768,1152]{1,0:T(8,128)(2,1)S(1)}, bf16[768,1152]{1,0:T(8,128)(2,1)S(1)}, u32[]{:S(2)}, u32[]{:S(2)}) collective-permute-start(bf16[768,1152]{1,0:T(8,128)(2,1)S(1)} %get-tuple-element.39.mine), channel_id=1, source_target_pairs={{0,8},{8,0},{16,24},{24,16},{32,40},{40,32},{48,56},{56,48},{64,72... | collective-permute-start | bytes 5308424 | tf_op jit(solution)/shard_map/ppermute | solution.py:392
  62.0 19.8 %collective-permute-start.12 = (bf16[768,384]{1,0:T(8,128)(2,1)S(1)}, bf16[768,384]{1,0:T(8,128)(2,1)S(1)}, u32[]{:S(2)}, u32[]{:S(2)}) collective-permute-start(bf16[768,384]{1,0:T(8,128)(2,1)S(1)} %get-tuple-element.46.refs_0_), channel_id=1, source_target_pairs={{0,1},{1,2},{2,3},{3,0},{4,5},{5,6},{6,7},{7,4},{8,9},{9,10},{10,1... | collective-permute-start | bytes 1769480 | tf_op jit(solution)/shard_map/ppermute | solution.py:398
  62.6 19.4 %collective-permute-start.13 = (bf16[768,384]{1,0:T(8,128)(2,1)S(1)}, bf16[768,384]{1,0:T(8,128)(2,1)S(1)}, u32[]{:S(2)}, u32[]{:S(2)}) collective-permute-start(bf16[768,384]{1,0:T(8,128)(2,1)S(1)} %get-tuple-element.46.refs_0_), channel_id=1, source_target_pairs={{0,3},{1,0},{2,1},{3,2},{4,7},{5,4},{6,5},{7,6},{8,11},{9,8},{10,9... | collective-permute-start | bytes 1769480 | tf_op jit(solution)/shard_map/ppermute | solution.py:398
  64.8 26.3 %collective-permute-start.14 = (bf16[768,384]{1,0:T(8,128)(2,1)S(1)}, bf16[768,384]{1,0:T(8,128)(2,1)S(1)}, u32[]{:S(2)}, u32[]{:S(2)}) collective-permute-start(bf16[768,384]{1,0:T(8,128)(2,1)S(1)} %get-tuple-element.46.refs_0_), channel_id=1, source_target_pairs={{0,2},{1,3},{2,0},{3,1},{4,6},{5,7},{6,4},{7,5},{8,10},{9,11},{10,... | collective-permute-start | bytes 1769480 | tf_op jit(solution)/shard_map/ppermute | solution.py:398
  68.3 7.4 %collective-permute-start.11 = (bf16[128,768]{1,0:T(8,128)(2,1)S(1)}, bf16[128,768]{1,0:T(8,128)(2,1)S(1)}, u32[]{:S(2)}, u32[]{:S(2)}) collective-permute-start(bf16[128,768]{1,0:T(8,128)(2,1)S(1)} %conv.2), channel_id=1, source_target_pairs={{0,4},{1,5},{2,6},{3,7},{4,0},{5,1},{6,2},{7,3},{8,12},{9,13},{10,... | collective-permute-start | bytes 589832 | tf_op jit(solution)/shard_map/ppermute | solution.py:403
  76.4 19.6 %all-to-all-start.1 = ((bf16[16,16,768]{2,1,0:T(8,128)(2,1)}), bf16[16,16,768]{2,1,0:T(8,128)(2,1)S(1)}, u32[]{:S(2)}, u32[]{:S(2)}) async-start(bf16[16,16,768]{2,1,0:T(8,128)(2,1)} %bitcast.6), calls=%async_computation.1 | async-start | bytes 786432 | tf_op jit(solution)/shard_map/all_to_all | solution.py:409
  81.5 10.6 %collective-permute-start.15 = (bf16[768,384]{1,0:T(8,128)(2,1)S(1)}, bf16[768,384]{1,0:T(8,128)(2,1)S(1)}, u32[]{:S(2)}, u32[]{:S(2)}) collective-permute-start(bf16[768,384]{1,0:T(8,128)(2,1)S(1)} %get-tuple-element.46.refs_0_), channel_id=1, source_target_pairs={{0,8},{8,0},{16,24},{24,16},{32,40},{40,32},{48,56},{56,48},{64,72... | collective-permute-start | bytes 1769480 | tf_op jit(solution)/shard_map/ppermute | solution.py:405
  81.8 10.3 %collective-permute-start.16 = (bf16[768,384]{1,0:T(8,128)(2,1)S(1)}, bf16[768,384]{1,0:T(8,128)(2,1)}, u32[]{:S(2)}, u32[]{:S(2)}) collective-permute-start(bf16[768,384]{1,0:T(8,128)(2,1)S(1)} %collective-permute-done.12.refs_1_), channel_id=1, source_target_pairs={{0,8},{8,0},{16,24},{24,16},{32,40},{40,32},{48,56},{56,48},{64,72... | collective-permute-start | bytes 1769480 | tf_op jit(solution)/shard_map/ppermute | solution.py:405
  82.0 10.8 %collective-permute-start.17 = (bf16[768,384]{1,0:T(8,128)(2,1)S(1)}, bf16[768,384]{1,0:T(8,128)(2,1)}, u32[]{:S(2)}, u32[]{:S(2)}) collective-permute-start(bf16[768,384]{1,0:T(8,128)(2,1)S(1)} %collective-permute-done.13.refs_2_), channel_id=1, source_target_pairs={{0,8},{8,0},{16,24},{24,16},{32,40},{40,32},{48,56},{56,48},{64,72... | collective-permute-start | bytes 1769480 | tf_op jit(solution)/shard_map/ppermute | solution.py:405
  91.1 2.6 %collective-permute-start.18 = (bf16[768,384]{1,0:T(8,128)(2,1)S(1)}, bf16[768,384]{1,0:T(8,128)(2,1)}, u32[]{:S(2)}, u32[]{:S(2)}) collective-permute-start(bf16[768,384]{1,0:T(8,128)(2,1)S(1)} %collective-permute-done.14.refs_3_), channel_id=1, source_target_pairs={{0,8},{8,0},{16,24},{24,16},{32,40},{40,32},{48,56},{56,48},{64,72... | collective-permute-start | bytes 1769480 | tf_op jit(solution)/shard_map/ppermute | solution.py:405
  101.6 17.5 %all-to-all-start.2 = ((bf16[16,16,768]{2,1,0:T(8,128)(2,1)}), bf16[16,16,768]{2,1,0:T(8,128)(2,1)S(1)}, u32[]{:S(2)}, u32[]{:S(2)}) async-start(bf16[16,16,768]{2,1,0:T(8,128)(2,1)} %bitcast.8), calls=%async_computation.2 | async-start | bytes 786432 | tf_op jit(solution)/shard_map/all_to_all | solution.py:415
  (4 other events, 44.3 us)

commit v5 on v4

--- a/solution.py
+++ b/solution.py
@@ -129,15 +129,19 @@
     return lengths[lax.axis_index("tm") // ROWS]
 
 
+PARTS = (2, 3, 1)
+
+
 def attend_pairs(length, norm_s, query_s, weights, context_ref):
     allowed = lax.broadcasted_iota(jnp.int32, (1, FRAMES), 1) < length
-    query_two = mm(query_s[...], weights[:, :256]).astype(jnp.bfloat16) * jnp.bfloat16(0.125)
-    both = mm(norm_s[...], weights[:, 256:]).astype(jnp.bfloat16)
-    for n in range(2):
+    width = weights.shape[1] // 3
+    queries = mm(query_s[...], weights[:, :width]).astype(jnp.bfloat16) * jnp.bfloat16(0.125)
+    both = mm(norm_s[...], weights[:, width:]).astype(jnp.bfloat16)
+    for n in range(width // 128):
         lanes = slice(n * 128, (n + 1) * 128)
-        key, value = both[:, :256][:, lanes], both[:, 256:][:, lanes]
+        key, value = both[:, lanes], both[:, width + n * 128 : width + (n + 1) * 128]
         value_ones = jnp.concatenate([value, jnp.ones_like(value)], axis=1)
-        context_ref[:, lanes] = pair_attention(query_two[:, lanes], key, value_ones, allowed)
+        context_ref[:, lanes] = pair_attention(queries[:, lanes], key, value_ones, allowed)
 
 
 def attend_a_kernel(
@@ -147,8 +151,9 @@
     copies = []
     for n, group in enumerate((group_a, group_b, group_c)):
         for m in range(3):
-            columns = pl.ds(m * D + n * 256, 256)
-            copies.append((qkv.at[:, columns], group.at[:, pl.ds(m * 256, 256)]))
+            width = PARTS[n] * 128
+            columns = pl.ds(m * D + sum(PARTS[:n]) * 128, width)
+            copies.append((qkv.at[:, columns], group.at[:, pl.ds(m * width, width)]))
     copies.append((wout, wout_ref))
     copies = [pltpu.make_async_copy(a, b, sems.at[n]) for n, (a, b) in enumerate(copies)]
     for copy in copies:
@@ -183,9 +188,8 @@
     first_ref, normed_ref, context_c,
 ):
     attend_pairs(my_length(lengths), norm_s, query_s, weights, context_c)
-    third = D // 3
     out = sum(
-        mm(c[...], wout[n * third : (n + 1) * third])
+        mm(c[...], wout[sum(PARTS[:n]) * 128 : sum(PARTS[: n + 1]) * 128])
         for n, c in enumerate((context_a, context_b, context_c))
     )
     first = (raw_s[...].astype(jnp.float32) + out).astype(jnp.bfloat16)
@@ -198,25 +202,25 @@
 
 
 def run_attend_a(lengths, blocks, gains, qkv, wout):
-    group = bf16(D, D)
+    group_a, group_b, group_c = ((D, n * 384) for n in PARTS)
     return call(
         attend_a_kernel,
-        [bf16(WIDE, D // 3), bf16(FRAMES, D), bf16(WIDE, D), bf16(WIDE, D), group, group, group],
-        [pltpu.VMEM((D, D), jnp.bfloat16), pltpu.SemaphoreType.DMA((10,))],
+        [bf16(WIDE, D // 3), bf16(FRAMES, D), bf16(WIDE, D), bf16(WIDE, D), bf16(*group_b), bf16(*group_c), bf16(D, D)],
+        [pltpu.VMEM(group_a, jnp.bfloat16), pltpu.SemaphoreType.DMA((10,))],
         ATTEND_COST, "attend_a", [blocks, gains, Far(qkv), Far(wout)], lengths, limit=44,
     )
 
 
 def run_attend_b(lengths, norm, query, weights):
     (context,) = call(
-        attend_b_kernel, [bf16(WIDE, D // 3)], [], ATTEND_COST, "attend_b", [norm, query, weights], lengths,
+        attend_b_kernel, [bf16(WIDE, PARTS[1] * 128)], [], ATTEND_COST, "attend_b", [norm, query, weights], lengths,
     )
     return context
 
 
 def run_attend_c(lengths, *operands):
     return call(
-        attend_c_kernel, [bf16(WIDE, D)] * 2, [pltpu.VMEM((WIDE, D // 3), jnp.bfloat16)],
+        attend_c_kernel, [bf16(WIDE, D)] * 2, [pltpu.VMEM((WIDE, PARTS[2] * 128), jnp.bfloat16)],
         ATTEND_COST, "attend_c", list(operands), lengths,
     )
 

time: 120 us -> 121 us (level)
  starting transfers between devices: 56.1 us -> 53.3 us
  waiting for transfers between devices: 33.6 us -> 36.3 us
    ppermute x4, waiting for transfers between devices: 1.5 us -> 13.3 us  [step(): lax.ppermute(after(high, *others) if others else high, 'chan', self.up)]
    ppermute x4, waiting for transfers between devices: 11.1 us -> 0.01 us  [step(): lax.ppermute(after(low, *others) if others else low, 'chan', self.down)]
    ppermute x4, starting transfers between devices: 17.4 us -> 13.6 us  [step(): lax.ppermute(after(low, *others) if others else low, 'chan', self.down)]
    ppermute x4, starting transfers between devices: 10.3 us -> 8.07 us  [shards(): eighths = held + [lax.ppermute(one, 'chan', point.swap) for one in held]]
    ppermute x4, starting transfers between devices: 0.27 us -> 2.24 us  [step(): lax.ppermute(after(high, *others) if others else high, 'chan', self.up)]
    all_to_all x1, waiting for transfers between devices: 2.34 us -> 4.26 us  [shards(): lax.all_to_all(second.reshape(channels, part, D), 'chan', split_axis=0, c...]
    all_to_all x1, starting transfers between devices: 5.1 us -> 7.01 us  [shards(): lax.all_to_all(second.reshape(channels, part, D), 'chan', split_axis=0, c...]
  transfers between devices with their start and end apart: 22 -> 22, of which waited for: 11 -> 10; matrix products, arithmetic and copies ran while one was open for 1% -> 1% of each run, Pallas kernels for 15% -> 16%
where the time goes in v5:
time: 121 us; the launch traced here: 120 us
  starting transfers between devices  53.3 us (44%)
  waiting for transfers between devices  36.3 us (30%)
  Pallas kernels  27.3 us (23%)
  other arithmetic  1.68 us (1%)
  local copies, waits for them, and re-layouts  1.5 us (1%)
    pallas_call x8, Pallas kernels, call(): pl.pallas_call(kernel, in_specs=[pl.BlockSpec(memory_space=pltpu.SMEM)] *...  27.3 us
    all_to_all x1, waiting for transfers between devices, shards(): lax.all_to_all(merged.reshape(channels, part, D), 'chan', split_axis=0, c...  14 us
    ppermute x4, starting transfers between devices, step(): lax.ppermute(after(low, *others) if others else low, 'chan', self.down)  13.6 us
    ppermute x4, waiting for transfers between devices, step(): lax.ppermute(after(high, *others) if others else high, 'chan', self.up)  13.3 us
    ppermute x4, starting transfers between devices, shards(): eighths = held + [lax.ppermute(one, 'chan', point.swap) for one in held]  8.07 us
    all_to_all x1, starting transfers between devices, shards(): lax.all_to_all(second.reshape(channels, part, D), 'chan', split_axis=0, c...  7.01 us
    all_to_all x1, starting transfers between devices, shards(): lax.all_to_all(spread, 'tm', split_axis=0, concat_axis=0, tiled=True)  6.49 us
    all_to_all x1, waiting for transfers between devices, shards(): lax.all_to_all(second.reshape(channels, part, D), 'chan', split_axis=0, c...  4.26 us
  transfers between devices with their start and end apart: 22, of which 10 were waited for; matrix products, arithmetic and copies ran while one was open for 1% of the time, Pallas kernels for 16%

profile of v5, /device:TPU:1, one launch (start us, length us, event | category | flops | bytes accessed | tf_op | source)
XLA Modules:
  0.0 120.3 jit_solution(9749112383710278176)
XLA Ops:
  0.0 2.5 %prepare.1 = (bf16[24,3072]{1,0:T(8,128)(2,1)}, bf16[8,128,768]{2,1,0:T(8,128)(2,1)}) custom-call(bf16[24,1536]{1,0:T(8,128)(2,1)} %pin.1, bf16[24,768]{1,0:T(8,128)(2,1)} %pout.1, bf16[24,2304]{1,0:T(8,128)(2,1)} %mqkv.1, bf16[24,768]{1,0:T(8,128)(2,1)} %mout.1, bf16[2,1,128,768]{3,2,1,0:T(8,128)(2,1)} %features.1), custom_call_target="tpu_custom_call" | custom-call | bytes 3000000 | tf_op jit(solution)/shard_map/prepare/pallas_call | solution.py:58
  2.5 2.2 %collective-permute-start = (bf16[24,3072]{1,0:T(8,128)(2,1)}, bf16[24,3072]{1,0:T(8,128)(2,1)S(1)}, u32[]{:S(2)}, u32[]{:S(2)}) collective-permute-start(bf16[24,3072]{1,0:T(8,128)(2,1)} %get-tuple-element.33), channel_id=1, source_target_pairs={{0,128},{128,0},{1,129},{129,1},{2,130},{130,2},{3,131},{131,3},{4... | collective-permute-start | bytes 442376 | tf_op jit(solution)/shard_map/ppermute | solution.py:343
  4.7 6.5 %all-to-all-start = ((bf16[8,128,768]{2,1,0:T(8,128)(2,1)}), bf16[8,128,768]{2,1,0:T(8,128)(2,1)S(1)}, u32[]{:S(2)}, u32[]{:S(2)}) async-start(bf16[8,128,768]{2,1,0:T(8,128)(2,1)} %get-tuple-element.26), calls=%async_computation | async-start | bytes 3145728 | tf_op jit(solution)/shard_map/all_to_all | solution.py:386
  15.4 4.0 %collective-permute-start.3 = (bf16[96,1536]{1,0:T(8,128)(2,1)S(1)}, bf16[96,1536]{1,0:T(8,128)(2,1)S(1)}, u32[]{:S(2)}, u32[]{:S(2)}) collective-permute-start(bf16[96,1536]{1,0:T(8,128)(2,1)S(1)} %bitcast.15), channel_id=1, source_target_pairs={{0,112},{8,120},{16,0},{24,8},{32,16},{40,24},{48,32},{56,40},{64,... | collective-permute-start | bytes 884744 | tf_op jit(solution)/shard_map/ppermute | solution.py:363
  19.4 7.0 %collective-permute-done.2.refs_1_ = bf16[96,1536]{1,0:T(8,128)(2,1)S(1)} collective-permute-done((bf16[96,1536]{1,0:T(8,128)(2,1)S(1)}, bf16[96,1536]{1,0:T(8,128)(2,1)S(1)}, u32[]{:S(2)}, u32[]{:S(2)}) %collective-permute-start.2) | collective-permute-done | bytes 294944 | tf_op jit(solution)/shard_map/ppermute | solution.py:362
  26.4 2.7 %collective-permute-start.5 = (bf16[96,1536]{1,0:T(8,128)(2,1)S(1)}, bf16[96,1536]{1,0:T(8,128)(2,1)S(1)}, u32[]{:S(2)}, u32[]{:S(2)}) collective-permute-start(bf16[96,1536]{1,0:T(8,128)(2,1)S(1)} %collective-permute-done.3.refs_2_), channel_id=1, source_target_pairs={{0,112},{8,120},{16,0},{24,8},{32,16},{40,24},{48,32},{56,40},{64,... | collective-permute-start | bytes 884744 | tf_op jit(solution)/shard_map/ppermute | solution.py:363
  29.1 6.2 %collective-permute-done.4.refs_3_ = bf16[96,1536]{1,0:T(8,128)(2,1)S(1)} collective-permute-done((bf16[96,1536]{1,0:T(8,128)(2,1)S(1)}, bf16[96,1536]{1,0:T(8,128)(2,1)S(1)}, u32[]{:S(2)}, u32[]{:S(2)}) %collective-permute-start.4) | collective-permute-done | bytes 294944 | tf_op jit(solution)/shard_map/ppermute | solution.py:362
  35.7 3.9 %collective-permute-start.7 = (bf16[96,1536]{1,0:T(8,128)(2,1)S(1)}, bf16[96,1536]{1,0:T(8,128)(2,1)S(1)}, u32[]{:S(2)}, u32[]{:S(2)}) collective-permute-start(bf16[96,1536]{1,0:T(8,128)(2,1)S(1)} %collective-permute-done.5.refs_4_), channel_id=1, source_target_pairs={{0,112},{8,120},{16,0},{24,8},{32,16},{40,24},{48,32},{56,40},{64,... | collective-permute-start | bytes 884744 | tf_op jit(solution)/shard_map/ppermute | solution.py:363
  41.0 5.2 %attend_a.1 = (bf16[320,256]{1,0:T(8,128)(2,1)S(1)}, bf16[1024,768]{1,0:T(8,128)(2,1)S(1)}, bf16[320,768]{1,0:T(8,128)(2,1)S(1)}, bf16[320,768]{1,0:T(8,128)(2,1...) custom-call(s32[2]{0:T(128)S(1)} %copy-done.1, ...), custom_call_target="tpu_custom_call" | custom-call | flops 3000000000 | bytes 5000000 | tf_op jit(solution)/shard_map/attend_a/pallas_call | solution.py:58
  46.3 2.9 %collective-permute-start.9 = (bf16[48,1536]{1,0:T(8,128)(2,1)S(1)}, bf16[48,1536]{1,0:T(8,128)(2,1)S(1)}, u32[]{:S(2)}, u32[]{:S(2)}) collective-permute-start(bf16[48,1536]{1,0:T(8,128)(2,1)S(1)} %slice.21), channel_id=1, source_target_pairs={{0,112},{8,120},{16,0},{24,8},{32,16},{40,24},{48,32},{56,40},{64,... | collective-permute-start | bytes 442376 | tf_op jit(solution)/shard_map/ppermute | solution.py:363
  49.3 5.1 %attend_b.1.context_b = bf16[320,384]{1,0:T(8,128)(2,1)S(1)} custom-call(s32[2]{0:T(128)S(1)} %copy-done.1, bf16[1024,768]{1,0:T(8,128)(2,1)S(1)} %get-tuple-element.27.norm_s, bf16[320,768]{1,0:T(8,128)(2,1)S(1)} %get-tuple-element.28.query_s, bf16[768,1152]{1,0:T(8,128)(2,1)S(1)} %get-tuple-element.31.weights), custom_call_target="tpu_custom_call" | custom-call | flops 3000000000 | bytes 5000000 | tf_op jit(solution)/shard_map/attend_b/pallas_call | solution.py:58
  54.6 2.1 %collective-permute-start.10 = (bf16[768,1152]{1,0:T(8,128)(2,1)S(1)}, bf16[768,1152]{1,0:T(8,128)(2,1)S(1)}, u32[]{:S(2)}, u32[]{:S(2)}) collective-permute-start(bf16[768,1152]{1,0:T(8,128)(2,1)S(1)} %get-tuple-element.39.mine), channel_id=1, source_target_pairs={{0,8},{8,0},{16,24},{24,16},{32,40},{40,32},{48,56},{56,48},{64,72... | collective-permute-start | bytes 5308424 | tf_op jit(solution)/shard_map/ppermute | solution.py:396
  56.7 3.5 %attend_c.1 = (bf16[320,768]{1,0:T(8,128)(2,1)S(1)}, bf16[320,768]{1,0:T(8,128)(2,1)S(1)}) custom-call(s32[2]{0:T(128)S(1)} %copy-done.1, bf16[1024,768]{1,0:T(8,128)(2,1)S(1)} %get-tuple-element.27.norm_s, bf16[320,768]{1,0:T(8,128)(2,1)S(1)} %get-tuple-element.28.query_s, bf16[320,768]{1,0:T(8,128)(2,1)S(1)} %get-tuple-element.29.raw_s, ...), custom_call_target="tpu_custom_call" | custom-call | flops 3000000000 | bytes 5000000 | tf_op jit(solution)/shard_map/attend_c/pallas_call | solution.py:58
  61.1 1.8 %collective-permute-start.13 = (bf16[768,384]{1,0:T(8,128)(2,1)S(1)}, bf16[768,384]{1,0:T(8,128)(2,1)S(1)}, u32[]{:S(2)}, u32[]{:S(2)}) collective-permute-start(bf16[768,384]{1,0:T(8,128)(2,1)S(1)} %get-tuple-element.46.refs_0_), channel_id=1, source_target_pairs={{0,3},{1,0},{2,1},{3,2},{4,7},{5,4},{6,5},{7,6},{8,11},{9,8},{10,9... | collective-permute-start | bytes 1769480 | tf_op jit(solution)/shard_map/ppermute | solution.py:402
  64.1 2.6 %conv.2 = bf16[128,768]{1,0:T(8,128)(2,1)S(1)} custom-call(s32[2]{0:T(128)S(1)} %copy-done.1, bf16[320,768]{1,0:T(8,128)(2,1)S(1)} %get-tuple-element.44.normed, bf16[320,768]{1,0:T(8,128)(2,1)S(1)} %get-tuple-element.43.first, bf16[768,1152]{1,0:T(8,128)(2,1)S(1)} %get-tuple-element.39.mine, bf16[768,1152]{1,0:T(8,128)(2,1)S(1)} %collective-permute-done.10.other, ...), custom_call_target="tpu_custom_call" | custom-call | flops 1000000000 | bytes 6000000 | tf_op jit(solution)/shard_map/conv/pallas_call | solution.py:58
  66.8 3.0 %collective-permute-start.11 = (bf16[128,768]{1,0:T(8,128)(2,1)S(1)}, bf16[128,768]{1,0:T(8,128)(2,1)S(1)}, u32[]{:S(2)}, u32[]{:S(2)}) collective-permute-start(bf16[128,768]{1,0:T(8,128)(2,1)S(1)} %conv.2), channel_id=1, source_target_pairs={{0,4},{1,5},{2,6},{3,7},{4,0},{5,1},{6,2},{7,3},{8,12},{9,13},{10,... | collective-permute-start | bytes 589832 | tf_op jit(solution)/shard_map/ppermute | solution.py:407
  69.8 2.6 %conv.3 = bf16[128,768]{1,0:T(8,128)(2,1)S(1)} custom-call(s32[2]{0:T(128)S(1)} %copy-done.1, bf16[320,768]{1,0:T(8,128)(2,1)S(1)} %get-tuple-element.44.normed, bf16[320,768]{1,0:T(8,128)(2,1)S(1)} %get-tuple-element.43.first, bf16[768,1152]{1,0:T(8,128)(2,1)S(1)} %get-tuple-element.39.mine, bf16[768,1152]{1,0:T(8,128)(2,1)S(1)} %collective-permute-done.10.other, ...), custom_call_target="tpu_custom_call" | custom-call | flops 1000000000 | bytes 6000000 | tf_op jit(solution)/shard_map/conv/pallas_call | solution.py:58
  72.4 1.8 %collective-permute-done.11 = bf16[128,768]{1,0:T(8,128)(2,1)S(1)} collective-permute-done((bf16[128,768]{1,0:T(8,128)(2,1)S(1)}, bf16[128,768]{1,0:T(8,128)(2,1)S(1)}, u32[]{:S(2)}, u32[]{:S(2)}) %collective-permute-start.11) | collective-permute-done | bytes 196640 | tf_op jit(solution)/shard_map/ppermute | solution.py:407
  74.9 7.0 %all-to-all-start.1 = ((bf16[16,16,768]{2,1,0:T(8,128)(2,1)}), bf16[16,16,768]{2,1,0:T(8,128)(2,1)S(1)}, u32[]{:S(2)}, u32[]{:S(2)}) async-start(bf16[16,16,768]{2,1,0:T(8,128)(2,1)} %bitcast.6), calls=%async_computation.1 | async-start | bytes 786432 | tf_op jit(solution)/shard_map/all_to_all | solution.py:413
  82.5 6.8 %collective-permute-start.17 = (bf16[768,384]{1,0:T(8,128)(2,1)S(1)}, bf16[768,384]{1,0:T(8,128)(2,1)}, u32[]{:S(2)}, u32[]{:S(2)}) collective-permute-start(bf16[768,384]{1,0:T(8,128)(2,1)S(1)} %collective-permute-done.13.refs_2_), channel_id=1, source_target_pairs={{0,8},{8,0},{16,24},{24,16},{32,40},{40,32},{48,56},{56,48},{64,72... | collective-permute-start | bytes 1769480 | tf_op jit(solution)/shard_map/ppermute | solution.py:409
  92.2 4.3 %all-to-all-done.1 = bf16[16,16,768]{2,1,0:T(8,128)(2,1)S(1)} async-done(((bf16[16,16,768]{2,1,0:T(8,128)(2,1)}), bf16[16,16,768]{2,1,0:T(8,128)(2,1)S(1)}, u32[]{:S(2)}, u32[]{:S(2)}) %all-to-all-start.1) | async-done | bytes 393248 | tf_op jit(solution)/shard_map/all_to_all | solution.py:413
  96.5 5.6 %merge.1 = bf16[256,768]{1,0:T(8,128)(2,1)} custom-call(s32[1,256]{1,0:T(1,128)S(1)} %broadcast_in_dim_reshape.3.live, bf16[256,768]{1,0:T(8,128)(2,1)S(1)} %bitcast.17, f32[3,768]{1,0:T(4,128)S(1)} %copy-done.3, bf16[768,384]{1,0:T(8,128)(2,1)S(1)} %get-tuple-element.46.refs_0_, bf16[768,384]{1,0:T(8,128)(2,1)S(1)} %collective-permute-done.12.refs_1_, ...), custom_call_target="tpu_custom_call" | custom-call | flops 2000000000 | bytes 8000000 | tf_op jit(solution)/shard_map/merge/pallas_call | solution.py:58
  102.1 3.5 %all-to-all-start.2 = ((bf16[16,16,768]{2,1,0:T(8,128)(2,1)}), bf16[16,16,768]{2,1,0:T(8,128)(2,1)S(1)}, u32[]{:S(2)}, u32[]{:S(2)}) async-start(bf16[16,16,768]{2,1,0:T(8,128)(2,1)} %bitcast.8), calls=%async_computation.2 | async-start | bytes 786432 | tf_op jit(solution)/shard_map/all_to_all | solution.py:419
  105.5 14.0 %all-to-all-done.2 = bf16[16,16,768]{2,1,0:T(8,128)(2,1)S(1)} async-done(((bf16[16,16,768]{2,1,0:T(8,128)(2,1)}), bf16[16,16,768]{2,1,0:T(8,128)(2,1)S(1)}, u32[]{:S(2)}, u32[]{:S(2)}) %all-to-all-start.2) | async-done | bytes 393248 | tf_op jit(solution)/shard_map/all_to_all | solution.py:419
  (52 shorter events, 13.5 us)
Async XLA Ops:
  0.0 90.5 %copy-start = (s32[2,16]{1,0:T(2,128)S(1)}, s32[2,16]{1,0:T(2,128)}, u32[]{:S(2)}) copy-start(s32[2,16]{1,0:T(2,128)} %param.13) | copy-start | bytes 388
  2.5 8.7 %collective-permute-start = (bf16[24,3072]{1,0:T(8,128)(2,1)}, bf16[24,3072]{1,0:T(8,128)(2,1)S(1)}, u32[]{:S(2)}, u32[]{:S(2)}) collective-permute-start(bf16[24,3072]{1,0:T(8,128)(2,1)} %get-tuple-element.33), channel_id=1, source_target_pairs={{0,128},{128,0},{1,129},{129,1},{2,130},{130,2},{3,131},{131,3},{4... | collective-permute-start | bytes 442376 | tf_op jit(solution)/shard_map/ppermute | solution.py:343
  4.7 30.6 %all-to-all-start = ((bf16[8,128,768]{2,1,0:T(8,128)(2,1)}), bf16[8,128,768]{2,1,0:T(8,128)(2,1)S(1)}, u32[]{:S(2)}, u32[]{:S(2)}) async-start(bf16[8,128,768]{2,1,0:T(8,128)(2,1)} %get-tuple-element.26), calls=%async_computation | async-start | bytes 3145728 | tf_op jit(solution)/shard_map/all_to_all | solution.py:386
  11.2 28.5 %copy-start.1 = (s32[2]{0:T(128)S(1)}, s32[2]{0:T(128)}, u32[]{:S(2)}) copy-start(s32[2]{0:T(128)} %lengths.9) | copy-start | bytes 28
  11.3 2.3 %collective-permute-start.1 = (bf16[2,24,1536]{2,1,0:T(8,128)(2,1)S(1)}, bf16[2,24,1536]{2,1,0:T(8,128)(2,1)S(1)}, u32[]{:S(2)}, u32[]{:S(2)}) collective-permute-start(bf16[2,24,1536]{2,1,0:T(8,128)(2,1)S(1)} %get-tuple-element.48), channel_id=1, source_target_pairs={{0,8},{8,0},{16,24},{24,16},{32,40},{40,32},{48,56},{56,48},{64,72... | collective-permute-start | bytes 442376 | tf_op jit(solution)/shard_map/ppermute | solution.py:348
  13.7 12.7 %collective-permute-start.2 = (bf16[96,1536]{1,0:T(8,128)(2,1)S(1)}, bf16[96,1536]{1,0:T(8,128)(2,1)S(1)}, u32[]{:S(2)}, u32[]{:S(2)}) collective-permute-start(bf16[96,1536]{1,0:T(8,128)(2,1)S(1)} %bitcast.14), channel_id=1, source_target_pairs={{0,16},{8,24},{16,32},{24,40},{32,48},{40,56},{48,64},{56,72},{64,... | collective-permute-start | bytes 884744 | tf_op jit(solution)/shard_map/ppermute | solution.py:362
  15.4 11.0 %collective-permute-start.3 = (bf16[96,1536]{1,0:T(8,128)(2,1)S(1)}, bf16[96,1536]{1,0:T(8,128)(2,1)S(1)}, u32[]{:S(2)}, u32[]{:S(2)}) collective-permute-start(bf16[96,1536]{1,0:T(8,128)(2,1)S(1)} %bitcast.15), channel_id=1, source_target_pairs={{0,112},{8,120},{16,0},{24,8},{32,16},{40,24},{48,32},{56,40},{64,... | collective-permute-start | bytes 884744 | tf_op jit(solution)/shard_map/ppermute | solution.py:363
  26.4 8.9 %collective-permute-start.4 = (bf16[96,1536]{1,0:T(8,128)(2,1)S(1)}, bf16[96,1536]{1,0:T(8,128)(2,1)S(1)}, u32[]{:S(2)}, u32[]{:S(2)}) collective-permute-start(bf16[96,1536]{1,0:T(8,128)(2,1)S(1)} %collective-permute-done.2.refs_1_), channel_id=1, source_target_pairs={{0,16},{8,24},{16,32},{24,40},{32,48},{40,56},{48,64},{56,72},{64,... | collective-permute-start | bytes 884744 | tf_op jit(solution)/shard_map/ppermute | solution.py:362
  26.4 9.3 %collective-permute-start.5 = (bf16[96,1536]{1,0:T(8,128)(2,1)S(1)}, bf16[96,1536]{1,0:T(8,128)(2,1)S(1)}, u32[]{:S(2)}, u32[]{:S(2)}) collective-permute-start(bf16[96,1536]{1,0:T(8,128)(2,1)S(1)} %collective-permute-done.3.refs_2_), channel_id=1, source_target_pairs={{0,112},{8,120},{16,0},{24,8},{32,16},{40,24},{48,32},{56,40},{64,... | collective-permute-start | bytes 884744 | tf_op jit(solution)/shard_map/ppermute | solution.py:363
  35.3 10.9 %collective-permute-start.6 = (bf16[96,1536]{1,0:T(8,128)(2,1)S(1)}, bf16[96,1536]{1,0:T(8,128)(2,1)S(1)}, u32[]{:S(2)}, u32[]{:S(2)}) collective-permute-start(bf16[96,1536]{1,0:T(8,128)(2,1)S(1)} %collective-permute-done.4.refs_3_), channel_id=1, source_target_pairs={{0,16},{8,24},{16,32},{24,40},{32,48},{40,56},{48,64},{56,72},{64,... | collective-permute-start | bytes 884744 | tf_op jit(solution)/shard_map/ppermute | solution.py:362
  35.7 10.6 %collective-permute-start.7 = (bf16[96,1536]{1,0:T(8,128)(2,1)S(1)}, bf16[96,1536]{1,0:T(8,128)(2,1)S(1)}, u32[]{:S(2)}, u32[]{:S(2)}) collective-permute-start(bf16[96,1536]{1,0:T(8,128)(2,1)S(1)} %collective-permute-done.5.refs_4_), channel_id=1, source_target_pairs={{0,112},{8,120},{16,0},{24,8},{32,16},{40,24},{48,32},{56,40},{64,... | collective-permute-start | bytes 884744 | tf_op jit(solution)/shard_map/ppermute | solution.py:363
  46.2 8.2 %collective-permute-start.8 = (bf16[48,1536]{1,0:T(8,128)(2,1)S(1)}, bf16[48,1536]{1,0:T(8,128)(2,1)S(1)}, u32[]{:S(2)}, u32[]{:S(2)}) collective-permute-start(bf16[48,1536]{1,0:T(8,128)(2,1)S(1)} %slice.20), channel_id=1, source_target_pairs={{0,16},{8,24},{16,32},{24,40},{32,48},{40,56},{48,64},{56,72},{64,... | collective-permute-start | bytes 442376 | tf_op jit(solution)/shard_map/ppermute | solution.py:362
  46.3 8.1 %collective-permute-start.9 = (bf16[48,1536]{1,0:T(8,128)(2,1)S(1)}, bf16[48,1536]{1,0:T(8,128)(2,1)S(1)}, u32[]{:S(2)}, u32[]{:S(2)}) collective-permute-start(bf16[48,1536]{1,0:T(8,128)(2,1)S(1)} %slice.21), channel_id=1, source_target_pairs={{0,112},{8,120},{16,0},{24,8},{32,16},{40,24},{48,32},{56,40},{64,... | collective-permute-start | bytes 442376 | tf_op jit(solution)/shard_map/ppermute | solution.py:363
  54.6 9.5 %collective-permute-start.10 = (bf16[768,1152]{1,0:T(8,128)(2,1)S(1)}, bf16[768,1152]{1,0:T(8,128)(2,1)S(1)}, u32[]{:S(2)}, u32[]{:S(2)}) collective-permute-start(bf16[768,1152]{1,0:T(8,128)(2,1)S(1)} %get-tuple-element.39.mine), channel_id=1, source_target_pairs={{0,8},{8,0},{16,24},{24,16},{32,40},{40,32},{48,56},{56,48},{64,72... | collective-permute-start | bytes 5308424 | tf_op jit(solution)/shard_map/ppermute | solution.py:396
  60.2 21.9 %collective-permute-start.12 = (bf16[768,384]{1,0:T(8,128)(2,1)S(1)}, bf16[768,384]{1,0:T(8,128)(2,1)S(1)}, u32[]{:S(2)}, u32[]{:S(2)}) collective-permute-start(bf16[768,384]{1,0:T(8,128)(2,1)S(1)} %get-tuple-element.46.refs_0_), channel_id=1, source_target_pairs={{0,1},{1,2},{2,3},{3,0},{4,5},{5,6},{6,7},{7,4},{8,9},{9,10},{10,1... | collective-permute-start | bytes 1769480 | tf_op jit(solution)/shard_map/ppermute | solution.py:402
  61.1 21.3 %collective-permute-start.13 = (bf16[768,384]{1,0:T(8,128)(2,1)S(1)}, bf16[768,384]{1,0:T(8,128)(2,1)S(1)}, u32[]{:S(2)}, u32[]{:S(2)}) collective-permute-start(bf16[768,384]{1,0:T(8,128)(2,1)S(1)} %get-tuple-element.46.refs_0_), channel_id=1, source_target_pairs={{0,3},{1,0},{2,1},{3,2},{4,7},{5,4},{6,5},{7,6},{8,11},{9,8},{10,9... | collective-permute-start | bytes 1769480 | tf_op jit(solution)/shard_map/ppermute | solution.py:402
  63.0 26.7 %collective-permute-start.14 = (bf16[768,384]{1,0:T(8,128)(2,1)S(1)}, bf16[768,384]{1,0:T(8,128)(2,1)S(1)}, u32[]{:S(2)}, u32[]{:S(2)}) collective-permute-start(bf16[768,384]{1,0:T(8,128)(2,1)S(1)} %get-tuple-element.46.refs_0_), channel_id=1, source_target_pairs={{0,2},{1,3},{2,0},{3,1},{4,6},{5,7},{6,4},{7,5},{8,10},{9,11},{10,... | collective-permute-start | bytes 1769480 | tf_op jit(solution)/shard_map/ppermute | solution.py:402
  66.8 7.4 %collective-permute-start.11 = (bf16[128,768]{1,0:T(8,128)(2,1)S(1)}, bf16[128,768]{1,0:T(8,128)(2,1)S(1)}, u32[]{:S(2)}, u32[]{:S(2)}) collective-permute-start(bf16[128,768]{1,0:T(8,128)(2,1)S(1)} %conv.2), channel_id=1, source_target_pairs={{0,4},{1,5},{2,6},{3,7},{4,0},{5,1},{6,2},{7,3},{8,12},{9,13},{10,... | collective-permute-start | bytes 589832 | tf_op jit(solution)/shard_map/ppermute | solution.py:407
  74.9 21.6 %all-to-all-start.1 = ((bf16[16,16,768]{2,1,0:T(8,128)(2,1)}), bf16[16,16,768]{2,1,0:T(8,128)(2,1)S(1)}, u32[]{:S(2)}, u32[]{:S(2)}) async-start(bf16[16,16,768]{2,1,0:T(8,128)(2,1)} %bitcast.6), calls=%async_computation.1 | async-start | bytes 786432 | tf_op jit(solution)/shard_map/all_to_all | solution.py:413
  81.9 8.7 %collective-permute-start.15 = (bf16[768,384]{1,0:T(8,128)(2,1)S(1)}, bf16[768,384]{1,0:T(8,128)(2,1)S(1)}, u32[]{:S(2)}, u32[]{:S(2)}) collective-permute-start(bf16[768,384]{1,0:T(8,128)(2,1)S(1)} %get-tuple-element.46.refs_0_), channel_id=1, source_target_pairs={{0,8},{8,0},{16,24},{24,16},{32,40},{40,32},{48,56},{56,48},{64,72... | collective-permute-start | bytes 1769480 | tf_op jit(solution)/shard_map/ppermute | solution.py:409
  82.1 8.5 %collective-permute-start.16 = (bf16[768,384]{1,0:T(8,128)(2,1)S(1)}, bf16[768,384]{1,0:T(8,128)(2,1)}, u32[]{:S(2)}, u32[]{:S(2)}) collective-permute-start(bf16[768,384]{1,0:T(8,128)(2,1)S(1)} %collective-permute-done.12.refs_1_), channel_id=1, source_target_pairs={{0,8},{8,0},{16,24},{24,16},{32,40},{40,32},{48,56},{56,48},{64,72... | collective-permute-start | bytes 1769480 | tf_op jit(solution)/shard_map/ppermute | solution.py:409
  82.5 8.5 %collective-permute-start.17 = (bf16[768,384]{1,0:T(8,128)(2,1)S(1)}, bf16[768,384]{1,0:T(8,128)(2,1)}, u32[]{:S(2)}, u32[]{:S(2)}) collective-permute-start(bf16[768,384]{1,0:T(8,128)(2,1)S(1)} %collective-permute-done.13.refs_2_), channel_id=1, source_target_pairs={{0,8},{8,0},{16,24},{24,16},{32,40},{40,32},{48,56},{56,48},{64,72... | collective-permute-start | bytes 1769480 | tf_op jit(solution)/shard_map/ppermute | solution.py:409
  89.7 2.6 %collective-permute-start.18 = (bf16[768,384]{1,0:T(8,128)(2,1)S(1)}, bf16[768,384]{1,0:T(8,128)(2,1)}, u32[]{:S(2)}, u32[]{:S(2)}) collective-permute-start(bf16[768,384]{1,0:T(8,128)(2,1)S(1)} %collective-permute-done.14.refs_3_), channel_id=1, source_target_pairs={{0,8},{8,0},{16,24},{24,16},{32,40},{40,32},{48,56},{56,48},{64,72... | collective-permute-start | bytes 1769480 | tf_op jit(solution)/shard_map/ppermute | solution.py:409
  102.1 17.4 %all-to-all-start.2 = ((bf16[16,16,768]{2,1,0:T(8,128)(2,1)}), bf16[16,16,768]{2,1,0:T(8,128)(2,1)S(1)}, u32[]{:S(2)}, u32[]{:S(2)}) async-start(bf16[16,16,768]{2,1,0:T(8,128)(2,1)} %bitcast.8), calls=%async_computation.2 | async-start | bytes 786432 | tf_op jit(solution)/shard_map/all_to_all | solution.py:419
  (4 other events, 43.7 us)
